TPU v7x, 512 devices: a whole 4x8x8 slice. The times are simulated.
512 devices in a mesh: node: 64 (over y_hi, z, core), local: 8 (over x, y_lo).
Axes of the slice: x: 4, y: 8 (y_hi: 4, y_lo: 2; y = y_hi * 2 + y_lo), z: 8, core: 2. Of those that a mesh axis runs over, the one named last changes fastest.
Arguments:
- tokens: bfloat16 [81920, 4096], P(('node', 'local')), may hold values from -24 to 24
- out_grad: bfloat16 [81920, 4096], P(('node', 'local')), may hold values from -24 to 24
- up_codes: bfloat16 [4096, 256], P('local'), may hold values from -127 to 127
- up_scales: float32 [4096, 2], P('local'), may hold values from 0.000109375 to 0.0004375
- down_codes: bfloat16 [4096, 256], P('local'), may hold values from -127 to 127
- down_scales: float32 [4096, 2], P('local'), may hold values from 0.000109375 to 0.0004375
Outputs:
- input_grad: bfloat16 [81920, 4096], P(('node', 'local'))
- grad_up: float32 [4096, 256], P(('local', 'node'))
- grad_down: float32 [4096, 256], P(('local', 'node'))
All inputs are finite; a program needn't handle non-finite values.
Results may differ from a plain program's by a relative error of at most 0.0075.
Values sent between devices are 32-bit elements; how exact they have to be, the bound alone decides.
No kernel may reach another device: no remote copies, remote signals or barrier semaphores. Data moves between devices by JAX's collectives and lax.ppermute only.
A program may use at most 128 MiB of HBM per device.

v0:
```python
import jax
import jax.numpy as jnp
from jax import lax
from jax.sharding import PartitionSpec as P

QBLOCK = 128


def side_by_side(arrays, axis, split_dim, concat_dim, along):
    widths = [a.shape[along] for a in arrays]
    both = jnp.concatenate(arrays, axis=along)
    whole = lax.all_to_all(both, axis, split_axis=split_dim, concat_axis=concat_dim, tiled=True)
    return tuple(jnp.split(whole, [sum(widths[:k]) for k in range(1, len(widths))], axis=along))


def gelu_tanh(values):
    return jax.nn.gelu(values, approximate=True)


def quantize(values):
    blocks = values.reshape(values.shape[:-1] + (values.shape[-1] // QBLOCK, QBLOCK))
    scales = 2.0 * jnp.sqrt(jnp.mean(blocks * blocks, axis=-1) + 1e-06) / 7.0
    block_codes = (
        jnp.clip(blocks / scales[..., None], -7.0, 7.0).astype(jnp.bfloat16).reshape(values.shape)
    )
    return (block_codes, scales)


def restore(block_codes, scales):
    blocks = block_codes.reshape(block_codes.shape[:-1] + (scales.shape[-1], -1))
    return (blocks * scales[..., None]).reshape(block_codes.shape)


def local(tokens, out_grad, up_codes, up_scales, down_codes, down_scales):
    gathered = (
        lax.all_gather(up_codes.astype(jnp.float32), "local", axis=0, tiled=True),
        lax.all_gather(up_scales, "local", axis=0, tiled=True),
        lax.all_gather(down_codes.astype(jnp.float32), "local", axis=0, tiled=True),
        lax.all_gather(down_scales, "local", axis=0, tiled=True),
    )
    up = restore(gathered[0], gathered[1]).astype(jnp.bfloat16)
    down = restore(gathered[2], gathered[3]).astype(jnp.bfloat16)
    preact = jnp.dot(tokens, up, preferred_element_type=jnp.float32)
    activated, slope_fn = jax.vjp(gelu_tanh, preact)
    activated = activated.astype(jnp.bfloat16)
    back_grad = jnp.dot(out_grad, down, preferred_element_type=jnp.float32)
    hidden_grad = slope_fn(back_grad)[0].astype(jnp.bfloat16)
    contract_rows = (((0,), (0,)), ((), ()))
    input_grad = lax.dot_general(
        hidden_grad, up, (((1,), (1,)), ((), ())), preferred_element_type=jnp.float32
    ).astype(jnp.bfloat16)
    first = lax.dot_general(tokens, hidden_grad, contract_rows, preferred_element_type=jnp.float32)
    second = lax.dot_general(out_grad, activated, contract_rows, preferred_element_type=jnp.float32)
    block_codes, scales = quantize(jnp.stack([first, second]))
    wide_codes = block_codes.astype(jnp.float32)
    devices_all = lax.axis_size("node") * lax.axis_size("local")
    received = (
        lax.all_to_all(wide_codes[None], "local", split_axis=2, concat_axis=0, tiled=True),
        lax.all_to_all(scales[None], "local", split_axis=2, concat_axis=0, tiled=True),
    )
    summed = jnp.sum(restore(received[0], received[1]), axis=0)
    node_codes, node_scales = quantize(summed)
    owned = side_by_side((node_codes.astype(jnp.float32)[None], node_scales[None]), "node", 2, 0, 3)
    reduced = jnp.sum(restore(owned[0], owned[1]), axis=0) / devices_all
    return (input_grad, reduced[0], reduced[1])


def solution(mesh):
    placed = (
        P(("node", "local"), None),
        P(("node", "local"), None),
        P("local", None),
        P("local", None),
        P("local", None),
        P("local", None),
    )
    return jax.shard_map(
        local,
        mesh=mesh,
        in_specs=placed,
        out_specs=(
            P(("node", "local"), None),
            P(("local", "node"), None),
            P(("local", "node"), None),
        ),
        check_vma=False,
    )
```

profile of v0, /device:TPU:1, one launch (start us, length us, event | category | flops | bytes accessed | tf_op | source)
XLA Modules:
  0.0 456.9 jit_solution(1883866873123119075)
XLA Ops:
  7.2 1.9 convert_element_type.65
  9.2 1.8 convert_element_type.63
  11.0 22.8 %all_gather.13 = f32[4096,2]{0,1:T(2,128)S(1)} all-gather(f32[512,2]{0,1:T(2,128)} %param.11), channel_id=1, replica_groups=mesh['node'=64,'local'=8] {'local'}, dimensions={0}, use_global_device_ids=true | all-gather | bytes 36864 | tf_op jit(solution)/shard_map/all_gather | solution.py:39
  33.8 2.0 copy.19
  35.7 23.7 %all_gather.15 = f32[4096,2]{0,1:T(2,128)S(1)} all-gather(f32[512,2]{0,1:T(2,128)S(1)} %copy-done.10), channel_id=1, replica_groups=mesh['node'=64,'local'=8] {'local'}, dimensions={0}, use_global_device_ids=true | all-gather | bytes 36864 | tf_op jit(solution)/shard_map/all_gather | solution.py:37
  60.1 52.7 %all-gather.5.cloned.1.call-done = f32[4096,256]{1,0:T(8,128)} async-done(((f32[512,256]{1,0:T(8,128)}), f32[4096,256]{1,0:T(8,128)}) %all-gather.5.cloned.1.call-update) | async-done | bytes 4194320 | tf_op jit(solution)/shard_map/all_gather | solution.py:36
  112.7 9.4 %mul.106 = f32[4096,2,128]{2,1,0:T(2,128)S(1)} broadcast(f32[4096,2]{1,0:T(8,128)S(1)} %copy.20), dimensions={0,1} | broadcast | bytes 4227072 | tf_op jit(solution)/shard_map/mul | solution.py:31
  122.2 0.8 fusion.5
  124.7 2.7 fusion.25
  127.5 83.5 %all-gather.3.cloned.1.call-done = f32[4096,256]{1,0:T(8,128)} async-done(((f32[512,256]{1,0:T(8,128)}), f32[4096,256]{1,0:T(8,128)}) %all-gather.3.cloned.1.call-update) | async-done | bytes 4194320 | tf_op jit(solution)/shard_map/all_gather | solution.py:38
  211.0 8.7 %mul.103 = f32[4096,2,128]{2,1,0:T(2,128)S(1)} broadcast(f32[4096,2]{1,0:T(8,128)} %copy.19), dimensions={0,1} | broadcast | bytes 4227072 | tf_op jit(solution)/shard_map/mul | solution.py:31
  221.7 2.7 copy-done.2
  225.4 4.3 copy.23
  229.7 8.1 %reshape.171 = f32[8,1,2048]{2,1,0:T(1,128)} reshape(f32[4096,1,2,2]{3,2,1,0:T(2,128)} %bitcast.94) | data formatting | bytes 131072
  237.8 3.8 all-to-all-start.1
  241.6 6.3 %fusion.4 = f32[1,2,4096,256]{2,3,1,0:T(8,128)} fusion(f32[1,1,4096,256]{2,3,1,0:T(8,128)} %bitcast.87, f32[1,1,4096,256]{2,3,1,0:T(8,128)} %bitcast.90, f32[2,4096,2]{1,2,0:T(2,128)S(1)} %get-tuple-element.3), kind=kLoop, calls=%fused_computation.8 | loop fusion | flops 10485760 | bytes 16842752 | tf_op jit(solution)/shard_map/convert_element_type | solution.py:55
  247.9 13.2 %copy.21 = f32[1,2,4096,256]{3,1,0,2:T(2,128)} copy(f32[1,2,4096,256]{2,3,1,0:T(8,128)} %fusion.4) | data formatting | bytes 16777216 | tf_op jit(solution)/shard_map/convert_element_type | solution.py:55
  261.1 5.1 %all-to-all-start = ((f32[1,2,4096,256]{3,1,0,2:T(2,128)}), f32[1,2,4096,256]{3,1,0,2:T(2,128)}, u32[]{:S(2)}, u32[]{:S(2)}) async-start(f32[1,2,4096,256]{3,1,0,2:T(2,128)} %copy.21), calls=%async_computation | async-start | bytes 16777216 | tf_op jit(solution)/shard_map/all_to_all | solution.py:58
  267.6 8.4 %reshape.172 = f32[4096,1,2,2]{3,2,1,0:T(2,128)} reshape(f32[8,2048]{1,0:T(8,128)S(1)} %reduce) | data formatting | bytes 131072
  275.9 3.5 copy.24
  279.5 79.8 %all-to-all-done = f32[1,2,4096,256]{3,1,0,2:T(2,128)} async-done(((f32[1,2,4096,256]{3,1,0,2:T(2,128)}), f32[1,2,4096,256]{3,1,0,2:T(2,128)}, u32[]{:S(2)}, u32[]{:S(2)}) %all-to-all-start) | async-done | bytes 8388640 | tf_op jit(solution)/shard_map/all_to_all | solution.py:58
  359.3 10.0 %copy.22 = f32[1,2,8,512,256]{3,2,4,1,0:T(8,128)} copy(f32[1,2,8,512,256]{4,1,3,2,0:T(2,128)} %bitcast.9) | data formatting | bytes 16777216 | tf_op jit(solution)/shard_map/all_to_all | solution.py:58
  369.2 4.3 mul.126
  373.5 9.9 %fusion.3 = f32[2,512,256]{1,2,0:T(8,128)S(1)} fusion(f32[8,2,512,256]{2,0,3,1:T(8,128)} %bitcast.91, f32[1,2,8,512,256]{3,2,4,1,0:T(8,128)} %copy.22), kind=kLoop, calls=%fused_computation.6 | loop fusion | flops 3932160 | bytes 17825792 | tf_op jit(solution)/shard_map/reduce_sum | solution.py:61
  383.8 2.2 copy.25
  386.0 15.4 %all-to-all-start.2 = ((f32[1,2,512,258]{3,1,0,2:T(2,128)}), f32[1,2,512,258]{3,1,0,2:T(2,128)}, u32[]{:S(2)}, u32[]{:S(2)}) async-start(f32[1,2,512,258]{3,1,0,2:T(2,128)} %copy.25), calls=%async_computation.2 | async-start | bytes 3145728 | tf_op jit(solution)/shard_map/all_to_all | solution.py:12
  401.5 1.9 convolution_convert_fusion
  403.4 40.5 %all-to-all-done.2 = f32[1,2,512,258]{3,1,0,2:T(2,128)} async-done(((f32[1,2,512,258]{3,1,0,2:T(2,128)}), f32[1,2,512,258]{3,1,0,2:T(2,128)}, u32[]{:S(2)}, u32[]{:S(2)}) %all-to-all-start.2) | async-done | bytes 1056800 | tf_op jit(solution)/shard_map/all_to_all | solution.py:12
  443.9 1.1 split.9
  444.9 1.2 mul.131
  446.2 1.2 mul.132
  447.4 2.0 fusion.12
  (41 shorter events, 7.7 us)
Async XLA Ops:
  7.2 117.6 %copy-start = (bf16[160,4096]{1,0:T(8,128)(2,1)S(1)}, bf16[160,4096]{1,0:T(8,128)(2,1)}, u32[]{:S(2)}) copy-start(bf16[160,4096]{1,0:T(8,128)(2,1)} %param.7) | copy-start | bytes 3932164
  7.2 28.6 %copy-start.10 = (f32[512,2]{0,1:T(2,128)S(1)}, f32[512,2]{0,1:T(2,128)}, u32[]{:S(2)}) copy-start(f32[512,2]{0,1:T(2,128)} %param.9) | copy-start | bytes 12292
  7.2 105.5 %all-gather.5.cloned.1.call-start = ((), (), s32[]{:S(2)}) async-start(), calls=%async_computation.4 | async-start | bytes 4718592 | tf_op jit(solution)/shard_map/all_gather | solution.py:36
  9.1 201.8 %all-gather.3.cloned.1.call-start = ((), (), s32[]{:S(2)}) async-start(), calls=%async_computation.3 | async-start | bytes 4718592 | tf_op jit(solution)/shard_map/all_gather | solution.py:38
  112.7 9.4 %copy-start.7 = (f32[4096,256]{1,0:T(8,128)S(1)}, f32[4096,256]{1,0:T(8,128)}, u32[]{:S(2)}) copy-start(f32[4096,256]{1,0:T(8,128)} %all-gather.5.cloned.1.call-done) | copy-start | bytes 12582916
  122.2 1.3 copy-start.4
  124.1 0.7 copy-start.8
  211.0 8.7 %copy-start.6 = (f32[4096,256]{1,0:T(8,128)S(1)}, f32[4096,256]{1,0:T(8,128)}, u32[]{:S(2)}) copy-start(f32[4096,256]{1,0:T(8,128)} %all-gather.3.cloned.1.call-done) | copy-start | bytes 12582916
  211.0 8.7 %copy-start.9 = (f32[160,256]{1,0:T(8,128)S(1)}, f32[160,256]{1,0:T(8,128)}, u32[]{:S(2)}) copy-start(f32[160,256]{1,0:T(8,128)} %copy-done.8) | copy-start | bytes 491524
  219.7 1.3 copy-start.5
  221.0 3.5 copy-start.2
  221.7 3.5 copy-start.3
  237.8 23.3 %all-to-all-start.1 = ((f32[8,1,2048]{2,1,0:T(1,128)}), f32[8,1,2048]{2,1,0:T(1,128)S(1)}, u32[]{:S(2)}, u32[]{:S(2)}) async-start(f32[8,1,2048]{2,1,0:T(1,128)} %reshape.171), calls=%async_computation.1 | async-start | bytes 131072 | tf_op jit(solution)/shard_map/all_to_all | solution.py:59
  261.1 98.2 %all-to-all-start = ((f32[1,2,4096,256]{3,1,0,2:T(2,128)}), f32[1,2,4096,256]{3,1,0,2:T(2,128)}, u32[]{:S(2)}, u32[]{:S(2)}) async-start(f32[1,2,4096,256]{3,1,0,2:T(2,128)} %copy.21), calls=%async_computation | async-start | bytes 16777216 | tf_op jit(solution)/shard_map/all_to_all | solution.py:58
  386.0 57.9 %all-to-all-start.2 = ((f32[1,2,512,258]{3,1,0,2:T(2,128)}), f32[1,2,512,258]{3,1,0,2:T(2,128)}, u32[]{:S(2)}, u32[]{:S(2)}) async-start(f32[1,2,512,258]{3,1,0,2:T(2,128)} %copy.25), calls=%async_computation.2 | async-start | bytes 3145728 | tf_op jit(solution)/shard_map/all_to_all | solution.py:12
  401.5 48.6 %copy-start.1 = (bf16[160,4096]{1,0:T(8,128)(2,1)S(1)}, bf16[160,4096]{1,0:T(8,128)(2,1)}, u32[]{:S(2)}) copy-start(bf16[160,4096]{1,0:T(8,128)(2,1)} %param.7) | copy-start | bytes 3932164
Sparse Core Ops, SparseCore 0:
  10.7 102.0 all-gather.4
  114.8 96.1 all-gather.2
where the time goes:
time: 458 us; the launch traced here: 457 us
  waiting for transfers between devices  256 us (56%)
  local copies, waits for them, and re-layouts  83.8 us (18%)
  blocking collectives  46.5 us (10%)
  other arithmetic  24.7 us (5%)
  starting transfers between devices  24.5 us (5%)
  between operations  14.3 us (3%)
  matrix products  6.67 us (1%)
    all_gather x1, waiting for transfers between devices, local(): lax.all_gather(down_codes.astype(jnp.float32), 'local', axis=0, tiled=True)  83.5 us
    all_to_all x1, waiting for transfers between devices, local(): lax.all_to_all(wide_codes[None], 'local', split_axis=2, concat_axis=0, ti...  79.8 us
    all_gather x1, waiting for transfers between devices, local(): lax.all_gather(up_codes.astype(jnp.float32), 'local', axis=0, tiled=True)  52.7 us
    all_to_all x1, waiting for transfers between devices, side_by_side(): lax.all_to_all(both, axis, split_axis=split_dim, concat_axis=concat_dim,...  40.5 us
    mul x6, local copies, waits for them, and re-layouts, restore(): return (blocks * scales[..., None]).reshape(block_codes.shape)  28.4 us
    all_gather x1, blocking collectives, local(): lax.all_gather(up_scales, 'local', axis=0, tiled=True)  23.7 us
    all_gather x1, blocking collectives, local(): lax.all_gather(down_scales, 'local', axis=0, tiled=True)  22.8 us
    unnamed x25, local copies, waits for them, and re-layouts  21.5 us
  transfers between devices with their start and end apart: 5, of which 4 were waited for; matrix products, arithmetic and copies ran while one was open for 11% of the time, Pallas kernels for 0%

commit v1 on v0

v1 whole, which is shorter than its diff:
```python
import functools
import math
import jax
import jax.numpy as jnp
from jax import lax
from jax.experimental import pallas as pl
from jax.experimental.pallas import tpu as pltpu
from jax.sharding import Mesh, PartitionSpec as P

QBLOCK = 128
AXES = ("yh", "z", "c", "x", "yl")
LOCAL = ("x", "yl")
GROUP = ("z", "c")
VMEM_LIMIT = 40 * 1024 * 1024


def exchange(array, axes):
    return lax.all_to_all(array, axes, split_axis=0, concat_axis=0, tiled=True)


def clip_blocks(values):
    parts = []
    for k in range(values.shape[1] // QBLOCK):
        block = values[:, k * QBLOCK : (k + 1) * QBLOCK]
        mean = jnp.mean(block * block, axis=-1, keepdims=True)
        scale = 2.0 * jnp.sqrt(mean + 1e-06) / 7.0
        codes = jnp.clip(block * (1.0 / scale), -7.0, 7.0).astype(jnp.bfloat16)
        parts.append(codes.astype(jnp.float32) * scale)
    return jnp.concatenate(parts, axis=1)


def inner_tanh(v):
    return jnp.tanh(math.sqrt(2.0 / math.pi) * (v + 0.044715 * v * v * v))


def forward_kernel(weights_ref, tokens_ref, preact_ref, act_ref, up_ref, total):
    step = pl.program_id(0)

    @pl.when(step == 0)
    def _():
        total[...] = jnp.zeros_like(total)

    w = weights_ref[...].reshape(-1, weights_ref.shape[-1]).astype(jnp.bfloat16)
    up_ref[...] = w
    total[...] += jnp.dot(tokens_ref[...], w, preferred_element_type=jnp.float32)

    @pl.when(step == pl.num_programs(0) - 1)
    def _():
        v = total[...]
        preact_ref[...] = v
        act = 0.5 * v * (1.0 + inner_tanh(v))
        act_ref[...] = act.astype(jnp.bfloat16).astype(jnp.float32)


def backward_kernel(weights_ref, grads_ref, preact_ref, hidden_ref, total):
    step = pl.program_id(0)

    @pl.when(step == 0)
    def _():
        total[...] = jnp.zeros_like(total)

    w = weights_ref[...].reshape(-1, weights_ref.shape[-1]).astype(jnp.bfloat16)
    total[...] += jnp.dot(grads_ref[...], w, preferred_element_type=jnp.float32)

    @pl.when(step == pl.num_programs(0) - 1)
    def _():
        v = preact_ref[...]
        t = inner_tanh(v)
        slope = 0.5 * (1.0 + t) + 0.5 * v * (1.0 - t * t) * math.sqrt(2.0 / math.pi) * (
            1.0 + 3.0 * 0.044715 * v * v
        )
        hidden_ref[...] = (total[...] * slope).astype(jnp.bfloat16).astype(jnp.float32)


def weight_spec(shape):
    return pl.BlockSpec((shape[0], None, shape[2], shape[3]), lambda k: (0, k, 0, 0))


def forward(weights, tokens):
    groups, n, piece, width = weights.shape
    rows, depth = tokens.shape
    whole = pl.BlockSpec((rows, width), lambda k: (0, 0))
    return pl.pallas_call(
        forward_kernel,
        grid=(n,),
        in_specs=[weight_spec(weights.shape), pl.BlockSpec((rows, depth // n), lambda k: (0, k))],
        out_specs=[whole, whole, pl.BlockSpec((depth // n, width), lambda k: (k, 0))],
        out_shape=[
            jax.ShapeDtypeStruct((rows, width), jnp.float32),
            jax.ShapeDtypeStruct((rows, width), jnp.float32),
            jax.ShapeDtypeStruct((depth, width), jnp.bfloat16),
        ],
        scratch_shapes=[pltpu.VMEM((rows, width), jnp.float32)],
        compiler_params=pltpu.CompilerParams(vmem_limit_bytes=VMEM_LIMIT),
        cost_estimate=pl.CostEstimate(
            flops=2 * rows * depth * width, bytes_accessed=8000000, transcendentals=rows * width
        ),
        name="forward",
    )(weights, tokens)


def backward(weights, grads, preact):
    groups, n, piece, width = weights.shape
    rows, depth = grads.shape
    whole = pl.BlockSpec((rows, width), lambda k: (0, 0))
    return pl.pallas_call(
        backward_kernel,
        grid=(n,),
        in_specs=[
            weight_spec(weights.shape),
            pl.BlockSpec((rows, depth // n), lambda k: (0, k)),
            whole,
        ],
        out_specs=whole,
        out_shape=jax.ShapeDtypeStruct((rows, width), jnp.float32),
        scratch_shapes=[pltpu.VMEM((rows, width), jnp.float32)],
        compiler_params=pltpu.CompilerParams(vmem_limit_bytes=VMEM_LIMIT),
        cost_estimate=pl.CostEstimate(
            flops=2 * rows * depth * width, bytes_accessed=6000000, transcendentals=rows * width
        ),
        name="backward",
    )(weights, grads, preact)


def node_kernel(core_ref, left_ref, right_ref, mine_ref, other_ref, total):
    step = pl.program_id(0)

    @pl.when(step == 0)
    def _():
        total[...] = jnp.zeros_like(total)

    term = lax.dot_general(
        left_ref[...].astype(jnp.bfloat16),
        right_ref[...].astype(jnp.bfloat16),
        (((0,), (0,)), ((), ())),
        preferred_element_type=jnp.float32,
    )
    total[...] += clip_blocks(term)

    @pl.when(step == pl.num_programs(0) - 1)
    def _():
        pairs, rows, width = mine_ref.shape
        summed = clip_blocks(total[...]).reshape(pairs, 2, rows, width)
        first = core_ref[0] == 0
        mine_ref[...] = jnp.where(first, summed[:, 0], summed[:, 1])
        other_ref[...] = jnp.where(first, summed[:, 1], summed[:, 0])


def node_sum(core, left, right, owned):
    n, rows, height = left.shape
    width = right.shape[2]
    half = (height // (2 * owned), owned, width)
    out = pl.BlockSpec(half, lambda k, core_ref: (0, 0, 0))
    return pl.pallas_call(
        node_kernel,
        grid_spec=pltpu.PrefetchScalarGridSpec(
            num_scalar_prefetch=1,
            grid=(n,),
            in_specs=[
                pl.BlockSpec((None, rows, height), lambda k, core_ref: (k, 0, 0)),
                pl.BlockSpec((None, rows, width), lambda k, core_ref: (k, 0, 0)),
            ],
            out_specs=[out, out],
            scratch_shapes=[pltpu.VMEM((height, width), jnp.float32)],
        ),
        out_shape=[jax.ShapeDtypeStruct(half, jnp.float32)] * 2,
        compiler_params=pltpu.CompilerParams(vmem_limit_bytes=VMEM_LIMIT),
        cost_estimate=pl.CostEstimate(
            flops=2 * n * rows * height * width, bytes_accessed=5000000, transcendentals=0
        ),
        name="node_sum",
    )(core, left, right)


def local(tokens, out_grad, up_codes, up_scales, down_codes, down_scales):
    n_local = lax.axis_size(LOCAL)
    n_group = lax.axis_size(GROUP)
    devices_all = lax.axis_size(AXES)
    rows, depth = tokens.shape
    shard, width = up_codes.shape
    owned = depth // devices_all
    core = lax.axis_index("c")

    def product(codes, scales):
        piece = shard // n_group
        start = lax.axis_index(GROUP) * piece
        own = lax.dynamic_slice_in_dim(codes, start, piece, 0).astype(jnp.float32)
        own_scales = lax.dynamic_slice_in_dim(scales, start, piece, 0)
        return own * jnp.repeat(own_scales, QBLOCK, axis=1)

    def by_slices(array):
        cut = array.reshape(rows, n_local, depth // n_local).transpose(1, 0, 2)
        return cut.astype(jnp.float32)

    def to_all(array):
        return exchange(jnp.broadcast_to(array[None], (n_local,) + array.shape), LOCAL)

    pieces = to_all(jnp.stack([product(up_codes, up_scales), product(down_codes, down_scales)]))
    up_all = lax.all_gather(pieces[:, 0], GROUP, axis=0)
    down_all = lax.all_gather(pieces[:, 1], GROUP, axis=0)
    grads_cut = exchange(by_slices(out_grad), LOCAL)
    preact, activated, up = forward(up_all, tokens)
    activated_all = to_all(activated)
    tokens_cut = exchange(by_slices(tokens), LOCAL)

    def finish(left, right):
        mine, other = node_sum(core[None], left, right, owned)
        both = mine + lax.ppermute(other, "c", [(0, 1), (1, 0)])
        return jnp.sum(exchange(both, ("yh", "z")), axis=0) / devices_all

    grad_down = finish(grads_cut, activated_all)
    hidden = backward(down_all, out_grad, preact)
    hidden_all = to_all(hidden)
    input_grad = lax.dot_general(
        hidden.astype(jnp.bfloat16), up, (((1,), (1,)), ((), ())), preferred_element_type=jnp.float32
    ).astype(jnp.bfloat16)
    grad_up = finish(tokens_cut, hidden_all)
    return (input_grad, grad_up, grad_down)


def solution(mesh):
    fine = Mesh(mesh.devices.reshape(4, 8, 2, 4, 2), AXES)
    by_tokens = P(AXES, None)
    by_rows = P(LOCAL, None)
    owned_rows = P(LOCAL + ("yh", "z", "c"), None)
    return jax.shard_map(
        local,
        mesh=fine,
        in_specs=(by_tokens, by_tokens, by_rows, by_rows, by_rows, by_rows),
        out_specs=(by_tokens, owned_rows, owned_rows),
        check_vma=False,
    )
```

time: 458 us -> 228 us (0.50)
  waiting for transfers between devices: 256 us -> 87.1 us
  local copies, waits for them, and re-layouts: 83.8 us -> 20.6 us
  other arithmetic: 24.7 us -> 5.35 us
  starting transfers between devices: 24.5 us -> 42.6 us
  Pallas kernels: 0 us -> 16.9 us
  blocking collectives: 46.5 us -> 35.8 us
    all_gather x2, waiting for transfers between devices: 136 us -> 49.4 us  [the longest x1 39.4 us: local(): down_all = lax.all_gather(pieces[:, 1], GROUP, axis=0)]
    all_to_all x3 -> x5, waiting for transfers between devices: 120 us -> 34.7 us  [exchange(): return lax.all_to_all(array, axes, split_axis=0, concat_axis=0, tiled=True)]
    all_gather x2 -> x0, blocking collectives: 46.5 us -> none  [the longest x1 23.7 us: local(): lax.all_gather(up_scales, 'local', axis=0, tiled=True)]
    all_to_all x0 -> x2, blocking collectives: none -> 35.8 us  [exchange(): return lax.all_to_all(array, axes, split_axis=0, concat_axis=0, tiled=True)]
    mul x6 -> x0, local copies, waits for them, and re-layouts: 28.4 us -> none  [restore(): return (blocks * scales[..., None]).reshape(block_codes.shape)]
    pallas_call x0 -> x4, Pallas kernels: none -> 16.9 us  [the longest x2 12.5 us: node_sum(): pl.pallas_call(node_kernel, grid_spec=pltpu.PrefetchScalarGridSpec(num_sc...]
    reduce_sum x4 -> x2, other arithmetic: 12.8 us -> 0.07 us  [finish(): return jnp.sum(exchange(both, ('yh', 'z')), axis=0) / devices_all]
    all_to_all x2 -> x0, local copies, waits for them, and re-layouts: 10.5 us -> none  [the longest x1 9.95 us: local(): lax.all_to_all(wide_codes[None], 'local', split_axis=2, concat_axis=0, ti...]
  transfers between devices with their start and end apart: 5 -> 9, of which waited for: 4 -> 7; matrix products, arithmetic and copies ran while one was open for 11% -> 5% of each run, Pallas kernels for 0% -> 7%
where the time goes in v1:
time: 228 us; the launch traced here: 226 us
  waiting for transfers between devices  87.1 us (38%)
  starting transfers between devices  42.6 us (19%)
  blocking collectives  35.8 us (16%)
  local copies, waits for them, and re-layouts  20.6 us (9%)
  Pallas kernels  16.9 us (7%)
  between operations  14.2 us (6%)
  other arithmetic  5.35 us (2%)
  matrix products  3.49 us (2%)
    all_gather x1, waiting for transfers between devices, local(): down_all = lax.all_gather(pieces[:, 1], GROUP, axis=0)  39.4 us
    all_to_all x2, blocking collectives, exchange(): return lax.all_to_all(array, axes, split_axis=0, concat_axis=0, tiled=True)  35.8 us
    all_to_all x5, waiting for transfers between devices, exchange(): return lax.all_to_all(array, axes, split_axis=0, concat_axis=0, tiled=True)  34.7 us
    all_to_all x5, starting transfers between devices, exchange(): return lax.all_to_all(array, axes, split_axis=0, concat_axis=0, tiled=True)  33.8 us
    unnamed x20, local copies, waits for them, and re-layouts  13.6 us
    pallas_call x2, Pallas kernels, node_sum(): pl.pallas_call(node_kernel, grid_spec=pltpu.PrefetchScalarGridSpec(num_sc...  12.5 us
    all_gather x1, waiting for transfers between devices, local(): up_all = lax.all_gather(pieces[:, 0], GROUP, axis=0)  9.99 us
    ppermute x2, starting transfers between devices, finish(): both = mine + lax.ppermute(other, 'c', [(0, 1), (1, 0)])  8.68 us
  transfers between devices with their start and end apart: 9, of which 7 were waited for; matrix products, arithmetic and copies ran while one was open for 5% of the time, Pallas kernels for 7%

profile of v1, /device:TPU:1, one launch (start us, length us, event | category | flops | bytes accessed | tf_op | source)
XLA Modules:
  0.0 226.0 jit_solution(18243875887644808210)
XLA Ops:
  9.9 13.2 %all_to_all.35 = f32[8,2,32,256]{3,2,1,0:T(8,128)S(1)} all-to-all(f32[8,2,32,256]{3,2,1,0:T(8,128)S(1)} %broadcast_in_dim.14), channel_id=1, replica_groups=mesh['yh'=4,'z'=8,'c'=2,'x'=4,'yl'=2] {'x','yl'}, dimensions={0} | all-to-all | bytes 1048576 | tf_op jit(solution)/shard_map/all_to_all | solution.py:18
  24.2 1.8 copy.28
  26.0 3.6 %all-to-all-start.1 = ((f32[8,160,512]{2,1,0:T(8,128)}), f32[8,160,512]{2,1,0:T(8,128)S(1)}, u32[]{:S(2)}, u32[]{:S(2)}) async-start(f32[8,160,512]{2,1,0:T(8,128)} %bitcast.35), calls=%async_computation.1 | async-start | bytes 5242880 | tf_op jit(solution)/shard_map/all_to_all | solution.py:18
  30.4 1.6 convert_element_type.43
  32.0 1.8 copy.27
  33.9 23.6 %all-to-all-done.1.left_ref = f32[8,160,512]{2,1,0:T(8,128)S(1)} async-done(((f32[8,160,512]{2,1,0:T(8,128)}), f32[8,160,512]{2,1,0:T(8,128)S(1)}, u32[]{:S(2)}, u32[]{:S(2)}) %all-to-all-start.1) | async-done | bytes 2621472 | tf_op jit(solution)/shard_map/all_to_all | solution.py:18
  57.5 1.6 copy-done.1
  59.1 5.8 %all-to-all-start.4 = ((f32[8,160,512]{2,1,0:T(8,128)}), f32[8,160,512]{2,1,0:T(8,128)S(1)}, u32[]{:S(2)}, u32[]{:S(2)}) async-start(f32[8,160,512]{2,1,0:T(8,128)} %bitcast.34), calls=%async_computation.4 | async-start | bytes 5242880 | tf_op jit(solution)/shard_map/all_to_all | solution.py:18
  64.9 10.0 %all-gather.7.cloned.1.call-done = f32[128,1,32,256]{3,2,1,0:T(8,128)} async-done(((f32[8,1,32,256]{3,2,1,0:T(8,128)}), f32[128,1,32,256]{3,2,1,0:T(8,128)}) %all-gather.7.cloned.1.call-update) | async-done | bytes 4194320 | tf_op jit(solution)/shard_map/all_gather | solution.py:199
  74.9 1.3 copy-done.5
  76.2 2.2 copy-done.7
  78.4 2.2 forward.1
  80.6 1.3 copy-done.9
  82.0 39.4 %all-gather.5.cloned.1.call-done = f32[128,1,32,256]{3,2,1,0:T(8,128)} async-done(((f32[8,1,32,256]{3,2,1,0:T(8,128)}), f32[128,1,32,256]{3,2,1,0:T(8,128)}) %all-gather.5.cloned.1.call-update) | async-done | bytes 4194320 | tf_op jit(solution)/shard_map/all_gather | solution.py:200
  121.4 1.3 copy-done.6
  122.7 2.2 copy-done.8
  124.9 2.2 backward.1
  127.2 22.6 %all_to_all.36.right_ref = f32[8,160,256]{2,1,0:T(8,128)} all-to-all(f32[8,160,256]{2,1,0:T(8,128)S(1)} %broadcast_in_dim.32), channel_id=1, replica_groups=mesh['yh'=4,'z'=8,'c'=2,'x'=4,'yl'=2] {'x','yl'}, dimensions={0} | all-to-all | bytes 2621440 | tf_op jit(solution)/shard_map/all_to_all | solution.py:18
  149.8 1.2 broadcast_in_dim.33
  151.0 4.3 %all-to-all-start.5 = ((f32[8,160,256]{2,1,0:T(8,128)}), f32[8,160,256]{2,1,0:T(8,128)}, u32[]{:S(2)}, u32[]{:S(2)}) async-start(f32[8,160,256]{2,1,0:T(8,128)} %broadcast_in_dim.33), calls=%async_computation.5 | async-start | bytes 2621440 | tf_op jit(solution)/shard_map/all_to_all | solution.py:18
  155.3 1.7 copy-done.2
  157.0 1.3 copy-done.3
  158.3 5.3 %node_sum.2 = (f32[32,8,256]{2,1,0:T(8,128)S(1)}, f32[32,8,256]{2,1,0:T(8,128)S(1)}) custom-call(s32[1]{0:T(128)} %bitcast.4.core_ref, f32[8,160,512]{2,1,0:T(8,128)S(1)} %copy-done.2, f32[8,160,256]{2,1,0:T(8,128)S(1)} %copy-done.3), custom_call_target="tpu_custom_call" | custom-call | flops 335544320 | bytes 5000000 | tf_op jit(solution)/shard_map/node_sum/pallas_call | solution.py:154
  163.6 3.6 %collective-permute-start = (f32[32,8,256]{2,1,0:T(8,128)S(1)}, f32[32,8,256]{2,1,0:T(8,128)S(1)}, u32[]{:S(2)}, u32[]{:S(2)}) collective-permute-start(f32[32,8,256]{2,1,0:T(8,128)S(1)} %get-tuple-element.13), channel_id=1, source_target_pairs={{0,8},{8,0},{1,9},{9,1},{2,10},{10,2},{3,11},{11,3},{4,12},{12,4},... | collective-permute-start | bytes 786440 | tf_op jit(solution)/shard_map/ppermute | solution.py:208
  167.2 1.1 collective-permute-done
  169.1 2.8 %all-to-all-done.5.right_ref = f32[8,160,256]{2,1,0:T(8,128)} async-done(((f32[8,160,256]{2,1,0:T(8,128)}), f32[8,160,256]{2,1,0:T(8,128)}, u32[]{:S(2)}, u32[]{:S(2)}) %all-to-all-start.5) | async-done | bytes 1310752 | tf_op jit(solution)/shard_map/all_to_all | solution.py:18
  171.9 8.2 %all-to-all-start.3 = ((f32[32,8,256]{2,1,0:T(8,128)}), f32[32,8,256]{2,1,0:T(8,128)S(1)}, u32[]{:S(2)}, u32[]{:S(2)}) async-start(f32[32,8,256]{2,1,0:T(8,128)} %add.18), calls=%async_computation.3 | async-start | bytes 524288 | tf_op jit(solution)/shard_map/all_to_all | solution.py:18
  180.1 7.2 %node_sum.3 = (f32[32,8,256]{2,1,0:T(8,128)S(1)}, f32[32,8,256]{2,1,0:T(8,128)S(1)}) custom-call(s32[1]{0:T(128)} %bitcast.4.core_ref, f32[8,160,512]{2,1,0:T(8,128)S(1)} %all-to-all-done.4.left_ref, f32[8,160,256]{2,1,0:T(8,128)} %all-to-all-done.5.right_ref), custom_call_target="tpu_custom_call" | custom-call | flops 335544320 | bytes 5000000 | tf_op jit(solution)/shard_map/node_sum/pallas_call | solution.py:154
  187.3 5.1 %collective-permute-start.1 = (f32[32,8,256]{2,1,0:T(8,128)S(1)}, f32[32,8,256]{2,1,0:T(8,128)S(1)}, u32[]{:S(2)}, u32[]{:S(2)}) collective-permute-start(f32[32,8,256]{2,1,0:T(8,128)S(1)} %get-tuple-element.16), channel_id=1, source_target_pairs={{0,8},{8,0},{1,9},{9,1},{2,10},{10,2},{3,11},{11,3},{4,12},{12,4},... | collective-permute-start | bytes 786440 | tf_op jit(solution)/shard_map/ppermute | solution.py:208
  194.3 11.9 %all-to-all-start.6 = ((f32[32,8,256]{2,1,0:T(8,128)}), f32[32,8,256]{2,1,0:T(8,128)S(1)}, u32[]{:S(2)}, u32[]{:S(2)}) async-start(f32[32,8,256]{2,1,0:T(8,128)} %add.19), calls=%async_computation.6 | async-start | bytes 524288 | tf_op jit(solution)/shard_map/all_to_all | solution.py:18
  206.2 3.5 %convolution_convert_fusion = bf16[160,4096]{1,0:T(8,128)(2,1)} fusion(bf16[4096,256]{1,0:T(8,128)(2,1)} %copy-done.9, f32[160,256]{1,0:T(8,128)S(1)} %backward.1), kind=kOutput, calls=%fused_computation | convolution fusion | flops 336240640 | bytes 3571712 | tf_op jit(solution)/shard_map/dot_general | solution.py:214
  210.3 8.2 %all-to-all-done.6 = f32[32,8,256]{2,1,0:T(8,128)S(1)} async-done(((f32[32,8,256]{2,1,0:T(8,128)}), f32[32,8,256]{2,1,0:T(8,128)S(1)}, u32[]{:S(2)}, u32[]{:S(2)}) %all-to-all-start.6) | async-done | bytes 262176 | tf_op jit(solution)/shard_map/all_to_all | solution.py:18
  (37 shorter events, 8.5 us)
Async XLA Ops:
  7.2 0.7 copy-start
  7.2 16.7 %copy-start.4 = (bf16[160,4096]{1,0:T(8,128)(2,1)S(1)}, bf16[160,4096]{1,0:T(8,128)(2,1)}, u32[]{:S(2)}) copy-start(bf16[160,4096]{1,0:T(8,128)(2,1)} %tokens_ref.1) | copy-start | bytes 3932164
  7.2 67.7 %all-gather.7.cloned.1.call-start = ((), (), s32[]{:S(2)}) async-start(), calls=%async_computation.8 | async-start | bytes 4456448 | tf_op jit(solution)/shard_map/all_gather | solution.py:199
  26.0 31.5 %all-to-all-start.1 = ((f32[8,160,512]{2,1,0:T(8,128)}), f32[8,160,512]{2,1,0:T(8,128)S(1)}, u32[]{:S(2)}, u32[]{:S(2)}) async-start(f32[8,160,512]{2,1,0:T(8,128)} %bitcast.35), calls=%async_computation.1 | async-start | bytes 5242880 | tf_op jit(solution)/shard_map/all_to_all | solution.py:18
  29.7 91.7 %all-gather.5.cloned.1.call-start = ((), (), s32[]{:S(2)}) async-start(), calls=%async_computation.7 | async-start | bytes 4456448 | tf_op jit(solution)/shard_map/all_gather | solution.py:200
  57.5 1.6 copy-start.1
  59.1 68.1 %all-to-all-start.4 = ((f32[8,160,512]{2,1,0:T(8,128)}), f32[8,160,512]{2,1,0:T(8,128)S(1)}, u32[]{:S(2)}, u32[]{:S(2)}) async-start(f32[8,160,512]{2,1,0:T(8,128)} %bitcast.34), calls=%async_computation.4 | async-start | bytes 5242880 | tf_op jit(solution)/shard_map/all_to_all | solution.py:18
  74.9 1.3 copy-start.5
  76.2 2.2 copy-start.7
  80.6 1.4 copy-start.9
  121.4 1.3 copy-start.6
  122.7 2.2 copy-start.8
  151.0 20.9 %all-to-all-start.5 = ((f32[8,160,256]{2,1,0:T(8,128)}), f32[8,160,256]{2,1,0:T(8,128)}, u32[]{:S(2)}, u32[]{:S(2)}) async-start(f32[8,160,256]{2,1,0:T(8,128)} %broadcast_in_dim.33), calls=%async_computation.5 | async-start | bytes 2621440 | tf_op jit(solution)/shard_map/all_to_all | solution.py:18
  155.3 1.7 copy-start.2
  157.0 1.3 copy-start.3
  163.6 4.7 %collective-permute-start = (f32[32,8,256]{2,1,0:T(8,128)S(1)}, f32[32,8,256]{2,1,0:T(8,128)S(1)}, u32[]{:S(2)}, u32[]{:S(2)}) collective-permute-start(f32[32,8,256]{2,1,0:T(8,128)S(1)} %get-tuple-element.13), channel_id=1, source_target_pairs={{0,8},{8,0},{1,9},{9,1},{2,10},{10,2},{3,11},{11,3},{4,12},{12,4},... | collective-permute-start | bytes 786440 | tf_op jit(solution)/shard_map/ppermute | solution.py:208
  171.9 22.4 %all-to-all-start.3 = ((f32[32,8,256]{2,1,0:T(8,128)}), f32[32,8,256]{2,1,0:T(8,128)S(1)}, u32[]{:S(2)}, u32[]{:S(2)}) async-start(f32[32,8,256]{2,1,0:T(8,128)} %add.18), calls=%async_computation.3 | async-start | bytes 524288 | tf_op jit(solution)/shard_map/all_to_all | solution.py:18
  187.3 6.2 %collective-permute-start.1 = (f32[32,8,256]{2,1,0:T(8,128)S(1)}, f32[32,8,256]{2,1,0:T(8,128)S(1)}, u32[]{:S(2)}, u32[]{:S(2)}) collective-permute-start(f32[32,8,256]{2,1,0:T(8,128)S(1)} %get-tuple-element.16), channel_id=1, source_target_pairs={{0,8},{8,0},{1,9},{9,1},{2,10},{10,2},{3,11},{11,3},{4,12},{12,4},... | collective-permute-start | bytes 786440 | tf_op jit(solution)/shard_map/ppermute | solution.py:208
  194.3 24.3 %all-to-all-start.6 = ((f32[32,8,256]{2,1,0:T(8,128)}), f32[32,8,256]{2,1,0:T(8,128)S(1)}, u32[]{:S(2)}, u32[]{:S(2)}) async-start(f32[32,8,256]{2,1,0:T(8,128)} %add.19), calls=%async_computation.6 | async-start | bytes 524288 | tf_op jit(solution)/shard_map/all_to_all | solution.py:18
Sparse Core Ops, SparseCore 0:
  24.0 50.7 all-gather.6
  77.6 43.7 all-gather.4

commit v2 on v1

v2 whole, which is shorter than its diff:
```python
import functools
import math
import jax
import jax.numpy as jnp
from jax import lax
from jax.experimental import pallas as pl
from jax.experimental.pallas import tpu as pltpu
from jax.sharding import Mesh, PartitionSpec as P

QBLOCK = 128
AXES = ("yh", "z", "c", "x", "yl")
LOCAL = ("x", "yl")
GROUP = ("z", "c")
VMEM_LIMIT = 40 * 1024 * 1024


def exchange(array, axes):
    return lax.all_to_all(array, axes, split_axis=0, concat_axis=0, tiled=True)


def clip_blocks(values):
    parts = []
    for k in range(values.shape[1] // QBLOCK):
        block = values[:, k * QBLOCK : (k + 1) * QBLOCK]
        mean = jnp.mean(block * block, axis=-1, keepdims=True)
        scale = 2.0 * jnp.sqrt(mean + 1e-06) / 7.0
        codes = jnp.clip(block * (1.0 / scale), -7.0, 7.0).astype(jnp.bfloat16)
        parts.append(codes.astype(jnp.float32) * scale)
    return jnp.concatenate(parts, axis=1)


def inner_tanh(v):
    return jnp.tanh(math.sqrt(2.0 / math.pi) * (v + 0.044715 * v * v * v))


def hidden_kernel(up_ref, down_ref, tokens_ref, grads_ref, act_ref, hidden_ref, upw_ref, pre, back):
    step = pl.program_id(0)

    @pl.when(step == 0)
    def _():
        pre[...] = jnp.zeros_like(pre)
        back[...] = jnp.zeros_like(back)

    width = up_ref.shape[-1]
    up = up_ref[...].reshape(-1, width).astype(jnp.bfloat16)
    down = down_ref[...].reshape(-1, width).astype(jnp.bfloat16)
    upw_ref[...] = up
    pre[...] += jnp.dot(tokens_ref[...], up, preferred_element_type=jnp.float32)
    back[...] += jnp.dot(grads_ref[...], down, preferred_element_type=jnp.float32)

    @pl.when(step == pl.num_programs(0) - 1)
    def _():
        v = pre[...]
        t = inner_tanh(v)
        act_ref[...] = (0.5 * v * (1.0 + t)).astype(jnp.bfloat16).astype(jnp.float32)
        slope = 0.5 * (1.0 + t) + 0.5 * v * (1.0 - t * t) * math.sqrt(2.0 / math.pi) * (
            1.0 + 3.0 * 0.044715 * v * v
        )
        hidden_ref[...] = (back[...] * slope).astype(jnp.bfloat16).astype(jnp.float32)


def hidden_pass(weights, tokens, grads):
    groups, n, _, piece, width = weights.shape
    rows, depth = tokens.shape
    whole = pl.BlockSpec((rows, width), lambda k: (0, 0))
    block = (groups, None, None, piece, width)
    cut = pl.BlockSpec((rows, depth // n), lambda k: (0, k))
    return pl.pallas_call(
        hidden_kernel,
        grid=(n,),
        in_specs=[
            pl.BlockSpec(block, lambda k: (0, k, 0, 0, 0)),
            pl.BlockSpec(block, lambda k: (0, k, 1, 0, 0)),
            cut,
            cut,
        ],
        out_specs=[whole, whole, pl.BlockSpec((depth // n, width), lambda k: (k, 0))],
        out_shape=[
            jax.ShapeDtypeStruct((rows, width), jnp.float32),
            jax.ShapeDtypeStruct((rows, width), jnp.float32),
            jax.ShapeDtypeStruct((depth, width), jnp.bfloat16),
        ],
        scratch_shapes=[pltpu.VMEM((rows, width), jnp.float32)] * 2,
        compiler_params=pltpu.CompilerParams(vmem_limit_bytes=VMEM_LIMIT),
        cost_estimate=pl.CostEstimate(
            flops=4 * rows * depth * width, bytes_accessed=13000000, transcendentals=rows * width
        ),
        name="hidden_pass",
    )(weights, weights, tokens, grads)


def cut_kernel(tokens_ref, grads_ref, out_ref):
    rows = tokens_ref.shape[0]
    out_ref[:rows] = tokens_ref[...].astype(jnp.float32)
    out_ref[rows:] = grads_ref[...].astype(jnp.float32)


def cut_columns(tokens, grads, n):
    rows, depth = tokens.shape
    cut = pl.BlockSpec((rows, depth // n), lambda k: (0, k))
    return pl.pallas_call(
        cut_kernel,
        grid=(n,),
        in_specs=[cut, cut],
        out_specs=pl.BlockSpec((None, 2 * rows, depth // n), lambda k: (k, 0, 0)),
        out_shape=jax.ShapeDtypeStruct((n, 2 * rows, depth // n), jnp.float32),
        compiler_params=pltpu.CompilerParams(vmem_limit_bytes=VMEM_LIMIT),
        cost_estimate=pl.CostEstimate(flops=0, bytes_accessed=8000000, transcendentals=0),
        name="cut_columns",
    )(tokens, grads)


def node_kernel(core_ref, left_ref, right_ref, mine_ref, other_ref, total):
    step = pl.program_id(0)

    @pl.when(step == 0)
    def _():
        total[...] = jnp.zeros_like(total)

    term = lax.dot_general(
        left_ref[...].astype(jnp.bfloat16),
        right_ref[...].astype(jnp.bfloat16),
        (((0,), (0,)), ((), ())),
        preferred_element_type=jnp.float32,
    )
    total[...] += clip_blocks(term)

    @pl.when(step == pl.num_programs(0) - 1)
    def _():
        pairs, rows, width = mine_ref.shape
        summed = clip_blocks(total[...]).reshape(pairs, 2, rows, width)
        first = core_ref[0] == 0
        mine_ref[...] = jnp.where(first, summed[:, 0], summed[:, 1])
        other_ref[...] = jnp.where(first, summed[:, 1], summed[:, 0])


def node_sum(core, left, which, right, owned):
    height = left.shape[2]
    n, rows, width = right.shape
    half = (height // (2 * owned), owned, width)
    out = pl.BlockSpec(half, lambda k, core_ref: (0, 0, 0))
    return pl.pallas_call(
        node_kernel,
        grid_spec=pltpu.PrefetchScalarGridSpec(
            num_scalar_prefetch=1,
            grid=(n,),
            in_specs=[
                pl.BlockSpec((None, rows, height), lambda k, core_ref: (k, which, 0)),
                pl.BlockSpec((None, rows, width), lambda k, core_ref: (k, 0, 0)),
            ],
            out_specs=[out, out],
            scratch_shapes=[pltpu.VMEM((height, width), jnp.float32)],
        ),
        out_shape=[jax.ShapeDtypeStruct(half, jnp.float32)] * 2,
        compiler_params=pltpu.CompilerParams(vmem_limit_bytes=VMEM_LIMIT),
        cost_estimate=pl.CostEstimate(
            flops=2 * n * rows * height * width, bytes_accessed=5000000, transcendentals=0
        ),
        name="node_sum",
    )(core, left, right)


def local(tokens, out_grad, up_codes, up_scales, down_codes, down_scales):
    n_local = lax.axis_size(LOCAL)
    n_group = lax.axis_size(GROUP)
    devices_all = lax.axis_size(AXES)
    rows, depth = tokens.shape
    shard, width = up_codes.shape
    owned = depth // devices_all
    core = lax.axis_index("c")

    def product(codes, scales):
        piece = shard // n_group
        start = lax.axis_index(GROUP) * piece
        own = lax.dynamic_slice_in_dim(codes, start, piece, 0).astype(jnp.float32)
        own_scales = lax.dynamic_slice_in_dim(scales, start, piece, 0)
        return own * jnp.repeat(own_scales, QBLOCK, axis=1)

    def to_all(array):
        return exchange(jnp.broadcast_to(array[None], (n_local,) + array.shape), LOCAL)

    pieces = to_all(jnp.stack([product(up_codes, up_scales), product(down_codes, down_scales)]))
    weights = lax.all_gather(pieces, GROUP, axis=0)
    columns = exchange(cut_columns(tokens, out_grad, n_local), LOCAL)
    activated, hidden, up = hidden_pass(weights, tokens, out_grad)

    def over_cores(which, right):
        mine, other = node_sum(core[None], columns, which, right, owned)
        return mine + lax.ppermute(other, "c", [(0, 1), (1, 0)])

    activated_all = to_all(activated)
    hidden_all = to_all(hidden)
    grad_down = over_cores(1, activated_all)
    grad_up = over_cores(0, hidden_all)
    input_grad = lax.dot_general(
        hidden.astype(jnp.bfloat16), up, (((1,), (1,)), ((), ())), preferred_element_type=jnp.float32
    ).astype(jnp.bfloat16)
    owned_sums = exchange(jnp.concatenate([grad_up, grad_down], axis=1), ("yh", "z"))
    grads = jnp.sum(owned_sums, axis=0) / devices_all
    return (input_grad, grads[:owned], grads[owned:])


def solution(mesh):
    fine = Mesh(mesh.devices.reshape(4, 8, 2, 4, 2), AXES)
    by_tokens = P(AXES, None)
    by_rows = P(LOCAL, None)
    owned_rows = P(LOCAL + ("yh", "z", "c"), None)
    return jax.shard_map(
        local,
        mesh=fine,
        in_specs=(by_tokens, by_tokens, by_rows, by_rows, by_rows, by_rows),
        out_specs=(by_tokens, owned_rows, owned_rows),
        check_vma=False,
    )
```

time: 228 us -> 192 us (0.84)
  starting transfers between devices: 42.6 us -> 27.3 us
  local copies, waits for them, and re-layouts: 20.6 us -> 10.7 us
  waiting for transfers between devices: 87.1 us -> 77.4 us
  other arithmetic: 5.35 us -> 2.68 us
    all_to_all x5 -> x3, starting transfers between devices: 33.8 us -> 18.7 us  [exchange(): return lax.all_to_all(array, axes, split_axis=0, concat_axis=0, tiled=True)]
    all_to_all x5 -> x3, waiting for transfers between devices: 34.7 us -> 20.4 us  [exchange(): return lax.all_to_all(array, axes, split_axis=0, concat_axis=0, tiled=True)]
    all_gather x2 -> x1, waiting for transfers between devices: 49.4 us -> 56.9 us  [local(): weights = lax.all_gather(pieces, GROUP, axis=0)]
    unnamed x20 -> x14, local copies, waits for them, and re-layouts: 13.6 us -> 7.62 us
    convert_element_type x2 -> x0, local copies, waits for them, and re-layouts: 3.66 us -> none  [by_slices(): return cut.astype(jnp.float32)]
    pallas_call x2, Pallas kernels: 12.5 us -> 14.9 us  [node_sum(): pl.pallas_call(node_kernel, grid_spec=pltpu.PrefetchScalarGridSpec(num_sc...]
  transfers between devices with their start and end apart: 9 -> 6, of which waited for: 7 -> 4; matrix products, arithmetic and copies ran while one was open for 5% -> 2% of each run, Pallas kernels for 7% -> 10%
where the time goes in v2:
time: 192 us; the launch traced here: 189 us
  waiting for transfers between devices  77.4 us (40%)
  blocking collectives  35.8 us (19%)
  starting transfers between devices  27.3 us (14%)
  Pallas kernels  18.7 us (10%)
  between operations  14.2 us (7%)
  local copies, waits for them, and re-layouts  10.7 us (6%)
  other arithmetic  2.68 us (1%)
    all_gather x1, waiting for transfers between devices, local(): weights = lax.all_gather(pieces, GROUP, axis=0)  56.9 us
    all_to_all x2, blocking collectives, exchange(): return lax.all_to_all(array, axes, split_axis=0, concat_axis=0, tiled=True)  35.8 us
    all_to_all x3, waiting for transfers between devices, exchange(): return lax.all_to_all(array, axes, split_axis=0, concat_axis=0, tiled=True)  20.4 us
    all_to_all x3, starting transfers between devices, exchange(): return lax.all_to_all(array, axes, split_axis=0, concat_axis=0, tiled=True)  18.7 us
    pallas_call x2, Pallas kernels, node_sum(): pl.pallas_call(node_kernel, grid_spec=pltpu.PrefetchScalarGridSpec(num_sc...  14.9 us
    ppermute x2, starting transfers between devices, over_cores(): return mine + lax.ppermute(other, 'c', [(0, 1), (1, 0)])  8.54 us
    unnamed x14, local copies, waits for them, and re-layouts  7.62 us
  transfers between devices with their start and end apart: 6, of which 4 were waited for; matrix products, arithmetic and copies ran while one was open for 2% of the time, Pallas kernels for 10%

profile of v2, /device:TPU:1, one launch (start us, length us, event | category | flops | bytes accessed | tf_op | source)
XLA Modules:
  0.0 188.8 jit_solution(8775683668064547065)
XLA Ops:
  7.3 0.6 copy-done
  7.9 0.1 constant_dynamic-slice_fusion
  7.9 0.1 copy.12
  8.0 0.7 constant_dynamic-slice_fusion.1
  8.8 0.1 copy.11
  8.9 0.1 broadcast_in_dim.13
  9.0 0.1 broadcast_in_dim.12
  9.1 0.8 fusion.1
  9.9 13.3 %all_to_all.25 = f32[8,2,32,256]{3,2,1,0:T(8,128)} all-to-all(f32[8,2,32,256]{3,2,1,0:T(8,128)S(1)} %broadcast_in_dim.14), channel_id=1, replica_groups=mesh['yh'=4,'z'=8,'c'=2,'x'=4,'yl'=2] {'x','yl'}, dimensions={0} | all-to-all | bytes 1048576 | tf_op jit(solution)/shard_map/all_to_all | solution.py:18
  23.2 0.7 cut_columns.1
  23.9 2.3 %copy-done.2 = f32[8,320,512]{2,1,0:T(8,128)} copy-done((f32[8,320,512]{2,1,0:T(8,128)}, f32[8,320,512]{2,1,0:T(8,128)S(1)}, u32[]{:S(2)}) %copy-start.2) | copy-done | bytes 5242904
  26.2 4.7 %all-to-all-start.1 = ((f32[8,320,512]{2,1,0:T(8,128)}), f32[8,320,512]{2,1,0:T(8,128)}, u32[]{:S(2)}, u32[]{:S(2)}) async-start(f32[8,320,512]{2,1,0:T(8,128)} %copy-done.2), calls=%async_computation.1 | async-start | bytes 10485760 | tf_op jit(solution)/shard_map/all_to_all | solution.py:18
  30.9 56.9 %all-gather.3.cloned.1.call-done = f32[128,2,32,256]{3,2,1,0:T(8,128)} async-done(((f32[8,2,32,256]{3,2,1,0:T(8,128)}), f32[128,2,32,256]{3,2,1,0:T(8,128)}) %all-gather.3.cloned.1.call-update) | async-done | bytes 8388624 | tf_op jit(solution)/shard_map/all_gather | solution.py:183
  87.8 3.4 %copy-done.1 = f32[128,2,32,256]{3,2,1,0:T(8,128)S(1)} copy-done((f32[128,2,32,256]{3,2,1,0:T(8,128)S(1)}, f32[128,2,32,256]{3,2,1,0:T(8,128)}, u32[]{:S(2)}) %copy-start.1) | copy-done | bytes 8388632
  91.2 3.1 %hidden_pass.1 = (f32[160,256]{1,0:T(8,128)S(1)}, f32[160,256]{1,0:T(8,128)S(1)}, bf16[4096,256]{1,0:T(8,128)(2,1)S(1)}) custom-call(f32[16,8,2,32,256]{4,3,2,1,0:T(8,128)S(1)} %bitcast.17, f32[16,8,2,32,256]{4,3,2,1,0:T(8,128)S(1)} %bitcast.18, bf16[160,4096]{1,0:T(8,128)(2,1)S(1)} %copy-done.3, bf16[160,4096]{1,0:T(8,128)(2,1)S(1)} %copy-done.4), custom_call_target="tpu_custom_call" | custom-call | flops 671088640 | bytes 13000000 | tf_op jit(solution)/shard_map/hidden_pass/pallas_call | solution.py:68
  94.3 1.3 copy-done.5
  95.7 0.1 broadcast_in_dim.33
  95.8 22.5 %all_to_all.26.right_ref = f32[8,160,256]{2,1,0:T(8,128)S(1)} all-to-all(f32[8,160,256]{2,1,0:T(8,128)S(1)} %broadcast_in_dim.33), channel_id=1, replica_groups=mesh['yh'=4,'z'=8,'c'=2,'x'=4,'yl'=2] {'x','yl'}, dimensions={0} | all-to-all | bytes 2621440 | tf_op jit(solution)/shard_map/all_to_all | solution.py:18
  118.2 1.2 broadcast_in_dim.32
  119.4 3.6 %all-to-all-start.2 = ((f32[8,160,256]{2,1,0:T(8,128)}), f32[8,160,256]{2,1,0:T(8,128)S(1)}, u32[]{:S(2)}, u32[]{:S(2)}) async-start(f32[8,160,256]{2,1,0:T(8,128)} %broadcast_in_dim.32), calls=%async_computation.2 | async-start | bytes 2621440 | tf_op jit(solution)/shard_map/all_to_all | solution.py:18
  123.0 7.5 %node_sum.3 = (f32[32,8,256]{2,1,0:T(8,128)S(1)}, f32[32,8,256]{2,1,0:T(8,128)S(1)}) custom-call(s32[1]{0:T(128)} %bitcast.3.core_ref, f32[8,320,512]{2,1,0:T(8,128)} %all-to-all-done.1.left_ref, f32[8,160,256]{2,1,0:T(8,128)S(1)} %all_to_all.26.right_ref), custom_call_target="tpu_custom_call" | custom-call | flops 335544320 | bytes 5000000 | tf_op jit(solution)/shard_map/node_sum/pallas_call | solution.py:142
  130.5 3.6 %collective-permute-start.1 = (f32[32,8,256]{2,1,0:T(8,128)S(1)}, f32[32,8,256]{2,1,0:T(8,128)}, u32[]{:S(2)}, u32[]{:S(2)}) collective-permute-start(f32[32,8,256]{2,1,0:T(8,128)S(1)} %get-tuple-element.16), channel_id=1, source_target_pairs={{0,8},{8,0},{1,9},{9,1},{2,10},{10,2},{3,11},{11,3},{4,12},{12,4},... | collective-permute-start | bytes 786440 | tf_op jit(solution)/shard_map/ppermute | solution.py:189
  134.1 5.4 %all-to-all-done.2.right_ref = f32[8,160,256]{2,1,0:T(8,128)S(1)} async-done(((f32[8,160,256]{2,1,0:T(8,128)}), f32[8,160,256]{2,1,0:T(8,128)S(1)}, u32[]{:S(2)}, u32[]{:S(2)}) %all-to-all-start.2) | async-done | bytes 1310752 | tf_op jit(solution)/shard_map/all_to_all | solution.py:18
  139.5 7.4 %node_sum.2 = (f32[32,8,256]{2,1,0:T(8,128)S(1)}, f32[32,8,256]{2,1,0:T(8,128)S(1)}) custom-call(s32[1]{0:T(128)} %bitcast.3.core_ref, f32[8,320,512]{2,1,0:T(8,128)} %all-to-all-done.1.left_ref, f32[8,160,256]{2,1,0:T(8,128)S(1)} %all-to-all-done.2.right_ref), custom_call_target="tpu_custom_call" | custom-call | flops 335544320 | bytes 5000000 | tf_op jit(solution)/shard_map/node_sum/pallas_call | solution.py:142
  146.9 4.9 %collective-permute-start = (f32[32,8,256]{2,1,0:T(8,128)S(1)}, f32[32,8,256]{2,1,0:T(8,128)S(1)}, u32[]{:S(2)}, u32[]{:S(2)}) collective-permute-start(f32[32,8,256]{2,1,0:T(8,128)S(1)} %get-tuple-element.13), channel_id=1, source_target_pairs={{0,8},{8,0},{1,9},{9,1},{2,10},{10,2},{3,11},{11,3},{4,12},{12,4},... | collective-permute-start | bytes 786440 | tf_op jit(solution)/shard_map/ppermute | solution.py:189
  151.9 1.0 add.19
  152.9 0.1 collective-permute-done
  153.1 0.8 pad_maximum_fusion
  153.9 10.5 %all-to-all-start.4 = ((f32[32,16,256]{2,1,0:T(8,128)}), f32[32,16,256]{2,1,0:T(8,128)S(1)}, u32[]{:S(2)}, u32[]{:S(2)}) async-start(f32[32,16,256]{2,1,0:T(8,128)} %pad_maximum_fusion), calls=%async_computation.4 | async-start | bytes 1048576 | tf_op jit(solution)/shard_map/all_to_all | solution.py:18
  164.4 1.9 %convolution_convert_fusion = bf16[160,4096]{1,0:T(8,128)(2,1)} fusion(bf16[4096,256]{1,0:T(8,128)(2,1)S(1)} %copy-done.6, f32[160,256]{1,0:T(8,128)S(1)} %get-tuple-element.10), kind=kOutput, calls=%fused_computation | convolution fusion | flops 336240640 | bytes 3571712 | tf_op jit(solution)/shard_map/dot_general | solution.py:195
  166.3 15.0 %all-to-all-done.4 = f32[32,16,256]{2,1,0:T(8,128)S(1)} async-done(((f32[32,16,256]{2,1,0:T(8,128)}), f32[32,16,256]{2,1,0:T(8,128)S(1)}, u32[]{:S(2)}, u32[]{:S(2)}) %all-to-all-start.4) | async-done | bytes 524320 | tf_op jit(solution)/shard_map/all_to_all | solution.py:18
  181.3 0.6 fusion.3
  (19 shorter events, 0.2 us)
Async XLA Ops:
  7.2 0.7 copy-start
  7.2 16.0 %copy-start.3 = (bf16[160,4096]{1,0:T(8,128)(2,1)S(1)}, bf16[160,4096]{1,0:T(8,128)(2,1)}, u32[]{:S(2)}) copy-start(bf16[160,4096]{1,0:T(8,128)(2,1)} %tokens_ref.3) | copy-start | bytes 3932164
  7.2 16.0 %copy-start.4 = (bf16[160,4096]{1,0:T(8,128)(2,1)S(1)}, bf16[160,4096]{1,0:T(8,128)(2,1)}, u32[]{:S(2)}) copy-start(bf16[160,4096]{1,0:T(8,128)(2,1)} %grads_ref.3) | copy-start | bytes 3932164
  7.2 80.6 %all-gather.3.cloned.1.call-start = ((), (), s32[]{:S(2)}) async-start(), calls=%async_computation.5 | async-start | bytes 8912896 | tf_op jit(solution)/shard_map/all_gather | solution.py:183
  23.9 2.3 %copy-start.2 = (f32[8,320,512]{2,1,0:T(8,128)}, f32[8,320,512]{2,1,0:T(8,128)S(1)}, u32[]{:S(2)}) copy-start(f32[8,320,512]{2,1,0:T(8,128)S(1)} %cut_columns.1) | copy-start | bytes 15728644
  26.2 69.4 %all-to-all-start.1 = ((f32[8,320,512]{2,1,0:T(8,128)}), f32[8,320,512]{2,1,0:T(8,128)}, u32[]{:S(2)}, u32[]{:S(2)}) async-start(f32[8,320,512]{2,1,0:T(8,128)} %copy-done.2), calls=%async_computation.1 | async-start | bytes 10485760 | tf_op jit(solution)/shard_map/all_to_all | solution.py:18
  87.8 3.4 %copy-start.1 = (f32[128,2,32,256]{3,2,1,0:T(8,128)S(1)}, f32[128,2,32,256]{3,2,1,0:T(8,128)}, u32[]{:S(2)}) copy-start(f32[128,2,32,256]{3,2,1,0:T(8,128)} %all-gather.3.cloned.1.call-done) | copy-start | bytes 25165828
  94.3 1.3 copy-start.5
  119.4 20.1 %all-to-all-start.2 = ((f32[8,160,256]{2,1,0:T(8,128)}), f32[8,160,256]{2,1,0:T(8,128)S(1)}, u32[]{:S(2)}, u32[]{:S(2)}) async-start(f32[8,160,256]{2,1,0:T(8,128)} %broadcast_in_dim.32), calls=%async_computation.2 | async-start | bytes 2621440 | tf_op jit(solution)/shard_map/all_to_all | solution.py:18
  130.5 21.4 %collective-permute-start.1 = (f32[32,8,256]{2,1,0:T(8,128)S(1)}, f32[32,8,256]{2,1,0:T(8,128)}, u32[]{:S(2)}, u32[]{:S(2)}) collective-permute-start(f32[32,8,256]{2,1,0:T(8,128)S(1)} %get-tuple-element.16), channel_id=1, source_target_pairs={{0,8},{8,0},{1,9},{9,1},{2,10},{10,2},{3,11},{11,3},{4,12},{12,4},... | collective-permute-start | bytes 786440 | tf_op jit(solution)/shard_map/ppermute | solution.py:189
  146.9 17.4 %copy-start.6 = (bf16[4096,256]{1,0:T(8,128)(2,1)S(1)}, bf16[4096,256]{1,0:T(8,128)(2,1)}, u32[]{:S(2)}) copy-start(bf16[4096,256]{1,0:T(8,128)(2,1)} %copy-done.5) | copy-start | bytes 6291460
  146.9 6.1 %collective-permute-start = (f32[32,8,256]{2,1,0:T(8,128)S(1)}, f32[32,8,256]{2,1,0:T(8,128)S(1)}, u32[]{:S(2)}, u32[]{:S(2)}) collective-permute-start(f32[32,8,256]{2,1,0:T(8,128)S(1)} %get-tuple-element.13), channel_id=1, source_target_pairs={{0,8},{8,0},{1,9},{9,1},{2,10},{10,2},{3,11},{11,3},{4,12},{12,4},... | collective-permute-start | bytes 786440 | tf_op jit(solution)/shard_map/ppermute | solution.py:189
  153.9 27.3 %all-to-all-start.4 = ((f32[32,16,256]{2,1,0:T(8,128)}), f32[32,16,256]{2,1,0:T(8,128)S(1)}, u32[]{:S(2)}, u32[]{:S(2)}) async-start(f32[32,16,256]{2,1,0:T(8,128)} %pad_maximum_fusion), calls=%async_computation.4 | async-start | bytes 1048576 | tf_op jit(solution)/shard_map/all_to_all | solution.py:18
Sparse Core Ops, SparseCore 0:
  23.3 64.4 all-gather.2

commit v3 on v2

--- a/solution.py
+++ b/solution.py
@@ -11,29 +11,36 @@
 AXES = ("yh", "z", "c", "x", "yl")
 LOCAL = ("x", "yl")
 GROUP = ("z", "c")
-VMEM_LIMIT = 40 * 1024 * 1024
+VMEM_LIMIT = 56 * 1024 * 1024
 
 
 def exchange(array, axes):
     return lax.all_to_all(array, axes, split_axis=0, concat_axis=0, tiled=True)
 
 
-def clip_blocks(values):
-    parts = []
-    for k in range(values.shape[1] // QBLOCK):
-        block = values[:, k * QBLOCK : (k + 1) * QBLOCK]
-        mean = jnp.mean(block * block, axis=-1, keepdims=True)
-        scale = 2.0 * jnp.sqrt(mean + 1e-06) / 7.0
-        codes = jnp.clip(block * (1.0 / scale), -7.0, 7.0).astype(jnp.bfloat16)
-        parts.append(codes.astype(jnp.float32) * scale)
-    return jnp.concatenate(parts, axis=1)
+def clip_blocks(values, averages):
+    squares = values * values
+    high = squares.astype(jnp.bfloat16)
+    low = (squares - high.astype(jnp.float32)).astype(jnp.bfloat16)
+    mean = jnp.dot(high, averages, preferred_element_type=jnp.float32)
+    mean += jnp.dot(low, averages, preferred_element_type=jnp.float32)
+    mean += 1e-06
+    root = lax.rsqrt(mean)
+    codes = jnp.clip(values * (3.5 * root), -7.0, 7.0).astype(jnp.bfloat16)
+    return codes.astype(jnp.float32) * (mean * root * (2.0 / 7.0))
+
+
+def block_averages(width):
+    rows = lax.broadcasted_iota(jnp.int32, (width, width), 0) // QBLOCK
+    columns = lax.broadcasted_iota(jnp.int32, (width, width), 1) // QBLOCK
+    return jnp.where(rows == columns, 1.0 / QBLOCK, 0.0).astype(jnp.bfloat16)
 
 
 def inner_tanh(v):
     return jnp.tanh(math.sqrt(2.0 / math.pi) * (v + 0.044715 * v * v * v))
 
 
-def hidden_kernel(up_ref, down_ref, tokens_ref, grads_ref, act_ref, hidden_ref, upw_ref, pre, back):
+def hidden_kernel(up_ref, down_ref, tokens_ref, grads_ref, both_ref, upw_ref, pre, back):
     step = pl.program_id(0)
 
     @pl.when(step == 0)
@@ -52,17 +59,19 @@
     def _():
         v = pre[...]
         t = inner_tanh(v)
-        act_ref[...] = (0.5 * v * (1.0 + t)).astype(jnp.bfloat16).astype(jnp.float32)
+        act = (0.5 * v * (1.0 + t)).astype(jnp.bfloat16).astype(jnp.float32)
         slope = 0.5 * (1.0 + t) + 0.5 * v * (1.0 - t * t) * math.sqrt(2.0 / math.pi) * (
             1.0 + 3.0 * 0.044715 * v * v
         )
-        hidden_ref[...] = (back[...] * slope).astype(jnp.bfloat16).astype(jnp.float32)
+        hidden = (back[...] * slope).astype(jnp.bfloat16).astype(jnp.float32)
+        for k in range(both_ref.shape[0]):
+            both_ref[k, 0] = hidden
+            both_ref[k, 1] = act
 
 
 def hidden_pass(weights, tokens, grads):
     groups, n, _, piece, width = weights.shape
     rows, depth = tokens.shape
-    whole = pl.BlockSpec((rows, width), lambda k: (0, 0))
     block = (groups, None, None, piece, width)
     cut = pl.BlockSpec((rows, depth // n), lambda k: (0, k))
     return pl.pallas_call(
@@ -74,10 +83,12 @@
             cut,
             cut,
         ],
-        out_specs=[whole, whole, pl.BlockSpec((depth // n, width), lambda k: (k, 0))],
+        out_specs=[
+            pl.BlockSpec((n, 2, rows, width), lambda k: (0, 0, 0, 0)),
+            pl.BlockSpec((depth // n, width), lambda k: (k, 0)),
+        ],
         out_shape=[
-            jax.ShapeDtypeStruct((rows, width), jnp.float32),
-            jax.ShapeDtypeStruct((rows, width), jnp.float32),
+            jax.ShapeDtypeStruct((n, 2, rows, width), jnp.float32),
             jax.ShapeDtypeStruct((depth, width), jnp.bfloat16),
         ],
         scratch_shapes=[pltpu.VMEM((rows, width), jnp.float32)] * 2,
@@ -123,12 +134,13 @@
         (((0,), (0,)), ((), ())),
         preferred_element_type=jnp.float32,
     )
-    total[...] += clip_blocks(term)
+    averages = block_averages(term.shape[1])
+    total[...] += clip_blocks(term, averages)
 
     @pl.when(step == pl.num_programs(0) - 1)
     def _():
         pairs, rows, width = mine_ref.shape
-        summed = clip_blocks(total[...]).reshape(pairs, 2, rows, width)
+        summed = clip_blocks(total[...], averages).reshape(pairs, 2, rows, width)
         first = core_ref[0] == 0
         mine_ref[...] = jnp.where(first, summed[:, 0], summed[:, 1])
         other_ref[...] = jnp.where(first, summed[:, 1], summed[:, 0])
@@ -136,7 +148,7 @@
 
 def node_sum(core, left, which, right, owned):
     height = left.shape[2]
-    n, rows, width = right.shape
+    n, _, rows, width = right.shape
     half = (height // (2 * owned), owned, width)
     out = pl.BlockSpec(half, lambda k, core_ref: (0, 0, 0))
     return pl.pallas_call(
@@ -146,7 +158,7 @@
             grid=(n,),
             in_specs=[
                 pl.BlockSpec((None, rows, height), lambda k, core_ref: (k, which, 0)),
-                pl.BlockSpec((None, rows, width), lambda k, core_ref: (k, 0, 0)),
+                pl.BlockSpec((None, None, rows, width), lambda k, core_ref: (k, which, 0, 0)),
             ],
             out_specs=[out, out],
             scratch_shapes=[pltpu.VMEM((height, width), jnp.float32)],
@@ -180,18 +192,19 @@
         return exchange(jnp.broadcast_to(array[None], (n_local,) + array.shape), LOCAL)
 
     pieces = to_all(jnp.stack([product(up_codes, up_scales), product(down_codes, down_scales)]))
+    pieces, cut = lax.optimization_barrier((pieces, cut_columns(tokens, out_grad, n_local)))
     weights = lax.all_gather(pieces, GROUP, axis=0)
-    columns = exchange(cut_columns(tokens, out_grad, n_local), LOCAL)
-    activated, hidden, up = hidden_pass(weights, tokens, out_grad)
-
-    def over_cores(which, right):
-        mine, other = node_sum(core[None], columns, which, right, owned)
+    columns = exchange(cut, LOCAL)
+    both, up = hidden_pass(weights, tokens, out_grad)
+    hidden = both[0, 0]
+    both_all = exchange(both, LOCAL)
+
+    def over_cores(which):
+        mine, other = node_sum(core[None], columns, which, both_all, owned)
         return mine + lax.ppermute(other, "c", [(0, 1), (1, 0)])
 
-    activated_all = to_all(activated)
-    hidden_all = to_all(hidden)
-    grad_down = over_cores(1, activated_all)
-    grad_up = over_cores(0, hidden_all)
+    grad_down = over_cores(1)
+    grad_up = over_cores(0)
     input_grad = lax.dot_general(
         hidden.astype(jnp.bfloat16), up, (((1,), (1,)), ((), ())), preferred_element_type=jnp.float32
     ).astype(jnp.bfloat16)

time: 192 us -> 198 us (1.031)
  Pallas kernels: 18.7 us -> 33.3 us
  local copies, waits for them, and re-layouts: 10.7 us -> 4.11 us
  starting transfers between devices: 27.3 us -> 24.8 us
    pallas_call x1, Pallas kernels: 3.1 us -> 9.31 us  [hidden_pass(): pl.pallas_call(hidden_kernel, grid=(n,), in_specs=[pl.BlockSpec(block, la...]
    unnamed x14 -> x8, local copies, waits for them, and re-layouts: 7.62 us -> 1.48 us
    pallas_call x1, Pallas kernels: 0.71 us -> 6.59 us  [cut_columns(): pl.pallas_call(cut_kernel, grid=(n,), in_specs=[cut, cut], out_specs=pl.B...]
    all_to_all x3, waiting for transfers between devices: 20.4 us -> 15.1 us  [exchange(): return lax.all_to_all(array, axes, split_axis=0, concat_axis=0, tiled=True)]
    ppermute x2, starting transfers between devices: 8.54 us -> 5.76 us  [over_cores(): return mine + lax.ppermute(other, 'c', [(0, 1), (1, 0)])]
    all_gather x1, waiting for transfers between devices: 56.9 us -> 59.6 us  [local(): weights = lax.all_gather(pieces, GROUP, axis=0)]
    pallas_call x2, Pallas kernels: 14.9 us -> 17.4 us  [node_sum(): pl.pallas_call(node_kernel, grid_spec=pltpu.PrefetchScalarGridSpec(num_sc...]
    all_to_all x2 -> x1, blocking collectives: 35.8 us -> 36.8 us  [exchange(): return lax.all_to_all(array, axes, split_axis=0, concat_axis=0, tiled=True)]
  transfers between devices with their start and end apart: 6 -> 6, of which waited for: 4 -> 4; matrix products, arithmetic and copies ran while one was open for 2% -> 1% of each run, Pallas kernels for 10% -> 13%
where the time goes in v3:
time: 198 us; the launch traced here: 195 us
  waiting for transfers between devices  76.4 us (39%)
  blocking collectives  36.8 us (19%)
  Pallas kernels  33.3 us (17%)
  starting transfers between devices  24.8 us (13%)
  between operations  14.1 us (7%)
  local copies, waits for them, and re-layouts  4.11 us (2%)
  matrix products  2.82 us (1%)
  other arithmetic  2.65 us (1%)
    all_gather x1, waiting for transfers between devices, local(): weights = lax.all_gather(pieces, GROUP, axis=0)  59.6 us
    all_to_all x1, blocking collectives, exchange(): return lax.all_to_all(array, axes, split_axis=0, concat_axis=0, tiled=True)  36.8 us
    all_to_all x3, starting transfers between devices, exchange(): return lax.all_to_all(array, axes, split_axis=0, concat_axis=0, tiled=True)  19.1 us
    pallas_call x2, Pallas kernels, node_sum(): pl.pallas_call(node_kernel, grid_spec=pltpu.PrefetchScalarGridSpec(num_sc...  17.4 us
    all_to_all x3, waiting for transfers between devices, exchange(): return lax.all_to_all(array, axes, split_axis=0, concat_axis=0, tiled=True)  15.1 us
    pallas_call x1, Pallas kernels, hidden_pass(): pl.pallas_call(hidden_kernel, grid=(n,), in_specs=[pl.BlockSpec(block, la...  9.31 us
    pallas_call x1, Pallas kernels, cut_columns(): pl.pallas_call(cut_kernel, grid=(n,), in_specs=[cut, cut], out_specs=pl.B...  6.59 us
    ppermute x2, starting transfers between devices, over_cores(): return mine + lax.ppermute(other, 'c', [(0, 1), (1, 0)])  5.76 us
  transfers between devices with their start and end apart: 6, of which 4 were waited for; matrix products, arithmetic and copies ran while one was open for 1% of the time, Pallas kernels for 13%

profile of v3, /device:TPU:1, one launch (start us, length us, event | category | flops | bytes accessed | tf_op | source)
XLA Modules:
  0.0 195.1 jit_solution(1678410176336666169)
XLA Ops:
  7.2 0.0 copy-start
  7.2 0.7 copy-done
  7.9 0.1 constant_dynamic-slice_fusion.1
  7.9 0.7 constant_dynamic-slice_fusion
  8.7 0.1 copy.12
  8.8 0.1 copy.11
  8.9 0.1 broadcast_in_dim.16
  9.0 0.1 broadcast_in_dim.17
  9.1 0.8 fusion.2
  9.8 0.8 broadcast_in_dim.18
  10.7 5.9 %all-to-all-start = ((f32[8,2,32,256]{3,2,1,0:T(8,128)}), f32[8,2,32,256]{3,2,1,0:T(8,128)S(1)}, u32[]{:S(2)}, u32[]{:S(2)}) async-start(f32[8,2,32,256]{3,2,1,0:T(8,128)} %broadcast_in_dim.18), calls=%async_computation | async-start | bytes 1048576 | tf_op jit(solution)/shard_map/all_to_all | solution.py:18
  16.5 0.0 all-gather.3.cloned.1.call-start
  16.6 6.6 %cut_columns.1 = f32[8,320,512]{2,1,0:T(8,128)} custom-call(bf16[160,4096]{1,0:T(8,128)(2,1)} %tokens_ref.3, bf16[160,4096]{1,0:T(8,128)(2,1)} %grads_ref.3), custom_call_target="tpu_custom_call" | custom-call | bytes 8000000 | tf_op jit(solution)/shard_map/cut_columns/pallas_call | solution.py:112
  23.2 0.9 all-to-all-done
  24.1 0.8 copy-done.2
  24.9 0.0 all-gather.3.cloned.1.call-update
  24.9 4.7 %all-to-all-start.1 = ((f32[8,320,512]{2,1,0:T(8,128)}), f32[8,320,512]{2,1,0:T(8,128)}, u32[]{:S(2)}, u32[]{:S(2)}) async-start(f32[8,320,512]{2,1,0:T(8,128)} %cut_columns.1), calls=%async_computation.1 | async-start | bytes 10485760 | tf_op jit(solution)/shard_map/all_to_all | solution.py:18
  29.6 59.6 %all-gather.3.cloned.1.call-done = f32[128,2,32,256]{3,2,1,0:T(8,128)} async-done(((f32[8,2,32,256]{3,2,1,0:T(8,128)}), f32[128,2,32,256]{3,2,1,0:T(8,128)}) %all-gather.3.cloned.1.call-update) | async-done | bytes 8388624 | tf_op jit(solution)/shard_map/all_gather | solution.py:196
  89.2 9.3 %hidden_pass.1 = (f32[8,2,160,256]{3,2,1,0:T(8,128)}, bf16[4096,256]{1,0:T(8,128)(2,1)}) custom-call(f32[16,8,2,32,256]{4,3,2,1,0:T(8,128)} %bitcast.20, f32[16,8,2,32,256]{4,3,2,1,0:T(8,128)} %bitcast.21, bf16[160,4096]{1,0:T(8,128)(2,1)} %tokens_ref.3, bf16[160,4096]{1,0:T(8,128)(2,1)} %grads_ref.3), custom_call_target="tpu_custom_call" | custom-call | flops 671088640 | bytes 13000000 | tf_op jit(solution)/shard_map/hidden_pass/pallas_call | solution.py:77
  98.5 0.0 all-to-all-done.1.left_ref
  98.5 36.8 %all_to_all.20.right_ref = f32[8,2,160,256]{3,2,1,0:T(8,128)} all-to-all(f32[8,2,160,256]{3,2,1,0:T(8,128)} %get-tuple-element.12), channel_id=1, replica_groups=mesh['yh'=4,'z'=8,'c'=2,'x'=4,'yl'=2] {'x','yl'}, dimensions={0} | all-to-all | bytes 5242880 | tf_op jit(solution)/shard_map/all_to_all | solution.py:18
  135.3 8.7 %node_sum.3 = (f32[32,8,256]{2,1,0:T(8,128)}, f32[32,8,256]{2,1,0:T(8,128)}) custom-call(s32[1]{0:T(128)} %bitcast.4.core_ref, f32[8,320,512]{2,1,0:T(8,128)} %all-to-all-done.1.left_ref, f32[8,2,160,256]{3,2,1,0:T(8,128)} %all_to_all.20.right_ref), custom_call_target="tpu_custom_call" | custom-call | flops 335544320 | bytes 5000000 | tf_op jit(solution)/shard_map/node_sum/pallas_call | solution.py:154
  144.0 3.7 %collective-permute-start.1 = (f32[32,8,256]{2,1,0:T(8,128)}, f32[32,8,256]{2,1,0:T(8,128)S(1)}, u32[]{:S(2)}, u32[]{:S(2)}) collective-permute-start(f32[32,8,256]{2,1,0:T(8,128)} %get-tuple-element.18), channel_id=1, source_target_pairs={{0,8},{8,0},{1,9},{9,1},{2,10},{10,2},{3,11},{11,3},{4,12},{12,4},... | collective-permute-start | bytes 786440 | tf_op jit(solution)/shard_map/ppermute | solution.py:204
  147.8 8.7 %node_sum.2 = (f32[32,8,256]{2,1,0:T(8,128)}, f32[32,8,256]{2,1,0:T(8,128)}) custom-call(s32[1]{0:T(128)} %bitcast.4.core_ref, f32[8,320,512]{2,1,0:T(8,128)} %all-to-all-done.1.left_ref, f32[8,2,160,256]{3,2,1,0:T(8,128)} %all_to_all.20.right_ref), custom_call_target="tpu_custom_call" | custom-call | flops 335544320 | bytes 5000000 | tf_op jit(solution)/shard_map/node_sum/pallas_call | solution.py:154
  156.5 2.0 %collective-permute-start = (f32[32,8,256]{2,1,0:T(8,128)}, f32[32,8,256]{2,1,0:T(8,128)S(1)}, u32[]{:S(2)}, u32[]{:S(2)}) collective-permute-start(f32[32,8,256]{2,1,0:T(8,128)} %get-tuple-element.16), channel_id=1, source_target_pairs={{0,8},{8,0},{1,9},{9,1},{2,10},{10,2},{3,11},{11,3},{4,12},{12,4},... | collective-permute-start | bytes 786440 | tf_op jit(solution)/shard_map/ppermute | solution.py:204
  158.6 1.6 collective-permute-done
  160.2 1.0 add.18
  161.2 0.8 pad_maximum_fusion
  162.0 8.5 %all-to-all-start.3 = ((f32[32,16,256]{2,1,0:T(8,128)}), f32[32,16,256]{2,1,0:T(8,128)S(1)}, u32[]{:S(2)}, u32[]{:S(2)}) async-start(f32[32,16,256]{2,1,0:T(8,128)} %pad_maximum_fusion), calls=%async_computation.3 | async-start | bytes 1048576 | tf_op jit(solution)/shard_map/all_to_all | solution.py:18
  170.5 2.8 %convolution_convert_fusion = bf16[160,4096]{1,0:T(8,128)(2,1)} fusion(bf16[4096,256]{1,0:T(8,128)(2,1)S(1)} %copy-done.1, f32[8,2,160,256]{3,2,1,0:T(8,128)} %get-tuple-element.12), kind=kOutput, calls=%fused_computation | convolution fusion | flops 336199680 | bytes 3489792 | tf_op jit(solution)/shard_map/dot_general | solution.py:208
  173.3 14.2 %all-to-all-done.3 = f32[32,16,256]{2,1,0:T(8,128)S(1)} async-done(((f32[32,16,256]{2,1,0:T(8,128)}), f32[32,16,256]{2,1,0:T(8,128)S(1)}, u32[]{:S(2)}, u32[]{:S(2)}) %all-to-all-start.3) | async-done | bytes 524320 | tf_op jit(solution)/shard_map/all_to_all | solution.py:18
  187.6 0.6 fusion.4
  (10 shorter events, 0.1 us)
Async XLA Ops:
  7.2 0.7 copy-start
  10.7 13.4 %all-to-all-start = ((f32[8,2,32,256]{3,2,1,0:T(8,128)}), f32[8,2,32,256]{3,2,1,0:T(8,128)S(1)}, u32[]{:S(2)}, u32[]{:S(2)}) async-start(f32[8,2,32,256]{3,2,1,0:T(8,128)} %broadcast_in_dim.18), calls=%async_computation | async-start | bytes 1048576 | tf_op jit(solution)/shard_map/all_to_all | solution.py:18
  16.5 72.7 %all-gather.3.cloned.1.call-start = ((), (), s32[]{:S(2)}) async-start(), calls=%async_computation.4 | async-start | bytes 8912896 | tf_op jit(solution)/shard_map/all_gather | solution.py:196
  24.1 0.8 copy-start.2
  24.9 73.6 %all-to-all-start.1 = ((f32[8,320,512]{2,1,0:T(8,128)}), f32[8,320,512]{2,1,0:T(8,128)}, u32[]{:S(2)}, u32[]{:S(2)}) async-start(f32[8,320,512]{2,1,0:T(8,128)} %cut_columns.1), calls=%async_computation.1 | async-start | bytes 10485760 | tf_op jit(solution)/shard_map/all_to_all | solution.py:18
  144.0 14.5 %copy-start.3 = (f32[32,8,256]{2,1,0:T(8,128)S(1)}, f32[32,8,256]{2,1,0:T(8,128)}, u32[]{:S(2)}) copy-start(f32[32,8,256]{2,1,0:T(8,128)} %get-tuple-element.17) | copy-start | bytes 786436
  144.0 14.5 %collective-permute-start.1 = (f32[32,8,256]{2,1,0:T(8,128)}, f32[32,8,256]{2,1,0:T(8,128)S(1)}, u32[]{:S(2)}, u32[]{:S(2)}) collective-permute-start(f32[32,8,256]{2,1,0:T(8,128)} %get-tuple-element.18), channel_id=1, source_target_pairs={{0,8},{8,0},{1,9},{9,1},{2,10},{10,2},{3,11},{11,3},{4,12},{12,4},... | collective-permute-start | bytes 786440 | tf_op jit(solution)/shard_map/ppermute | solution.py:204
  156.5 14.0 %copy-start.1 = (bf16[4096,256]{1,0:T(8,128)(2,1)S(1)}, bf16[4096,256]{1,0:T(8,128)(2,1)}, u32[]{:S(2)}) copy-start(bf16[4096,256]{1,0:T(8,128)(2,1)} %get-tuple-element.13) | copy-start | bytes 6291460
  156.5 3.8 %collective-permute-start = (f32[32,8,256]{2,1,0:T(8,128)}, f32[32,8,256]{2,1,0:T(8,128)S(1)}, u32[]{:S(2)}, u32[]{:S(2)}) collective-permute-start(f32[32,8,256]{2,1,0:T(8,128)} %get-tuple-element.16), channel_id=1, source_target_pairs={{0,8},{8,0},{1,9},{9,1},{2,10},{10,2},{3,11},{11,3},{4,12},{12,4},... | collective-permute-start | bytes 786440 | tf_op jit(solution)/shard_map/ppermute | solution.py:204
  162.0 25.5 %all-to-all-start.3 = ((f32[32,16,256]{2,1,0:T(8,128)}), f32[32,16,256]{2,1,0:T(8,128)S(1)}, u32[]{:S(2)}, u32[]{:S(2)}) async-start(f32[32,16,256]{2,1,0:T(8,128)} %pad_maximum_fusion), calls=%async_computation.3 | async-start | bytes 1048576 | tf_op jit(solution)/shard_map/all_to_all | solution.py:18
Sparse Core Ops, SparseCore 0:
  25.0 64.1 all-gather.2

commit v4 on v3

v4 whole, which is shorter than its diff:
```python
import functools
import math
import jax
import jax.numpy as jnp
from jax import lax
from jax.experimental import pallas as pl
from jax.experimental.pallas import tpu as pltpu
from jax.sharding import Mesh, PartitionSpec as P

QBLOCK = 128
AXES = ("yh", "z", "c", "x", "yl")
LOCAL = ("x", "yl")
GROUP = ("z", "c")
SHARDS = 2
VMEM_LIMIT = 16 * 1024 * 1024


def exchange(array, axes):
    return lax.all_to_all(array, axes, split_axis=0, concat_axis=0, tiled=True)


def clip_blocks(values):
    parts = []
    for k in range(values.shape[0] // QBLOCK):
        block = values[k * QBLOCK : (k + 1) * QBLOCK]
        mean = jnp.mean(block * block, axis=0, keepdims=True) + 1e-06
        root = lax.rsqrt(mean)
        codes = jnp.clip(block * (3.5 * root), -7.0, 7.0).astype(jnp.bfloat16)
        parts.append(codes.astype(jnp.float32) * (mean * root * (2.0 / 7.0)))
    return jnp.concatenate(parts, axis=0)


def inner_tanh(v):
    return jnp.tanh(math.sqrt(2.0 / math.pi) * (v + 0.044715 * v * v * v))


def hidden_kernel(weights_ref, tokens_ref, grads_ref, both_ref, pre, back):
    step = pl.program_id(0)

    @pl.when(step == 0)
    def _():
        pre[...] = jnp.zeros_like(pre)
        back[...] = jnp.zeros_like(back)

    _, shards, _, _, width = weights_ref.shape
    shard = tokens_ref.shape[1] // shards
    for q in range(shards):
        up = weights_ref[:, q, 0].reshape(shard, width).astype(jnp.bfloat16)
        down = weights_ref[:, q, 1].reshape(shard, width).astype(jnp.bfloat16)
        columns = slice(q * shard, (q + 1) * shard)
        pre[...] += jnp.dot(tokens_ref[:, columns], up, preferred_element_type=jnp.float32)
        back[...] += jnp.dot(grads_ref[:, columns], down, preferred_element_type=jnp.float32)

    @pl.when(step == pl.num_programs(0) - 1)
    def _():
        v = pre[...]
        t = inner_tanh(v)
        act = (0.5 * v * (1.0 + t)).astype(jnp.bfloat16).astype(jnp.float32)
        slope = 0.5 * (1.0 + t) + 0.5 * v * (1.0 - t * t) * math.sqrt(2.0 / math.pi) * (
            1.0 + 3.0 * 0.044715 * v * v
        )
        hidden = (back[...] * slope).astype(jnp.bfloat16).astype(jnp.float32)
        for k in range(both_ref.shape[0]):
            both_ref[k, 0] = hidden
            both_ref[k, 1] = act


def hidden_pass(weights, tokens, grads):
    groups, n, kinds, piece, width = weights.shape
    rows, depth = tokens.shape
    cut = pl.BlockSpec((rows, SHARDS * depth // n), lambda k: (0, k))
    return pl.pallas_call(
        hidden_kernel,
        grid=(n // SHARDS,),
        in_specs=[
            pl.BlockSpec((groups, SHARDS, kinds, piece, width), lambda k: (0, k, 0, 0, 0)),
            cut,
            cut,
        ],
        out_specs=pl.BlockSpec((n, 2, rows, width), lambda k: (0, 0, 0, 0)),
        out_shape=jax.ShapeDtypeStruct((n, 2, rows, width), jnp.float32),
        scratch_shapes=[pltpu.VMEM((rows, width), jnp.float32)] * 2,
        compiler_params=pltpu.CompilerParams(vmem_limit_bytes=VMEM_LIMIT),
        cost_estimate=pl.CostEstimate(
            flops=4 * rows * depth * width, bytes_accessed=13000000, transcendentals=rows * width
        ),
        name="hidden_pass",
    )(weights, tokens, grads)


def input_kernel(hidden_ref, weights_ref, out_ref):
    _, shards, _, width = weights_ref.shape
    shard = out_ref.shape[1] // shards
    hidden = hidden_ref[...].astype(jnp.bfloat16)
    for q in range(shards):
        up = weights_ref[:, q].reshape(shard, width).astype(jnp.bfloat16)
        out_ref[:, q * shard : (q + 1) * shard] = lax.dot_general(
            hidden, up, (((1,), (1,)), ((), ())), preferred_element_type=jnp.float32
        ).astype(out_ref.dtype)


def input_pass(both, weights):
    groups, n, _, piece, width = weights.shape
    rows = both.shape[2]
    depth = groups * n * piece
    return pl.pallas_call(
        input_kernel,
        grid=(n // SHARDS,),
        in_specs=[
            pl.BlockSpec((None, None, rows, width), lambda k: (0, 0, 0, 0)),
            pl.BlockSpec((groups, SHARDS, None, piece, width), lambda k: (0, k, 0, 0, 0)),
        ],
        out_specs=pl.BlockSpec((rows, SHARDS * depth // n), lambda k: (0, k)),
        out_shape=jax.ShapeDtypeStruct((rows, depth), jnp.bfloat16),
        compiler_params=pltpu.CompilerParams(vmem_limit_bytes=VMEM_LIMIT),
        cost_estimate=pl.CostEstimate(
            flops=2 * rows * depth * width, bytes_accessed=6000000, transcendentals=0
        ),
        name="input_pass",
    )(both, weights)


def piece_kernel(place_ref, up_ref, up_scales_ref, down_ref, down_scales_ref, out_ref):
    piece, width = up_ref.shape
    shard = up_scales_ref.shape[1]
    shape = (piece, shard)
    wanted = lax.broadcasted_iota(jnp.int32, shape, 0) + place_ref[0] * piece
    chosen = wanted == lax.broadcasted_iota(jnp.int32, shape, 1)
    for kind, (codes, scales) in enumerate(((up_ref, up_scales_ref), (down_ref, down_scales_ref))):
        for k in range(width // QBLOCK):
            own = jnp.sum(jnp.where(chosen, scales[k : k + 1], 0.0), axis=1, keepdims=True)
            columns = slice(k * QBLOCK, (k + 1) * QBLOCK)
            product = codes[:, columns].astype(jnp.float32) * own
            for p in range(out_ref.shape[0]):
                out_ref[p, kind, :, columns] = product


def make_pieces(place, n_group, n_local, up_codes, up_scales, down_codes, down_scales):
    shard, width = up_codes.shape
    piece = shard // n_group
    codes = pl.BlockSpec((piece, width), lambda k, place_ref: (place_ref[0], 0))
    scales = pl.BlockSpec(up_scales.T.shape, lambda k, place_ref: (0, 0))
    out = (n_local, 2, piece, width)
    return pl.pallas_call(
        piece_kernel,
        grid_spec=pltpu.PrefetchScalarGridSpec(
            num_scalar_prefetch=1,
            grid=(1,),
            in_specs=[codes, scales, codes, scales],
            out_specs=pl.BlockSpec(out, lambda k, place_ref: (0, 0, 0, 0)),
        ),
        out_shape=jax.ShapeDtypeStruct(out, jnp.float32),
        compiler_params=pltpu.CompilerParams(vmem_limit_bytes=VMEM_LIMIT),
        name="make_pieces",
    )(place[None], up_codes, up_scales.T, down_codes, down_scales.T)


def narrow_kernel(columns_ref, out_ref):
    out_ref[...] = columns_ref[...].astype(out_ref.dtype)


def narrow(columns):
    n = columns.shape[0]
    block = pl.BlockSpec((n // 2,) + columns.shape[1:], lambda k: (k, 0, 0))
    return pl.pallas_call(
        narrow_kernel,
        grid=(2,),
        in_specs=[block],
        out_specs=block,
        out_shape=jax.ShapeDtypeStruct(columns.shape, jnp.bfloat16),
        compiler_params=pltpu.CompilerParams(vmem_limit_bytes=VMEM_LIMIT),
        cost_estimate=pl.CostEstimate(flops=0, bytes_accessed=12000000, transcendentals=0),
        name="narrow",
    )(columns)


def cut_kernel(tokens_ref, grads_ref, out_ref):
    rows = tokens_ref.shape[0]
    out_ref[:rows] = tokens_ref[...].astype(jnp.float32)
    out_ref[rows:] = grads_ref[...].astype(jnp.float32)


def cut_columns(tokens, grads, n):
    rows, depth = tokens.shape
    cut = pl.BlockSpec((rows, depth // n), lambda k: (0, k))
    return pl.pallas_call(
        cut_kernel,
        grid=(n,),
        in_specs=[cut, cut],
        out_specs=pl.BlockSpec((None, 2 * rows, depth // n), lambda k: (k, 0, 0)),
        out_shape=jax.ShapeDtypeStruct((n, 2 * rows, depth // n), jnp.float32),
        compiler_params=pltpu.CompilerParams(vmem_limit_bytes=VMEM_LIMIT),
        cost_estimate=pl.CostEstimate(flops=0, bytes_accessed=8000000, transcendentals=0),
        name="cut_columns",
    )(tokens, grads)


def node_kernel(core_ref, left_ref, right_ref, mine_ref, other_ref):
    n, kinds, rows, _ = right_ref.shape
    owned = mine_ref.shape[1] // kinds
    for kind in range(kinds):
        total = None
        for p in range(n):
            term = lax.dot_general(
                right_ref[p, kind].astype(jnp.bfloat16),
                left_ref[p, kind * rows : (kind + 1) * rows],
                (((0,), (0,)), ((), ())),
                preferred_element_type=jnp.float32,
            )
            total = clip_blocks(term) if total is None else total + clip_blocks(term)
        summed = clip_blocks(total).T.reshape(mine_ref.shape[0], 2, owned, total.shape[0])
        first = core_ref[0] == 0
        part = slice(kind * owned, (kind + 1) * owned)
        mine_ref[:, part] = jnp.where(first, summed[:, 0], summed[:, 1])
        other_ref[:, part] = jnp.where(first, summed[:, 1], summed[:, 0])


def node_sums(core, left, right, owned):
    height = left.shape[2]
    n, kinds, rows, width = right.shape
    half = (height // (2 * owned), kinds * owned, width)
    out = pl.BlockSpec(half, lambda k, core_ref: (0, 0, 0))
    return pl.pallas_call(
        node_kernel,
        grid_spec=pltpu.PrefetchScalarGridSpec(
            num_scalar_prefetch=1,
            grid=(1,),
            in_specs=[
                pl.BlockSpec(left.shape, lambda k, core_ref: (0, 0, 0)),
                pl.BlockSpec(right.shape, lambda k, core_ref: (0, 0, 0, 0)),
            ],
            out_specs=[out, out],
        ),
        out_shape=[jax.ShapeDtypeStruct(half, jnp.float32)] * 2,
        compiler_params=pltpu.CompilerParams(vmem_limit_bytes=VMEM_LIMIT),
        cost_estimate=pl.CostEstimate(
            flops=4 * n * rows * height * width, bytes_accessed=9000000, transcendentals=0
        ),
        name="node_sums",
    )(core, left, right)


def local(tokens, out_grad, up_codes, up_scales, down_codes, down_scales):
    n_local = lax.axis_size(LOCAL)
    n_group = lax.axis_size(GROUP)
    devices_all = lax.axis_size(AXES)
    depth = tokens.shape[1]
    owned = depth // devices_all
    core = lax.axis_index("c")

    place = lax.axis_index(GROUP)
    pieces = exchange(
        make_pieces(place, n_group, n_local, up_codes, up_scales, down_codes, down_scales), LOCAL
    )
    pieces, cut = lax.optimization_barrier((pieces, cut_columns(tokens, out_grad, n_local)))
    weights = lax.all_gather(pieces, GROUP, axis=0)
    columns = exchange(cut, LOCAL)
    both = hidden_pass(weights, tokens, out_grad)
    both_all = exchange(both, LOCAL)

    mine, other = node_sums(core[None], narrow(columns), both_all, owned)
    input_grad = input_pass(both, weights)
    pairs = mine + lax.ppermute(other, "c", [(0, 1), (1, 0)])
    owned_sums = exchange(pairs, ("yh", "z"))
    grads = jnp.sum(owned_sums, axis=0) / devices_all
    return (input_grad, grads[:owned], grads[owned:])


def solution(mesh):
    fine = Mesh(mesh.devices.reshape(4, 8, 2, 4, 2), AXES)
    by_tokens = P(AXES, None)
    by_rows = P(LOCAL, None)
    owned_rows = P(LOCAL + ("yh", "z", "c"), None)
    return jax.shard_map(
        local,
        mesh=fine,
        in_specs=(by_tokens, by_tokens, by_rows, by_rows, by_rows, by_rows),
        out_specs=(by_tokens, owned_rows, owned_rows),
        check_vma=False,
    )
```

time: 198 us -> 181 us (0.914)
  blocking collectives: 36.8 us -> 0 us
  waiting for transfers between devices: 76.4 us -> 102 us
  Pallas kernels: 33.3 us -> 15.4 us
  local copies, waits for them, and re-layouts: 4.11 us -> 18.6 us
  matrix products: 2.82 us -> 0 us
  starting transfers between devices: 24.8 us -> 27.1 us
    all_to_all x1 -> x0, blocking collectives: 36.8 us -> none  [exchange(): return lax.all_to_all(array, axes, split_axis=0, concat_axis=0, tiled=True)]
    all_to_all x3 -> x4, waiting for transfers between devices: 15.1 us -> 41.1 us  [exchange(): return lax.all_to_all(array, axes, split_axis=0, concat_axis=0, tiled=True)]
    unnamed x8 -> x26, local copies, waits for them, and re-layouts: 1.48 us -> 18 us
    pallas_call x3 -> x5, Pallas kernels: 26.7 us -> 14.7 us  [the longest x1 3.94 us: hidden_pass(): pl.pallas_call(hidden_kernel, grid=(n // SHARDS,), in_specs=[pl.BlockSpec...]
    pallas_call x1, Pallas kernels: 6.59 us -> 0.69 us  [cut_columns(): pl.pallas_call(cut_kernel, grid=(n,), in_specs=[cut, cut], out_specs=pl.B...]
    all_to_all x3 -> x4, starting transfers between devices: 19.1 us -> 23.8 us  [exchange(): return lax.all_to_all(array, axes, split_axis=0, concat_axis=0, tiled=True)]
    dot_general x1 -> x0, matrix products: 2.82 us -> none  [local(): lax.dot_general(hidden.astype(jnp.bfloat16), up, (((1,), (1,)), ((), ()))...]
    ppermute x2 -> x1, starting transfers between devices: 5.76 us -> 3.31 us  [local(): pairs = mine + lax.ppermute(other, 'c', [(0, 1), (1, 0)])]
  transfers between devices with their start and end apart: 6 -> 6, of which waited for: 4 -> 5; matrix products, arithmetic and copies ran while one was open for 1% -> 0% of each run, Pallas kernels for 13% -> 6%
where the time goes in v4:
time: 181 us; the launch traced here: 178 us
  waiting for transfers between devices  102 us (56%)
  starting transfers between devices  27.1 us (15%)
  local copies, waits for them, and re-layouts  18.6 us (10%)
  Pallas kernels  15.4 us (9%)
  between operations  14.2 us (8%)
    all_gather x1, waiting for transfers between devices, local(): weights = lax.all_gather(pieces, GROUP, axis=0)  59.5 us
    all_to_all x4, waiting for transfers between devices, exchange(): return lax.all_to_all(array, axes, split_axis=0, concat_axis=0, tiled=True)  41.1 us
    all_to_all x4, starting transfers between devices, exchange(): return lax.all_to_all(array, axes, split_axis=0, concat_axis=0, tiled=True)  23.8 us
    unnamed x26, local copies, waits for them, and re-layouts  18 us
    pallas_call x1, Pallas kernels, hidden_pass(): pl.pallas_call(hidden_kernel, grid=(n // SHARDS,), in_specs=[pl.BlockSpec...  3.94 us
    pallas_call x1, Pallas kernels, node_sums(): pl.pallas_call(node_kernel, grid_spec=pltpu.PrefetchScalarGridSpec(num_sc...  3.69 us
  transfers between devices with their start and end apart: 6, of which 5 were waited for; matrix products, arithmetic and copies ran while one was open for 0% of the time, Pallas kernels for 6%

profile of v4, /device:TPU:1, one launch (start us, length us, event | category | flops | bytes accessed | tf_op | source)
XLA Modules:
  0.0 178.4 jit_solution(8207456866633703649)
XLA Ops:
  7.2 1.0 copy-done.8
  8.2 0.9 copy-done.9
  9.2 0.7 copy-done.10
  9.9 0.7 copy-done.11
  10.6 0.9 make_pieces.1
  11.5 5.9 %all-to-all-start = ((f32[8,2,32,256]{3,2,1,0:T(8,128)}), f32[8,2,32,256]{3,2,1,0:T(8,128)S(1)}, u32[]{:S(2)}, u32[]{:S(2)}) async-start(f32[8,2,32,256]{3,2,1,0:T(8,128)} %make_pieces.1), calls=%async_computation | async-start | bytes 1048576 | tf_op jit(solution)/shard_map/all_to_all | solution.py:19
  17.3 0.0 all-gather.3.cloned.1.call-start
  17.4 0.0 copy-start.6
  17.4 1.3 copy-done.6
  18.7 0.7 cut_columns.1
  19.4 2.4 %copy-done.2 = f32[8,320,512]{2,1,0:T(8,128)} copy-done((f32[8,320,512]{2,1,0:T(8,128)}, f32[8,320,512]{2,1,0:T(8,128)S(1)}, u32[]{:S(2)}) %copy-start.2) | copy-done | bytes 5242904
  21.8 3.0 %all-to-all-done = f32[8,2,32,256]{3,2,1,0:T(8,128)S(1)} async-done(((f32[8,2,32,256]{3,2,1,0:T(8,128)}), f32[8,2,32,256]{3,2,1,0:T(8,128)S(1)}, u32[]{:S(2)}, u32[]{:S(2)}) %all-to-all-start) | async-done | bytes 524320 | tf_op jit(solution)/shard_map/all_to_all | solution.py:19
  24.9 0.8 copy-done.12
  25.7 0.0 all-gather.3.cloned.1.call-update
  25.7 4.8 %all-to-all-start.1 = ((f32[8,320,512]{2,1,0:T(8,128)}), f32[8,320,512]{2,1,0:T(8,128)}, u32[]{:S(2)}, u32[]{:S(2)}) async-start(f32[8,320,512]{2,1,0:T(8,128)} %copy-done.2), calls=%async_computation.1 | async-start | bytes 10485760 | tf_op jit(solution)/shard_map/all_to_all | solution.py:19
  30.5 59.5 %all-gather.3.cloned.1.call-done = f32[128,2,32,256]{3,2,1,0:T(8,128)} async-done(((f32[8,2,32,256]{3,2,1,0:T(8,128)}), f32[128,2,32,256]{3,2,1,0:T(8,128)}) %all-gather.3.cloned.1.call-update) | async-done | bytes 8388624 | tf_op jit(solution)/shard_map/all_gather | solution.py:256
  90.0 3.4 %copy-done = f32[128,2,32,256]{3,2,1,0:T(8,128)S(1)} copy-done((f32[128,2,32,256]{3,2,1,0:T(8,128)S(1)}, f32[128,2,32,256]{3,2,1,0:T(8,128)}, u32[]{:S(2)}) %copy-start) | copy-done | bytes 8388632
  93.4 3.9 %hidden_pass.1.hidden_ref = f32[8,2,160,256]{3,2,1,0:T(8,128)} custom-call(f32[16,8,2,32,256]{4,3,2,1,0:T(8,128)S(1)} %bitcast.5, bf16[160,4096]{1,0:T(8,128)(2,1)S(1)} %copy-done.5, bf16[160,4096]{1,0:T(8,128)(2,1)S(1)} %copy-done.7), custom_call_target="tpu_custom_call" | custom-call | flops 671088640 | bytes 13000000 | tf_op jit(solution)/shard_map/hidden_pass/pallas_call | solution.py:72
  97.4 4.9 %all-to-all-start.2 = ((f32[8,2,160,256]{3,2,1,0:T(8,128)}), f32[8,2,160,256]{3,2,1,0:T(8,128)S(1)}, u32[]{:S(2)}, u32[]{:S(2)}) async-start(f32[8,2,160,256]{3,2,1,0:T(8,128)} %hidden_pass.1.hidden_ref), calls=%async_computation.2 | async-start | bytes 5242880 | tf_op jit(solution)/shard_map/all_to_all | solution.py:19
  102.2 2.7 %narrow.1.left_ref = bf16[8,320,512]{2,1,0:T(8,128)(2,1)S(1)} custom-call(f32[8,320,512]{2,1,0:T(8,128)} %all-to-all-done.1.columns_ref), custom_call_target="tpu_custom_call" | custom-call | bytes 12000000 | tf_op jit(solution)/shard_map/narrow/pallas_call | solution.py:165
  105.0 1.6 copy-done.3
  106.5 27.9 %all-to-all-done.2.right_ref = f32[8,2,160,256]{3,2,1,0:T(8,128)S(1)} async-done(((f32[8,2,160,256]{3,2,1,0:T(8,128)}), f32[8,2,160,256]{3,2,1,0:T(8,128)S(1)}, u32[]{:S(2)}, u32[]{:S(2)}) %all-to-all-start.2) | async-done | bytes 2621472 | tf_op jit(solution)/shard_map/all_to_all | solution.py:19
  134.4 1.7 copy-done.4
  136.1 3.7 %node_sums.1 = (f32[32,16,256]{2,1,0:T(8,128)S(1)}, f32[32,16,256]{2,1,0:T(8,128)S(1)}) custom-call(s32[1]{0:T(128)} %bitcast.4.core_ref, bf16[8,320,512]{2,1,0:T(8,128)(2,1)S(1)} %copy-done.4, f32[8,2,160,256]{3,2,1,0:T(8,128)S(1)} %all-to-all-done.2.right_ref), custom_call_target="tpu_custom_call" | custom-call | flops 671088640 | bytes 9000000 | tf_op jit(solution)/shard_map/node_sums/pallas_call | solution.py:223
  139.8 3.3 %collective-permute-start = (f32[32,16,256]{2,1,0:T(8,128)S(1)}, f32[32,16,256]{2,1,0:T(8,128)S(1)}, u32[]{:S(2)}, u32[]{:S(2)}) collective-permute-start(f32[32,16,256]{2,1,0:T(8,128)S(1)} %get-tuple-element.10), channel_id=1, source_target_pairs={{0,8},{8,0},{1,9},{9,1},{2,10},{10,2},{3,11},{11,3},{4,12},{12,4},... | collective-permute-start | bytes 1572872 | tf_op jit(solution)/shard_map/ppermute | solution.py:263
  143.2 1.5 collective-permute-done
  144.7 1.0 add.7
  145.6 8.2 %all-to-all-start.3 = ((f32[32,16,256]{2,1,0:T(8,128)}), f32[32,16,256]{2,1,0:T(8,128)S(1)}, u32[]{:S(2)}, u32[]{:S(2)}) async-start(f32[32,16,256]{2,1,0:T(8,128)} %add.7), calls=%async_computation.3 | async-start | bytes 1048576 | tf_op jit(solution)/shard_map/all_to_all | solution.py:19
  153.9 3.4 %copy-done.1 = f32[128,2,32,256]{3,2,1,0:T(8,128)S(1)} copy-done((f32[128,2,32,256]{3,2,1,0:T(8,128)S(1)}, f32[128,2,32,256]{3,2,1,0:T(8,128)}, u32[]{:S(2)}) %copy-start.1) | copy-done | bytes 8388632
  157.2 3.5 %input_pass.1 = bf16[160,4096]{1,0:T(8,128)(2,1)} custom-call(f32[8,2,160,256]{3,2,1,0:T(8,128)} %hidden_pass.1.hidden_ref, f32[16,8,2,32,256]{4,3,2,1,0:T(8,128)S(1)} %bitcast.6), custom_call_target="tpu_custom_call" | custom-call | flops 335544320 | bytes 6000000 | tf_op jit(solution)/shard_map/input_pass/pallas_call | solution.py:106
  160.7 10.2 %all-to-all-done.3 = f32[32,16,256]{2,1,0:T(8,128)S(1)} async-done(((f32[32,16,256]{2,1,0:T(8,128)}), f32[32,16,256]{2,1,0:T(8,128)S(1)}, u32[]{:S(2)}, u32[]{:S(2)}) %all-to-all-start.3) | async-done | bytes 524320 | tf_op jit(solution)/shard_map/all_to_all | solution.py:19
  171.0 0.6 fusion
  (17 shorter events, 0.1 us)
Async XLA Ops:
  7.2 10.2 %copy-start.5 = (bf16[160,4096]{1,0:T(8,128)(2,1)S(1)}, bf16[160,4096]{1,0:T(8,128)(2,1)}, u32[]{:S(2)}) copy-start(bf16[160,4096]{1,0:T(8,128)(2,1)} %tokens_ref.3) | copy-start | bytes 3932164
  7.2 1.1 copy-start.8
  8.2 0.9 copy-start.9
  9.2 0.7 copy-start.10
  9.9 0.7 copy-start.11
  11.5 13.4 %all-to-all-start = ((f32[8,2,32,256]{3,2,1,0:T(8,128)}), f32[8,2,32,256]{3,2,1,0:T(8,128)S(1)}, u32[]{:S(2)}, u32[]{:S(2)}) async-start(f32[8,2,32,256]{3,2,1,0:T(8,128)} %make_pieces.1), calls=%async_computation | async-start | bytes 1048576 | tf_op jit(solution)/shard_map/all_to_all | solution.py:19
  17.3 72.7 %all-gather.3.cloned.1.call-start = ((), (), s32[]{:S(2)}) async-start(), calls=%async_computation.4 | async-start | bytes 8912896 | tf_op jit(solution)/shard_map/all_gather | solution.py:256
  17.4 1.3 copy-start.6
  19.4 2.4 %copy-start.2 = (f32[8,320,512]{2,1,0:T(8,128)}, f32[8,320,512]{2,1,0:T(8,128)S(1)}, u32[]{:S(2)}) copy-start(f32[8,320,512]{2,1,0:T(8,128)S(1)} %cut_columns.1) | copy-start | bytes 15728644
  24.9 0.8 copy-start.12
  25.7 64.3 %copy-start.7 = (bf16[160,4096]{1,0:T(8,128)(2,1)S(1)}, bf16[160,4096]{1,0:T(8,128)(2,1)}, u32[]{:S(2)}) copy-start(bf16[160,4096]{1,0:T(8,128)(2,1)} %grads_ref.3) | copy-start | bytes 3932164
  25.7 71.6 %all-to-all-start.1 = ((f32[8,320,512]{2,1,0:T(8,128)}), f32[8,320,512]{2,1,0:T(8,128)}, u32[]{:S(2)}, u32[]{:S(2)}) async-start(f32[8,320,512]{2,1,0:T(8,128)} %copy-done.2), calls=%async_computation.1 | async-start | bytes 10485760 | tf_op jit(solution)/shard_map/all_to_all | solution.py:19
  90.0 3.4 %copy-start = (f32[128,2,32,256]{3,2,1,0:T(8,128)S(1)}, f32[128,2,32,256]{3,2,1,0:T(8,128)}, u32[]{:S(2)}) copy-start(f32[128,2,32,256]{3,2,1,0:T(8,128)} %all-gather.3.cloned.1.call-done) | copy-start | bytes 25165828
  97.4 37.0 %all-to-all-start.2 = ((f32[8,2,160,256]{3,2,1,0:T(8,128)}), f32[8,2,160,256]{3,2,1,0:T(8,128)S(1)}, u32[]{:S(2)}, u32[]{:S(2)}) async-start(f32[8,2,160,256]{3,2,1,0:T(8,128)} %hidden_pass.1.hidden_ref), calls=%async_computation.2 | async-start | bytes 5242880 | tf_op jit(solution)/shard_map/all_to_all | solution.py:19
  104.9 1.6 copy-start.3
  134.4 1.7 copy-start.4
  139.8 4.8 %collective-permute-start = (f32[32,16,256]{2,1,0:T(8,128)S(1)}, f32[32,16,256]{2,1,0:T(8,128)S(1)}, u32[]{:S(2)}, u32[]{:S(2)}) collective-permute-start(f32[32,16,256]{2,1,0:T(8,128)S(1)} %get-tuple-element.10), channel_id=1, source_target_pairs={{0,8},{8,0},{1,9},{9,1},{2,10},{10,2},{3,11},{11,3},{4,12},{12,4},... | collective-permute-start | bytes 1572872 | tf_op jit(solution)/shard_map/ppermute | solution.py:263
  145.6 25.3 %all-to-all-start.3 = ((f32[32,16,256]{2,1,0:T(8,128)}), f32[32,16,256]{2,1,0:T(8,128)S(1)}, u32[]{:S(2)}, u32[]{:S(2)}) async-start(f32[32,16,256]{2,1,0:T(8,128)} %add.7), calls=%async_computation.3 | async-start | bytes 1048576 | tf_op jit(solution)/shard_map/all_to_all | solution.py:19
  153.9 3.4 %copy-start.1 = (f32[128,2,32,256]{3,2,1,0:T(8,128)S(1)}, f32[128,2,32,256]{3,2,1,0:T(8,128)}, u32[]{:S(2)}) copy-start(f32[128,2,32,256]{3,2,1,0:T(8,128)} %all-gather.3.cloned.1.call-done) | copy-start | bytes 25165828
Sparse Core Ops, SparseCore 0:
  25.8 64.1 all-gather.2

commit v5 on v4

--- a/solution.py
+++ b/solution.py
@@ -13,6 +13,8 @@
 GROUP = ("z", "c")
 SHARDS = 2
 VMEM_LIMIT = 16 * 1024 * 1024
+HIDDEN_LIMIT = 52 * 1024 * 1024
+PIECE_LIMIT = 60 * 1024 * 1024
 
 
 def exchange(array, axes):
@@ -34,53 +36,60 @@
     return jnp.tanh(math.sqrt(2.0 / math.pi) * (v + 0.044715 * v * v * v))
 
 
-def hidden_kernel(weights_ref, tokens_ref, grads_ref, both_ref, pre, back):
-    step = pl.program_id(0)
-
-    @pl.when(step == 0)
-    def _():
-        pre[...] = jnp.zeros_like(pre)
-        back[...] = jnp.zeros_like(back)
-
-    _, shards, _, _, width = weights_ref.shape
-    shard = tokens_ref.shape[1] // shards
-    for q in range(shards):
-        up = weights_ref[:, q, 0].reshape(shard, width).astype(jnp.bfloat16)
-        down = weights_ref[:, q, 1].reshape(shard, width).astype(jnp.bfloat16)
-        columns = slice(q * shard, (q + 1) * shard)
+def hidden_kernel(weights_hbm, tokens_ref, grads_ref, both_hbm, weights, both, pre, back, in_sems, out_sems):
+    n, groups, _, piece, width = weights.shape
+    shard = groups * piece
+    arrivals = [
+        pltpu.make_async_copy(weights_hbm.at[:, k], weights.at[k], in_sems.at[k]) for k in range(n)
+    ]
+    for copy in arrivals:
+        copy.start()
+    pre[...] = jnp.zeros_like(pre)
+    back[...] = jnp.zeros_like(back)
+    for k in range(n):
+        arrivals[k].wait()
+        up = weights[k, :, 0].reshape(shard, width).astype(jnp.bfloat16)
+        down = weights[k, :, 1].reshape(shard, width).astype(jnp.bfloat16)
+        columns = slice(k * shard, (k + 1) * shard)
         pre[...] += jnp.dot(tokens_ref[:, columns], up, preferred_element_type=jnp.float32)
         back[...] += jnp.dot(grads_ref[:, columns], down, preferred_element_type=jnp.float32)
-
-    @pl.when(step == pl.num_programs(0) - 1)
-    def _():
-        v = pre[...]
-        t = inner_tanh(v)
-        act = (0.5 * v * (1.0 + t)).astype(jnp.bfloat16).astype(jnp.float32)
-        slope = 0.5 * (1.0 + t) + 0.5 * v * (1.0 - t * t) * math.sqrt(2.0 / math.pi) * (
-            1.0 + 3.0 * 0.044715 * v * v
-        )
-        hidden = (back[...] * slope).astype(jnp.bfloat16).astype(jnp.float32)
-        for k in range(both_ref.shape[0]):
-            both_ref[k, 0] = hidden
-            both_ref[k, 1] = act
+    v = pre[...]
+    t = inner_tanh(v)
+    act = (0.5 * v * (1.0 + t)).astype(jnp.bfloat16).astype(jnp.float32)
+    slope = 0.5 * (1.0 + t) + 0.5 * v * (1.0 - t * t) * math.sqrt(2.0 / math.pi) * (
+        1.0 + 3.0 * 0.044715 * v * v
+    )
+    hidden = (back[...] * slope).astype(jnp.bfloat16).astype(jnp.float32)
+    both[0] = hidden
+    both[1] = act
+    departures = [pltpu.make_async_copy(both, both_hbm.at[k], out_sems.at[k]) for k in range(n)]
+    for copy in departures:
+        copy.start()
+    for copy in departures:
+        copy.wait()
 
 
 def hidden_pass(weights, tokens, grads):
     groups, n, kinds, piece, width = weights.shape
     rows, depth = tokens.shape
-    cut = pl.BlockSpec((rows, SHARDS * depth // n), lambda k: (0, k))
     return pl.pallas_call(
         hidden_kernel,
-        grid=(n // SHARDS,),
         in_specs=[
-            pl.BlockSpec((groups, SHARDS, kinds, piece, width), lambda k: (0, k, 0, 0, 0)),
-            cut,
-            cut,
-        ],
-        out_specs=pl.BlockSpec((n, 2, rows, width), lambda k: (0, 0, 0, 0)),
+            pl.BlockSpec(memory_space=pltpu.HBM),
+            pl.BlockSpec(memory_space=pltpu.VMEM),
+            pl.BlockSpec(memory_space=pltpu.VMEM),
+        ],
+        out_specs=pl.BlockSpec(memory_space=pltpu.HBM),
         out_shape=jax.ShapeDtypeStruct((n, 2, rows, width), jnp.float32),
-        scratch_shapes=[pltpu.VMEM((rows, width), jnp.float32)] * 2,
-        compiler_params=pltpu.CompilerParams(vmem_limit_bytes=VMEM_LIMIT),
+        scratch_shapes=[
+            pltpu.VMEM((n, groups, kinds, piece, width), jnp.float32),
+            pltpu.VMEM((2, rows, width), jnp.float32),
+            pltpu.VMEM((rows, width), jnp.float32),
+            pltpu.VMEM((rows, width), jnp.float32),
+            pltpu.SemaphoreType.DMA((n,)),
+            pltpu.SemaphoreType.DMA((n,)),
+        ],
+        compiler_params=pltpu.CompilerParams(vmem_limit_bytes=HIDDEN_LIMIT),
         cost_estimate=pl.CostEstimate(
             flops=4 * rows * depth * width, bytes_accessed=13000000, transcendentals=rows * width
         ),
@@ -150,7 +159,7 @@
             out_specs=pl.BlockSpec(out, lambda k, place_ref: (0, 0, 0, 0)),
         ),
         out_shape=jax.ShapeDtypeStruct(out, jnp.float32),
-        compiler_params=pltpu.CompilerParams(vmem_limit_bytes=VMEM_LIMIT),
+        compiler_params=pltpu.CompilerParams(vmem_limit_bytes=PIECE_LIMIT),
         name="make_pieces",
     )(place[None], up_codes, up_scales.T, down_codes, down_scales.T)
 
@@ -168,7 +177,7 @@
         in_specs=[block],
         out_specs=block,
         out_shape=jax.ShapeDtypeStruct(columns.shape, jnp.bfloat16),
-        compiler_params=pltpu.CompilerParams(vmem_limit_bytes=VMEM_LIMIT),
+        compiler_params=pltpu.CompilerParams(vmem_limit_bytes=PIECE_LIMIT),
         cost_estimate=pl.CostEstimate(flops=0, bytes_accessed=12000000, transcendentals=0),
         name="narrow",
     )(columns)
@@ -195,20 +204,26 @@
     )(tokens, grads)
 
 
-def node_kernel(core_ref, left_ref, right_ref, mine_ref, other_ref):
+def node_kernel(core_ref, left_hbm, right_ref, mine_ref, other_ref, left, sems):
     n, kinds, rows, _ = right_ref.shape
     owned = mine_ref.shape[1] // kinds
-    for kind in range(kinds):
-        total = None
-        for p in range(n):
+    arrivals = [pltpu.make_async_copy(left_hbm.at[p], left.at[p], sems.at[p]) for p in range(n)]
+    for copy in arrivals:
+        copy.start()
+    totals = [None] * kinds
+    for p in range(n):
+        arrivals[p].wait()
+        for kind in range(kinds):
             term = lax.dot_general(
                 right_ref[p, kind].astype(jnp.bfloat16),
-                left_ref[p, kind * rows : (kind + 1) * rows],
+                left[p, kind * rows : (kind + 1) * rows],
                 (((0,), (0,)), ((), ())),
                 preferred_element_type=jnp.float32,
             )
-            total = clip_blocks(term) if total is None else total + clip_blocks(term)
-        summed = clip_blocks(total).T.reshape(mine_ref.shape[0], 2, owned, total.shape[0])
+            clipped = clip_blocks(term)
+            totals[kind] = clipped if totals[kind] is None else totals[kind] + clipped
+    for kind in range(kinds):
+        summed = clip_blocks(totals[kind]).T.reshape(mine_ref.shape[0], 2, owned, mine_ref.shape[2])
         first = core_ref[0] == 0
         part = slice(kind * owned, (kind + 1) * owned)
         mine_ref[:, part] = jnp.where(first, summed[:, 0], summed[:, 1])
@@ -219,25 +234,23 @@
     height = left.shape[2]
     n, kinds, rows, width = right.shape
     half = (height // (2 * owned), kinds * owned, width)
-    out = pl.BlockSpec(half, lambda k, core_ref: (0, 0, 0))
+    vmem = pl.BlockSpec(memory_space=pltpu.VMEM)
     return pl.pallas_call(
         node_kernel,
-        grid_spec=pltpu.PrefetchScalarGridSpec(
-            num_scalar_prefetch=1,
-            grid=(1,),
-            in_specs=[
-                pl.BlockSpec(left.shape, lambda k, core_ref: (0, 0, 0)),
-                pl.BlockSpec(right.shape, lambda k, core_ref: (0, 0, 0, 0)),
-            ],
-            out_specs=[out, out],
-        ),
+        in_specs=[
+            pl.BlockSpec(memory_space=pltpu.SMEM),
+            pl.BlockSpec(memory_space=pltpu.HBM),
+            vmem,
+        ],
+        out_specs=[vmem, vmem],
         out_shape=[jax.ShapeDtypeStruct(half, jnp.float32)] * 2,
+        scratch_shapes=[pltpu.VMEM(left.shape, left.dtype), pltpu.SemaphoreType.DMA((n,))],
         compiler_params=pltpu.CompilerParams(vmem_limit_bytes=VMEM_LIMIT),
         cost_estimate=pl.CostEstimate(
             flops=4 * n * rows * height * width, bytes_accessed=9000000, transcendentals=0
         ),
         name="node_sums",
-    )(core, left, right)
+    )(core, pltpu.with_memory_space_constraint(left, pltpu.HBM), right)
 
 
 def local(tokens, out_grad, up_codes, up_scales, down_codes, down_scales):

time: 181 us -> 179 us (0.989)
  local copies, waits for them, and re-layouts: 18.6 us -> 8.37 us
  Pallas kernels: 15.4 us -> 21.4 us
  waiting for transfers between devices: 102 us -> 104 us
    unnamed x26 -> x12, local copies, waits for them, and re-layouts: 18 us -> 7.76 us
    pallas_call x2, Pallas kernels: 7.63 us -> 12.5 us  [the longest x1 6.69 us: hidden_pass(): pl.pallas_call(hidden_kernel, in_specs=[pl.BlockSpec(memory_space=pltpu.H...]
  transfers between devices with their start and end apart: 6 -> 6, of which waited for: 5 -> 5; matrix products, arithmetic and copies ran while one was open for 0% -> 0% of each run, Pallas kernels for 6% -> 8%
where the time goes in v5:
time: 179 us; the launch traced here: 177 us
  waiting for transfers between devices  104 us (58%)
  starting transfers between devices  27.9 us (16%)
  Pallas kernels  21.4 us (12%)
  between operations  14.2 us (8%)
  local copies, waits for them, and re-layouts  8.37 us (5%)
    all_gather x1, waiting for transfers between devices, local(): weights = lax.all_gather(pieces, GROUP, axis=0)  59.6 us
    all_to_all x4, waiting for transfers between devices, exchange(): return lax.all_to_all(array, axes, split_axis=0, concat_axis=0, tiled=True)  42.6 us
    all_to_all x4, starting transfers between devices, exchange(): return lax.all_to_all(array, axes, split_axis=0, concat_axis=0, tiled=True)  24.2 us
    unnamed x12, local copies, waits for them, and re-layouts  7.76 us
    pallas_call x1, Pallas kernels, hidden_pass(): pl.pallas_call(hidden_kernel, in_specs=[pl.BlockSpec(memory_space=pltpu.H...  6.69 us
    pallas_call x1, Pallas kernels, node_sums(): pl.pallas_call(node_kernel, in_specs=[pl.BlockSpec(memory_space=pltpu.SME...  5.84 us
    pallas_call x1, Pallas kernels, narrow(): pl.pallas_call(narrow_kernel, grid=(2,), in_specs=[block], out_specs=bloc...  3.76 us
    ppermute x1, starting transfers between devices, local(): pairs = mine + lax.ppermute(other, 'c', [(0, 1), (1, 0)])  3.58 us
  transfers between devices with their start and end apart: 6, of which 5 were waited for; matrix products, arithmetic and copies ran while one was open for 0% of the time, Pallas kernels for 8%

profile of v5, /device:TPU:1, one launch (start us, length us, event | category | flops | bytes accessed | tf_op | source)
XLA Modules:
  0.0 176.6 jit_solution(11545772990672420032)
XLA Ops:
  7.2 0.0 copy-start.3
  7.2 1.8 %make_pieces.1 = f32[8,2,32,256]{3,2,1,0:T(8,128)} custom-call(s32[1]{0:T(128)} %bitcast.place_ref, bf16[512,256]{1,0:T(8,128)(2,1)} %up_ref.1, f32[2,512]{1,0:T(2,128)} %bitcast.7, bf16[512,256]{1,0:T(8,128)(2,1)} %down_ref.1, f32[2,512]{1,0:T(2,128)} %bitcast.8), custom_call_target="tpu_custom_call" | custom-call | tf_op jit(solution)/shard_map/make_pieces/pallas_call | solution.py:153
  9.0 5.9 %all-to-all-start = ((f32[8,2,32,256]{3,2,1,0:T(8,128)}), f32[8,2,32,256]{3,2,1,0:T(8,128)S(1)}, u32[]{:S(2)}, u32[]{:S(2)}) async-start(f32[8,2,32,256]{3,2,1,0:T(8,128)} %make_pieces.1), calls=%async_computation | async-start | bytes 1048576 | tf_op jit(solution)/shard_map/all_to_all | solution.py:21
  14.8 0.0 all-gather.3.cloned.1.call-start
  14.9 0.0 copy-done.3
  14.9 0.0 copy-start.4
  14.9 1.3 copy-done.4
  16.2 0.7 cut_columns.1
  16.9 0.0 copy-start.2
  16.9 2.3 %copy-done.2 = f32[8,320,512]{2,1,0:T(8,128)} copy-done((f32[8,320,512]{2,1,0:T(8,128)}, f32[8,320,512]{2,1,0:T(8,128)S(1)}, u32[]{:S(2)}) %copy-start.2) | copy-done | bytes 5242904
  19.2 3.2 %all-to-all-done = f32[8,2,32,256]{3,2,1,0:T(8,128)S(1)} async-done(((f32[8,2,32,256]{3,2,1,0:T(8,128)}), f32[8,2,32,256]{3,2,1,0:T(8,128)S(1)}, u32[]{:S(2)}, u32[]{:S(2)}) %all-to-all-start) | async-done | bytes 524320 | tf_op jit(solution)/shard_map/all_to_all | solution.py:21
  22.4 0.8 copy-done.5
  23.2 0.0 all-gather.3.cloned.1.call-update
  23.2 4.7 %all-to-all-start.1 = ((f32[8,320,512]{2,1,0:T(8,128)}), f32[8,320,512]{2,1,0:T(8,128)}, u32[]{:S(2)}, u32[]{:S(2)}) async-start(f32[8,320,512]{2,1,0:T(8,128)} %copy-done.2), calls=%async_computation.1 | async-start | bytes 10485760 | tf_op jit(solution)/shard_map/all_to_all | solution.py:21
  27.9 59.6 %all-gather.3.cloned.1.call-done = f32[128,2,32,256]{3,2,1,0:T(8,128)} async-done(((f32[8,2,32,256]{3,2,1,0:T(8,128)}), f32[128,2,32,256]{3,2,1,0:T(8,128)}) %all-gather.3.cloned.1.call-update) | async-done | bytes 8388624 | tf_op jit(solution)/shard_map/all_gather | solution.py:269
  87.5 6.7 %hidden_pass.1.hidden_ref = f32[8,2,160,256]{3,2,1,0:T(8,128)} custom-call(f32[16,8,2,32,256]{4,3,2,1,0:T(8,128)} %bitcast.5, bf16[160,4096]{1,0:T(8,128)(2,1)S(1)} %copy-done.3, bf16[160,4096]{1,0:T(8,128)(2,1)} %grads_ref.3), custom_call_target="tpu_custom_call" | custom-call | flops 671088640 | bytes 13000000 | tf_op jit(solution)/shard_map/hidden_pass/pallas_call | solution.py:75
  94.2 0.0 all-to-all-done.1.columns_ref
  94.2 4.9 %all-to-all-start.2 = ((f32[8,2,160,256]{3,2,1,0:T(8,128)}), f32[8,2,160,256]{3,2,1,0:T(8,128)S(1)}, u32[]{:S(2)}, u32[]{:S(2)}) async-start(f32[8,2,160,256]{3,2,1,0:T(8,128)} %hidden_pass.1.hidden_ref), calls=%async_computation.2 | async-start | bytes 5242880 | tf_op jit(solution)/shard_map/all_to_all | solution.py:21
  99.1 3.8 %narrow.1.left_hbm = bf16[8,320,512]{2,1,0:T(8,128)(2,1)} custom-call(f32[8,320,512]{2,1,0:T(8,128)} %all-to-all-done.1.columns_ref), custom_call_target="tpu_custom_call" | custom-call | bytes 12000000 | tf_op jit(solution)/shard_map/narrow/pallas_call | solution.py:174
  102.9 28.4 %all-to-all-done.2.right_ref = f32[8,2,160,256]{3,2,1,0:T(8,128)S(1)} async-done(((f32[8,2,160,256]{3,2,1,0:T(8,128)}), f32[8,2,160,256]{3,2,1,0:T(8,128)S(1)}, u32[]{:S(2)}, u32[]{:S(2)}) %all-to-all-start.2) | async-done | bytes 2621472 | tf_op jit(solution)/shard_map/all_to_all | solution.py:21
  131.3 5.8 %node_sums.1 = (f32[32,16,256]{2,1,0:T(8,128)S(1)}, f32[32,16,256]{2,1,0:T(8,128)S(1)}) custom-call(s32[1]{0:T(128)} %bitcast.4.core_ref, bf16[8,320,512]{2,1,0:T(8,128)(2,1)} %narrow.1.left_hbm, f32[8,2,160,256]{3,2,1,0:T(8,128)S(1)} %all-to-all-done.2.right_ref), custom_call_target="tpu_custom_call" | custom-call | flops 671088640 | bytes 9000000 | tf_op jit(solution)/shard_map/node_sums/pallas_call | solution.py:238
  137.1 0.0 copy-start.1
  137.1 3.6 %collective-permute-start = (f32[32,16,256]{2,1,0:T(8,128)S(1)}, f32[32,16,256]{2,1,0:T(8,128)S(1)}, u32[]{:S(2)}, u32[]{:S(2)}) collective-permute-start(f32[32,16,256]{2,1,0:T(8,128)S(1)} %get-tuple-element.10), channel_id=1, source_target_pairs={{0,8},{8,0},{1,9},{9,1},{2,10},{10,2},{3,11},{11,3},{4,12},{12,4},... | collective-permute-start | bytes 1572872 | tf_op jit(solution)/shard_map/ppermute | solution.py:276
  140.7 1.5 collective-permute-done
  142.2 0.9 add.7
  143.2 8.7 %all-to-all-start.3 = ((f32[32,16,256]{2,1,0:T(8,128)}), f32[32,16,256]{2,1,0:T(8,128)S(1)}, u32[]{:S(2)}, u32[]{:S(2)}) async-start(f32[32,16,256]{2,1,0:T(8,128)} %add.7), calls=%async_computation.3 | async-start | bytes 1048576 | tf_op jit(solution)/shard_map/all_to_all | solution.py:21
  151.9 0.0 copy-done.1
  151.9 0.0 copy-start
  151.9 3.4 %copy-done = f32[128,2,32,256]{3,2,1,0:T(8,128)S(1)} copy-done((f32[128,2,32,256]{3,2,1,0:T(8,128)S(1)}, f32[128,2,32,256]{3,2,1,0:T(8,128)}, u32[]{:S(2)}) %copy-start) | copy-done | bytes 8388632
  155.3 2.6 %input_pass.1 = bf16[160,4096]{1,0:T(8,128)(2,1)} custom-call(f32[8,2,160,256]{3,2,1,0:T(8,128)S(1)} %copy-done.1, f32[16,8,2,32,256]{4,3,2,1,0:T(8,128)S(1)} %bitcast.6), custom_call_target="tpu_custom_call" | custom-call | flops 335544320 | bytes 6000000 | tf_op jit(solution)/shard_map/input_pass/pallas_call | solution.py:115
  158.0 11.1 %all-to-all-done.3 = f32[32,16,256]{2,1,0:T(8,128)S(1)} async-done(((f32[32,16,256]{2,1,0:T(8,128)}), f32[32,16,256]{2,1,0:T(8,128)S(1)}, u32[]{:S(2)}, u32[]{:S(2)}) %all-to-all-start.3) | async-done | bytes 524320 | tf_op jit(solution)/shard_map/all_to_all | solution.py:21
  169.1 0.6 fusion
  (3 shorter events, 0.1 us)
Async XLA Ops:
  7.2 7.7 %copy-start.3 = (bf16[160,4096]{1,0:T(8,128)(2,1)S(1)}, bf16[160,4096]{1,0:T(8,128)(2,1)}, u32[]{:S(2)}) copy-start(bf16[160,4096]{1,0:T(8,128)(2,1)} %tokens_ref.3) | copy-start | bytes 3932164
  9.0 13.4 %all-to-all-start = ((f32[8,2,32,256]{3,2,1,0:T(8,128)}), f32[8,2,32,256]{3,2,1,0:T(8,128)S(1)}, u32[]{:S(2)}, u32[]{:S(2)}) async-start(f32[8,2,32,256]{3,2,1,0:T(8,128)} %make_pieces.1), calls=%async_computation | async-start | bytes 1048576 | tf_op jit(solution)/shard_map/all_to_all | solution.py:21
  14.8 72.7 %all-gather.3.cloned.1.call-start = ((), (), s32[]{:S(2)}) async-start(), calls=%async_computation.4 | async-start | bytes 8912896 | tf_op jit(solution)/shard_map/all_gather | solution.py:269
  14.9 1.3 copy-start.4
  16.9 2.3 %copy-start.2 = (f32[8,320,512]{2,1,0:T(8,128)}, f32[8,320,512]{2,1,0:T(8,128)S(1)}, u32[]{:S(2)}) copy-start(f32[8,320,512]{2,1,0:T(8,128)S(1)} %cut_columns.1) | copy-start | bytes 15728644
  22.4 0.8 copy-start.5
  23.2 71.0 %all-to-all-start.1 = ((f32[8,320,512]{2,1,0:T(8,128)}), f32[8,320,512]{2,1,0:T(8,128)}, u32[]{:S(2)}, u32[]{:S(2)}) async-start(f32[8,320,512]{2,1,0:T(8,128)} %copy-done.2), calls=%async_computation.1 | async-start | bytes 10485760 | tf_op jit(solution)/shard_map/all_to_all | solution.py:21
  94.2 37.1 %all-to-all-start.2 = ((f32[8,2,160,256]{3,2,1,0:T(8,128)}), f32[8,2,160,256]{3,2,1,0:T(8,128)S(1)}, u32[]{:S(2)}, u32[]{:S(2)}) async-start(f32[8,2,160,256]{3,2,1,0:T(8,128)} %hidden_pass.1.hidden_ref), calls=%async_computation.2 | async-start | bytes 5242880 | tf_op jit(solution)/shard_map/all_to_all | solution.py:21
  137.1 14.8 %copy-start.1 = (f32[8,2,160,256]{3,2,1,0:T(8,128)S(1)}, f32[8,2,160,256]{3,2,1,0:T(8,128)}, u32[]{:S(2)}) copy-start(f32[8,2,160,256]{3,2,1,0:T(8,128)} %hidden_pass.1.hidden_ref) | copy-start | bytes 7864324
  137.1 5.1 %collective-permute-start = (f32[32,16,256]{2,1,0:T(8,128)S(1)}, f32[32,16,256]{2,1,0:T(8,128)S(1)}, u32[]{:S(2)}, u32[]{:S(2)}) collective-permute-start(f32[32,16,256]{2,1,0:T(8,128)S(1)} %get-tuple-element.10), channel_id=1, source_target_pairs={{0,8},{8,0},{1,9},{9,1},{2,10},{10,2},{3,11},{11,3},{4,12},{12,4},... | collective-permute-start | bytes 1572872 | tf_op jit(solution)/shard_map/ppermute | solution.py:276
  143.2 25.9 %all-to-all-start.3 = ((f32[32,16,256]{2,1,0:T(8,128)}), f32[32,16,256]{2,1,0:T(8,128)S(1)}, u32[]{:S(2)}, u32[]{:S(2)}) async-start(f32[32,16,256]{2,1,0:T(8,128)} %add.7), calls=%async_computation.3 | async-start | bytes 1048576 | tf_op jit(solution)/shard_map/all_to_all | solution.py:21
  151.9 3.4 %copy-start = (f32[128,2,32,256]{3,2,1,0:T(8,128)S(1)}, f32[128,2,32,256]{3,2,1,0:T(8,128)}, u32[]{:S(2)}) copy-start(f32[128,2,32,256]{3,2,1,0:T(8,128)} %all-gather.3.cloned.1.call-done) | copy-start | bytes 25165828
Sparse Core Ops, SparseCore 0:
  23.3 64.1 all-gather.2

commit v6 on v5

--- a/solution.py
+++ b/solution.py
@@ -13,7 +13,7 @@
 GROUP = ("z", "c")
 SHARDS = 2
 VMEM_LIMIT = 16 * 1024 * 1024
-HIDDEN_LIMIT = 52 * 1024 * 1024
+PASS_LIMIT = 24 * 1024 * 1024
 PIECE_LIMIT = 60 * 1024 * 1024
 
 
@@ -36,65 +36,98 @@
     return jnp.tanh(math.sqrt(2.0 / math.pi) * (v + 0.044715 * v * v * v))
 
 
-def hidden_kernel(weights_hbm, tokens_ref, grads_ref, both_hbm, weights, both, pre, back, in_sems, out_sems):
-    n, groups, _, piece, width = weights.shape
+def product(kind, weights_hbm, weights, left, sems):
+    n, groups, piece, width = weights.shape
     shard = groups * piece
-    arrivals = [
-        pltpu.make_async_copy(weights_hbm.at[:, k], weights.at[k], in_sems.at[k]) for k in range(n)
+    copies = [
+        pltpu.make_async_copy(weights_hbm.at[:, k, kind], weights.at[k], sems.at[k]) for k in range(n)
     ]
-    for copy in arrivals:
+    for copy in copies:
         copy.start()
-    pre[...] = jnp.zeros_like(pre)
-    back[...] = jnp.zeros_like(back)
+    total = None
     for k in range(n):
-        arrivals[k].wait()
-        up = weights[k, :, 0].reshape(shard, width).astype(jnp.bfloat16)
-        down = weights[k, :, 1].reshape(shard, width).astype(jnp.bfloat16)
-        columns = slice(k * shard, (k + 1) * shard)
-        pre[...] += jnp.dot(tokens_ref[:, columns], up, preferred_element_type=jnp.float32)
-        back[...] += jnp.dot(grads_ref[:, columns], down, preferred_element_type=jnp.float32)
-    v = pre[...]
+        copies[k].wait()
+        block = weights[k].reshape(shard, width).astype(jnp.bfloat16)
+        columns = left[:, k * shard : (k + 1) * shard]
+        term = jnp.dot(columns, block, preferred_element_type=jnp.float32)
+        total = term if total is None else total + term
+    return total
+
+
+def send_all(values, rounded, out_hbm, sems):
+    rounded[...] = values.astype(jnp.bfloat16).astype(jnp.float32)
+    copies = [
+        pltpu.make_async_copy(rounded, out_hbm.at[k], sems.at[k]) for k in range(out_hbm.shape[0])
+    ]
+    for copy in copies:
+        copy.start()
+    return copies
+
+
+def forward_kernel(weights_hbm, tokens_ref, act_hbm, preact_ref, weights, rounded, in_sems, out_sems):
+    v = product(0, weights_hbm, weights, tokens_ref, in_sems)
+    copies = send_all(0.5 * v * (1.0 + inner_tanh(v)), rounded, act_hbm, out_sems)
+    preact_ref[...] = v
+    for copy in copies:
+        copy.wait()
+
+
+def backward_kernel(weights_hbm, grads_ref, preact_ref, hidden_hbm, weights, rounded, in_sems, out_sems):
+    v = preact_ref[...]
     t = inner_tanh(v)
-    act = (0.5 * v * (1.0 + t)).astype(jnp.bfloat16).astype(jnp.float32)
     slope = 0.5 * (1.0 + t) + 0.5 * v * (1.0 - t * t) * math.sqrt(2.0 / math.pi) * (
         1.0 + 3.0 * 0.044715 * v * v
     )
-    hidden = (back[...] * slope).astype(jnp.bfloat16).astype(jnp.float32)
-    both[0] = hidden
-    both[1] = act
-    departures = [pltpu.make_async_copy(both, both_hbm.at[k], out_sems.at[k]) for k in range(n)]
-    for copy in departures:
-        copy.start()
-    for copy in departures:
+    back = product(1, weights_hbm, weights, grads_ref, in_sems)
+    for copy in send_all(back * slope, rounded, hidden_hbm, out_sems):
         copy.wait()
 
 
-def hidden_pass(weights, tokens, grads):
-    groups, n, kinds, piece, width = weights.shape
-    rows, depth = tokens.shape
-    return pl.pallas_call(
-        hidden_kernel,
-        in_specs=[
-            pl.BlockSpec(memory_space=pltpu.HBM),
-            pl.BlockSpec(memory_space=pltpu.VMEM),
-            pl.BlockSpec(memory_space=pltpu.VMEM),
-        ],
-        out_specs=pl.BlockSpec(memory_space=pltpu.HBM),
-        out_shape=jax.ShapeDtypeStruct((n, 2, rows, width), jnp.float32),
+def pass_params(weights, rows, depth):
+    groups, n, _, piece, width = weights.shape
+    return dict(
         scratch_shapes=[
-            pltpu.VMEM((n, groups, kinds, piece, width), jnp.float32),
-            pltpu.VMEM((2, rows, width), jnp.float32),
-            pltpu.VMEM((rows, width), jnp.float32),
+            pltpu.VMEM((n, groups, piece, width), jnp.float32),
             pltpu.VMEM((rows, width), jnp.float32),
             pltpu.SemaphoreType.DMA((n,)),
             pltpu.SemaphoreType.DMA((n,)),
         ],
-        compiler_params=pltpu.CompilerParams(vmem_limit_bytes=HIDDEN_LIMIT),
+        compiler_params=pltpu.CompilerParams(vmem_limit_bytes=PASS_LIMIT),
         cost_estimate=pl.CostEstimate(
-            flops=4 * rows * depth * width, bytes_accessed=13000000, transcendentals=rows * width
+            flops=2 * rows * depth * width, bytes_accessed=8000000, transcendentals=rows * width
         ),
-        name="hidden_pass",
-    )(weights, tokens, grads)
+    )
+
+
+def forward(weights, tokens):
+    _, n, _, _, width = weights.shape
+    rows, depth = tokens.shape
+    hbm, vmem = pl.BlockSpec(memory_space=pltpu.HBM), pl.BlockSpec(memory_space=pltpu.VMEM)
+    return pl.pallas_call(
+        forward_kernel,
+        in_specs=[hbm, vmem],
+        out_specs=[hbm, vmem],
+        out_shape=[
+            pltpu.HBM((n, rows, width), jnp.float32),
+            jax.ShapeDtypeStruct((rows, width), jnp.float32),
+        ],
+        name="forward",
+        **pass_params(weights, rows, depth),
+    )(pltpu.with_memory_space_constraint(weights, pltpu.HBM), tokens)
+
+
+def backward(weights, grads, preact):
+    _, n, _, _, width = weights.shape
+    rows, depth = grads.shape
+    hbm, vmem = pl.BlockSpec(memory_space=pltpu.HBM), pl.BlockSpec(memory_space=pltpu.VMEM)
+    return pl.pallas_call(
+        backward_kernel,
+        in_specs=[hbm, vmem, vmem],
+        out_specs=hbm,
+        out_shape=pltpu.HBM((n, rows, width), jnp.float32),
+        name="backward",
+        **pass_params(weights, rows, depth),
+    )(pltpu.with_memory_space_constraint(weights, pltpu.HBM), grads, preact)
 
 
 def input_kernel(hidden_ref, weights_ref, out_ref):
@@ -108,15 +141,15 @@
         ).astype(out_ref.dtype)
 
 
-def input_pass(both, weights):
+def input_pass(hidden, weights):
     groups, n, _, piece, width = weights.shape
-    rows = both.shape[2]
+    rows = hidden.shape[1]
     depth = groups * n * piece
     return pl.pallas_call(
         input_kernel,
         grid=(n // SHARDS,),
         in_specs=[
-            pl.BlockSpec((None, None, rows, width), lambda k: (0, 0, 0, 0)),
+            pl.BlockSpec((None, rows, width), lambda k: (0, 0, 0)),
             pl.BlockSpec((groups, SHARDS, None, piece, width), lambda k: (0, k, 0, 0, 0)),
         ],
         out_specs=pl.BlockSpec((rows, SHARDS * depth // n), lambda k: (0, k)),
@@ -126,7 +159,7 @@
             flops=2 * rows * depth * width, bytes_accessed=6000000, transcendentals=0
         ),
         name="input_pass",
-    )(both, weights)
+    )(hidden, weights)
 
 
 def piece_kernel(place_ref, up_ref, up_scales_ref, down_ref, down_scales_ref, out_ref):
@@ -204,39 +237,41 @@
     )(tokens, grads)
 
 
-def node_kernel(core_ref, left_hbm, right_ref, mine_ref, other_ref, left, sems):
-    n, kinds, rows, _ = right_ref.shape
-    owned = mine_ref.shape[1] // kinds
-    arrivals = [pltpu.make_async_copy(left_hbm.at[p], left.at[p], sems.at[p]) for p in range(n)]
-    for copy in arrivals:
+def node_kernel(kind, core_ref, left_hbm, right_ref, mine_ref, other_ref, left, sems):
+    n, rows, width = right_ref.shape
+    copies = [
+        pltpu.make_async_copy(
+            left_hbm.at[p, pl.ds(kind * rows, rows)], left.at[p], sems.at[p]
+        )
+        for p in range(n)
+    ]
+    for copy in copies:
         copy.start()
-    totals = [None] * kinds
+    total = None
     for p in range(n):
-        arrivals[p].wait()
-        for kind in range(kinds):
-            term = lax.dot_general(
-                right_ref[p, kind].astype(jnp.bfloat16),
-                left[p, kind * rows : (kind + 1) * rows],
-                (((0,), (0,)), ((), ())),
-                preferred_element_type=jnp.float32,
-            )
-            clipped = clip_blocks(term)
-            totals[kind] = clipped if totals[kind] is None else totals[kind] + clipped
-    for kind in range(kinds):
-        summed = clip_blocks(totals[kind]).T.reshape(mine_ref.shape[0], 2, owned, mine_ref.shape[2])
-        first = core_ref[0] == 0
-        part = slice(kind * owned, (kind + 1) * owned)
-        mine_ref[:, part] = jnp.where(first, summed[:, 0], summed[:, 1])
-        other_ref[:, part] = jnp.where(first, summed[:, 1], summed[:, 0])
-
-
-def node_sums(core, left, right, owned):
+        copies[p].wait()
+        term = lax.dot_general(
+            right_ref[p].astype(jnp.bfloat16),
+            left[p],
+            (((0,), (0,)), ((), ())),
+            preferred_element_type=jnp.float32,
+        )
+        clipped = clip_blocks(term)
+        total = clipped if total is None else total + clipped
+    pairs, owned, _ = mine_ref.shape
+    summed = clip_blocks(total).T.reshape(pairs, 2, owned, width)
+    first = core_ref[0] == 0
+    mine_ref[...] = jnp.where(first, summed[:, 0], summed[:, 1])
+    other_ref[...] = jnp.where(first, summed[:, 1], summed[:, 0])
+
+
+def node_sum(core, left, kind, right, owned):
     height = left.shape[2]
-    n, kinds, rows, width = right.shape
-    half = (height // (2 * owned), kinds * owned, width)
+    n, rows, width = right.shape
+    half = (height // (2 * owned), owned, width)
     vmem = pl.BlockSpec(memory_space=pltpu.VMEM)
     return pl.pallas_call(
-        node_kernel,
+        functools.partial(node_kernel, kind),
         in_specs=[
             pl.BlockSpec(memory_space=pltpu.SMEM),
             pl.BlockSpec(memory_space=pltpu.HBM),
@@ -244,12 +279,12 @@
         ],
         out_specs=[vmem, vmem],
         out_shape=[jax.ShapeDtypeStruct(half, jnp.float32)] * 2,
-        scratch_shapes=[pltpu.VMEM(left.shape, left.dtype), pltpu.SemaphoreType.DMA((n,))],
+        scratch_shapes=[pltpu.VMEM((n, rows, height), left.dtype), pltpu.SemaphoreType.DMA((n,))],
         compiler_params=pltpu.CompilerParams(vmem_limit_bytes=VMEM_LIMIT),
         cost_estimate=pl.CostEstimate(
-            flops=4 * n * rows * height * width, bytes_accessed=9000000, transcendentals=0
+            flops=2 * n * rows * height * width, bytes_accessed=5000000, transcendentals=0
         ),
-        name="node_sums",
+        name="node_sum",
     )(core, pltpu.with_memory_space_constraint(left, pltpu.HBM), right)
 
 
@@ -268,13 +303,20 @@
     pieces, cut = lax.optimization_barrier((pieces, cut_columns(tokens, out_grad, n_local)))
     weights = lax.all_gather(pieces, GROUP, axis=0)
     columns = exchange(cut, LOCAL)
-    both = hidden_pass(weights, tokens, out_grad)
-    both_all = exchange(both, LOCAL)
-
-    mine, other = node_sums(core[None], narrow(columns), both_all, owned)
-    input_grad = input_pass(both, weights)
-    pairs = mine + lax.ppermute(other, "c", [(0, 1), (1, 0)])
-    owned_sums = exchange(pairs, ("yh", "z"))
+    activated, preact = forward(weights, tokens)
+    activated_all = exchange(activated, LOCAL)
+    hidden = backward(weights, out_grad, preact)
+    hidden_all = exchange(hidden, LOCAL)
+    narrowed = narrow(columns)
+
+    def over_cores(kind, right):
+        mine, other = node_sum(core[None], narrowed, kind, right, owned)
+        return mine + lax.ppermute(other, "c", [(0, 1), (1, 0)])
+
+    grad_down = over_cores(1, activated_all)
+    grad_up = over_cores(0, hidden_all)
+    input_grad = input_pass(hidden, weights)
+    owned_sums = exchange(jnp.concatenate([grad_up, grad_down], axis=1), ("yh", "z"))
     grads = jnp.sum(owned_sums, axis=0) / devices_all
     return (input_grad, grads[:owned], grads[owned:])
 

time: 179 us -> 184 us (1.028)
  starting transfers between devices: 27.9 us -> 38.5 us
  waiting for transfers between devices: 104 us -> 94.6 us
  Pallas kernels: 21.4 us -> 24.5 us
    all_to_all x4 -> x5, waiting for transfers between devices: 42.6 us -> 33.9 us  [exchange(): return lax.all_to_all(array, axes, split_axis=0, concat_axis=0, tiled=True)]
    all_to_all x4 -> x5, starting transfers between devices: 24.2 us -> 30.6 us  [exchange(): return lax.all_to_all(array, axes, split_axis=0, concat_axis=0, tiled=True)]
    ppermute x1 -> x2, starting transfers between devices: 3.58 us -> 7.84 us  [over_cores(): return mine + lax.ppermute(other, 'c', [(0, 1), (1, 0)])]
    pallas_call x2 -> x4, Pallas kernels: 12.5 us -> 15.6 us  [the longest x2 8.44 us: node_sum(): pl.pallas_call(functools.partial(node_kernel, kind), in_specs=[pl.BlockSp...]
    unnamed x12 -> x14, local copies, waits for them, and re-layouts: 7.76 us -> 7.76 us
  transfers between devices with their start and end apart: 6 -> 8, of which waited for: 5 -> 6; matrix products, arithmetic and copies ran while one was open for 0% -> 0% of each run, Pallas kernels for 8% -> 13%
where the time goes in v6:
time: 184 us; the launch traced here: 181 us
  waiting for transfers between devices  94.6 us (51%)
  starting transfers between devices  38.5 us (21%)
  Pallas kernels  24.5 us (13%)
  between operations  14.2 us (8%)
  local copies, waits for them, and re-layouts  8.36 us (5%)
    all_gather x1, waiting for transfers between devices, local(): weights = lax.all_gather(pieces, GROUP, axis=0)  59.6 us
    all_to_all x5, waiting for transfers between devices, exchange(): return lax.all_to_all(array, axes, split_axis=0, concat_axis=0, tiled=True)  33.9 us
    all_to_all x5, starting transfers between devices, exchange(): return lax.all_to_all(array, axes, split_axis=0, concat_axis=0, tiled=True)  30.6 us
    pallas_call x2, Pallas kernels, node_sum(): pl.pallas_call(functools.partial(node_kernel, kind), in_specs=[pl.BlockSp...  8.44 us
    ppermute x2, starting transfers between devices, over_cores(): return mine + lax.ppermute(other, 'c', [(0, 1), (1, 0)])  7.84 us
    unnamed x14, local copies, waits for them, and re-layouts  7.76 us
    pallas_call x1, Pallas kernels, narrow(): pl.pallas_call(narrow_kernel, grid=(2,), in_specs=[block], out_specs=bloc...  3.76 us
  transfers between devices with their start and end apart: 8, of which 6 were waited for; matrix products, arithmetic and copies ran while one was open for 0% of the time, Pallas kernels for 13%

profile of v6, /device:TPU:1, one launch (start us, length us, event | category | flops | bytes accessed | tf_op | source)
XLA Modules:
  0.0 181.2 jit_solution(18319483417162069576)
XLA Ops:
  7.2 1.8 make_pieces.1
  9.0 5.9 %all-to-all-start = ((f32[8,2,32,256]{3,2,1,0:T(8,128)}), f32[8,2,32,256]{3,2,1,0:T(8,128)S(1)}, u32[]{:S(2)}, u32[]{:S(2)}) async-start(f32[8,2,32,256]{3,2,1,0:T(8,128)} %make_pieces.1), calls=%async_computation | async-start | bytes 1048576 | tf_op jit(solution)/shard_map/all_to_all | solution.py:21
  14.8 0.0 all-gather.3.cloned.1.call-start
  14.9 0.0 copy-start.4
  14.9 1.3 copy-done.4
  16.2 0.7 cut_columns.1
  16.9 2.3 %copy-done.1 = f32[8,320,512]{2,1,0:T(8,128)} copy-done((f32[8,320,512]{2,1,0:T(8,128)}, f32[8,320,512]{2,1,0:T(8,128)S(1)}, u32[]{:S(2)}) %copy-start.1) | copy-done | bytes 5242904
  19.2 3.2 %all-to-all-done = f32[8,2,32,256]{3,2,1,0:T(8,128)S(1)} async-done(((f32[8,2,32,256]{3,2,1,0:T(8,128)}), f32[8,2,32,256]{3,2,1,0:T(8,128)S(1)}, u32[]{:S(2)}, u32[]{:S(2)}) %all-to-all-start) | async-done | bytes 524320 | tf_op jit(solution)/shard_map/all_to_all | solution.py:21
  22.4 0.8 copy-done.6
  23.2 0.0 all-gather.3.cloned.1.call-update
  23.2 4.7 %all-to-all-start.1 = ((f32[8,320,512]{2,1,0:T(8,128)}), f32[8,320,512]{2,1,0:T(8,128)}, u32[]{:S(2)}, u32[]{:S(2)}) async-start(f32[8,320,512]{2,1,0:T(8,128)} %copy-done.1), calls=%async_computation.1 | async-start | bytes 10485760 | tf_op jit(solution)/shard_map/all_to_all | solution.py:21
  27.9 59.6 %all-gather.3.cloned.1.call-done = f32[128,2,32,256]{3,2,1,0:T(8,128)} async-done(((f32[8,2,32,256]{3,2,1,0:T(8,128)}), f32[128,2,32,256]{3,2,1,0:T(8,128)}) %all-gather.3.cloned.1.call-update) | async-done | bytes 8388624 | tf_op jit(solution)/shard_map/all_gather | solution.py:304
  87.5 3.6 %forward.1 = (f32[8,160,256]{2,1,0:T(8,128)}, f32[160,256]{1,0:T(8,128)S(1)}) custom-call(f32[16,8,2,32,256]{4,3,2,1,0:T(8,128)} %bitcast.5, bf16[160,4096]{1,0:T(8,128)(2,1)S(1)} %copy-done.3), custom_call_target="tpu_custom_call" | custom-call | flops 335544320 | bytes 8000000 | tf_op jit(solution)/shard_map/forward/pallas_call | solution.py:106
  91.1 0.0 copy-start.5
  91.1 5.0 %all-to-all-start.3 = ((f32[8,160,256]{2,1,0:T(8,128)}), f32[8,160,256]{2,1,0:T(8,128)S(1)}, u32[]{:S(2)}, u32[]{:S(2)}) async-start(f32[8,160,256]{2,1,0:T(8,128)} %get-tuple-element.16), calls=%async_computation.3 | async-start | bytes 2621440 | tf_op jit(solution)/shard_map/all_to_all | solution.py:21
  96.2 3.6 %backward.1.hidden_ref = f32[8,160,256]{2,1,0:T(8,128)} custom-call(f32[16,8,2,32,256]{4,3,2,1,0:T(8,128)} %bitcast.6, bf16[160,4096]{1,0:T(8,128)(2,1)S(1)} %copy-done.5, f32[160,256]{1,0:T(8,128)S(1)} %get-tuple-element.12.preact_ref), custom_call_target="tpu_custom_call" | custom-call | flops 335544320 | bytes 8000000 | tf_op jit(solution)/shard_map/backward/pallas_call | solution.py:123
  99.8 14.5 %all-to-all-done.3.right_ref = f32[8,160,256]{2,1,0:T(8,128)S(1)} async-done(((f32[8,160,256]{2,1,0:T(8,128)}), f32[8,160,256]{2,1,0:T(8,128)S(1)}, u32[]{:S(2)}, u32[]{:S(2)}) %all-to-all-start.3) | async-done | bytes 1310752 | tf_op jit(solution)/shard_map/all_to_all | solution.py:21
  114.3 3.6 %all-to-all-start.2 = ((f32[8,160,256]{2,1,0:T(8,128)}), f32[8,160,256]{2,1,0:T(8,128)S(1)}, u32[]{:S(2)}, u32[]{:S(2)}) async-start(f32[8,160,256]{2,1,0:T(8,128)} %backward.1.hidden_ref), calls=%async_computation.2 | async-start | bytes 2621440 | tf_op jit(solution)/shard_map/all_to_all | solution.py:21
  117.9 3.8 %narrow.1.left_hbm = bf16[8,320,512]{2,1,0:T(8,128)(2,1)} custom-call(f32[8,320,512]{2,1,0:T(8,128)} %all-to-all-done.1.columns_ref), custom_call_target="tpu_custom_call" | custom-call | bytes 12000000 | tf_op jit(solution)/shard_map/narrow/pallas_call | solution.py:207
  121.6 4.2 %node_sum.3 = (f32[32,8,256]{2,1,0:T(8,128)S(1)}, f32[32,8,256]{2,1,0:T(8,128)S(1)}) custom-call(s32[1]{0:T(128)} %bitcast.4.core_ref, bf16[8,320,512]{2,1,0:T(8,128)(2,1)} %narrow.1.left_hbm, f32[8,160,256]{2,1,0:T(8,128)S(1)} %all-to-all-done.3.right_ref), custom_call_target="tpu_custom_call" | custom-call | flops 335544320 | bytes 5000000 | tf_op jit(solution)/shard_map/node_sum/pallas_call | solution.py:273
  125.9 3.3 %collective-permute-start.1 = (f32[32,8,256]{2,1,0:T(8,128)S(1)}, f32[32,8,256]{2,1,0:T(8,128)S(1)}, u32[]{:S(2)}, u32[]{:S(2)}) collective-permute-start(f32[32,8,256]{2,1,0:T(8,128)S(1)} %get-tuple-element.18), channel_id=1, source_target_pairs={{0,8},{8,0},{1,9},{9,1},{2,10},{10,2},{3,11},{11,3},{4,12},{12,4},... | collective-permute-start | bytes 786440 | tf_op jit(solution)/shard_map/ppermute | solution.py:314
  129.2 5.5 %all-to-all-done.2.right_ref = f32[8,160,256]{2,1,0:T(8,128)S(1)} async-done(((f32[8,160,256]{2,1,0:T(8,128)}), f32[8,160,256]{2,1,0:T(8,128)S(1)}, u32[]{:S(2)}, u32[]{:S(2)}) %all-to-all-start.2) | async-done | bytes 1310752 | tf_op jit(solution)/shard_map/all_to_all | solution.py:21
  134.6 4.2 %node_sum.2 = (f32[32,8,256]{2,1,0:T(8,128)S(1)}, f32[32,8,256]{2,1,0:T(8,128)S(1)}) custom-call(s32[1]{0:T(128)} %bitcast.4.core_ref, bf16[8,320,512]{2,1,0:T(8,128)(2,1)} %narrow.1.left_hbm, f32[8,160,256]{2,1,0:T(8,128)S(1)} %all-to-all-done.2.right_ref), custom_call_target="tpu_custom_call" | custom-call | flops 335544320 | bytes 5000000 | tf_op jit(solution)/shard_map/node_sum/pallas_call | solution.py:273
  138.9 4.5 %collective-permute-start = (f32[32,8,256]{2,1,0:T(8,128)S(1)}, f32[32,8,256]{2,1,0:T(8,128)S(1)}, u32[]{:S(2)}, u32[]{:S(2)}) collective-permute-start(f32[32,8,256]{2,1,0:T(8,128)S(1)} %get-tuple-element.15), channel_id=1, source_target_pairs={{0,8},{8,0},{1,9},{9,1},{2,10},{10,2},{3,11},{11,3},{4,12},{12,4},... | collective-permute-start | bytes 786440 | tf_op jit(solution)/shard_map/ppermute | solution.py:314
  143.4 0.0 collective-permute-done.1
  143.5 1.1 collective-permute-done
  144.6 0.9 pad_maximum_fusion
  145.5 11.4 %all-to-all-start.4 = ((f32[32,16,256]{2,1,0:T(8,128)}), f32[32,16,256]{2,1,0:T(8,128)S(1)}, u32[]{:S(2)}, u32[]{:S(2)}) async-start(f32[32,16,256]{2,1,0:T(8,128)} %pad_maximum_fusion), calls=%async_computation.4 | async-start | bytes 1048576 | tf_op jit(solution)/shard_map/all_to_all | solution.py:21
  156.9 3.4 %copy-done = f32[128,2,32,256]{3,2,1,0:T(8,128)S(1)} copy-done((f32[128,2,32,256]{3,2,1,0:T(8,128)S(1)}, f32[128,2,32,256]{3,2,1,0:T(8,128)}, u32[]{:S(2)}) %copy-start) | copy-done | bytes 8388632
  160.3 2.7 %input_pass.1 = bf16[160,4096]{1,0:T(8,128)(2,1)} custom-call(f32[8,160,256]{2,1,0:T(8,128)S(1)} %copy-done.2, f32[16,8,2,32,256]{4,3,2,1,0:T(8,128)S(1)} %bitcast.7), custom_call_target="tpu_custom_call" | custom-call | flops 335544320 | bytes 6000000 | tf_op jit(solution)/shard_map/input_pass/pallas_call | solution.py:148
  163.0 10.7 %all-to-all-done.4 = f32[32,16,256]{2,1,0:T(8,128)S(1)} async-done(((f32[32,16,256]{2,1,0:T(8,128)}), f32[32,16,256]{2,1,0:T(8,128)S(1)}, u32[]{:S(2)}, u32[]{:S(2)}) %all-to-all-start.4) | async-done | bytes 524320 | tf_op jit(solution)/shard_map/all_to_all | solution.py:21
  173.8 0.6 fusion
  (13 shorter events, 0.1 us)
Async XLA Ops:
  7.2 7.7 %copy-start.3 = (bf16[160,4096]{1,0:T(8,128)(2,1)S(1)}, bf16[160,4096]{1,0:T(8,128)(2,1)}, u32[]{:S(2)}) copy-start(bf16[160,4096]{1,0:T(8,128)(2,1)} %tokens_ref.3) | copy-start | bytes 3932164
  9.0 13.4 %all-to-all-start = ((f32[8,2,32,256]{3,2,1,0:T(8,128)}), f32[8,2,32,256]{3,2,1,0:T(8,128)S(1)}, u32[]{:S(2)}, u32[]{:S(2)}) async-start(f32[8,2,32,256]{3,2,1,0:T(8,128)} %make_pieces.1), calls=%async_computation | async-start | bytes 1048576 | tf_op jit(solution)/shard_map/all_to_all | solution.py:21
  14.8 72.7 %all-gather.3.cloned.1.call-start = ((), (), s32[]{:S(2)}) async-start(), calls=%async_computation.5 | async-start | bytes 8912896 | tf_op jit(solution)/shard_map/all_gather | solution.py:304
  14.9 1.3 copy-start.4
  16.9 2.3 %copy-start.1 = (f32[8,320,512]{2,1,0:T(8,128)}, f32[8,320,512]{2,1,0:T(8,128)S(1)}, u32[]{:S(2)}) copy-start(f32[8,320,512]{2,1,0:T(8,128)S(1)} %cut_columns.1) | copy-start | bytes 15728644
  22.4 0.8 copy-start.6
  23.2 67.9 %all-to-all-start.1 = ((f32[8,320,512]{2,1,0:T(8,128)}), f32[8,320,512]{2,1,0:T(8,128)}, u32[]{:S(2)}, u32[]{:S(2)}) async-start(f32[8,320,512]{2,1,0:T(8,128)} %copy-done.1), calls=%async_computation.1 | async-start | bytes 10485760 | tf_op jit(solution)/shard_map/all_to_all | solution.py:21
  91.1 5.1 %copy-start.5 = (bf16[160,4096]{1,0:T(8,128)(2,1)S(1)}, bf16[160,4096]{1,0:T(8,128)(2,1)}, u32[]{:S(2)}) copy-start(bf16[160,4096]{1,0:T(8,128)(2,1)} %grads_ref.3) | copy-start | bytes 3932164
  91.1 23.1 %all-to-all-start.3 = ((f32[8,160,256]{2,1,0:T(8,128)}), f32[8,160,256]{2,1,0:T(8,128)S(1)}, u32[]{:S(2)}, u32[]{:S(2)}) async-start(f32[8,160,256]{2,1,0:T(8,128)} %get-tuple-element.16), calls=%async_computation.3 | async-start | bytes 2621440 | tf_op jit(solution)/shard_map/all_to_all | solution.py:21
  114.3 20.4 %all-to-all-start.2 = ((f32[8,160,256]{2,1,0:T(8,128)}), f32[8,160,256]{2,1,0:T(8,128)S(1)}, u32[]{:S(2)}, u32[]{:S(2)}) async-start(f32[8,160,256]{2,1,0:T(8,128)} %backward.1.hidden_ref), calls=%async_computation.2 | async-start | bytes 2621440 | tf_op jit(solution)/shard_map/all_to_all | solution.py:21
  125.9 17.6 %collective-permute-start.1 = (f32[32,8,256]{2,1,0:T(8,128)S(1)}, f32[32,8,256]{2,1,0:T(8,128)S(1)}, u32[]{:S(2)}, u32[]{:S(2)}) collective-permute-start(f32[32,8,256]{2,1,0:T(8,128)S(1)} %get-tuple-element.18), channel_id=1, source_target_pairs={{0,8},{8,0},{1,9},{9,1},{2,10},{10,2},{3,11},{11,3},{4,12},{12,4},... | collective-permute-start | bytes 786440 | tf_op jit(solution)/shard_map/ppermute | solution.py:314
  138.9 5.7 %collective-permute-start = (f32[32,8,256]{2,1,0:T(8,128)S(1)}, f32[32,8,256]{2,1,0:T(8,128)S(1)}, u32[]{:S(2)}, u32[]{:S(2)}) collective-permute-start(f32[32,8,256]{2,1,0:T(8,128)S(1)} %get-tuple-element.15), channel_id=1, source_target_pairs={{0,8},{8,0},{1,9},{9,1},{2,10},{10,2},{3,11},{11,3},{4,12},{12,4},... | collective-permute-start | bytes 786440 | tf_op jit(solution)/shard_map/ppermute | solution.py:314
  144.6 12.4 %copy-start.2 = (f32[8,160,256]{2,1,0:T(8,128)S(1)}, f32[8,160,256]{2,1,0:T(8,128)}, u32[]{:S(2)}) copy-start(f32[8,160,256]{2,1,0:T(8,128)} %backward.1.hidden_ref) | copy-start | bytes 3932164
  145.5 28.2 %all-to-all-start.4 = ((f32[32,16,256]{2,1,0:T(8,128)}), f32[32,16,256]{2,1,0:T(8,128)S(1)}, u32[]{:S(2)}, u32[]{:S(2)}) async-start(f32[32,16,256]{2,1,0:T(8,128)} %pad_maximum_fusion), calls=%async_computation.4 | async-start | bytes 1048576 | tf_op jit(solution)/shard_map/all_to_all | solution.py:21
  156.9 3.4 %copy-start = (f32[128,2,32,256]{3,2,1,0:T(8,128)S(1)}, f32[128,2,32,256]{3,2,1,0:T(8,128)}, u32[]{:S(2)}) copy-start(f32[128,2,32,256]{3,2,1,0:T(8,128)} %all-gather.3.cloned.1.call-done) | copy-start | bytes 25165828
Sparse Core Ops, SparseCore 0:
  23.3 64.1 all-gather.2

commit v7 on v5

--- a/solution.py
+++ b/solution.py
@@ -8,6 +8,7 @@
 from jax.sharding import Mesh, PartitionSpec as P
 
 QBLOCK = 128
+SWAP = ((0, 1), (1, 0))
 AXES = ("yh", "z", "c", "x", "yl")
 LOCAL = ("x", "yl")
 GROUP = ("z", "c")
@@ -26,9 +27,8 @@
     for k in range(values.shape[0] // QBLOCK):
         block = values[k * QBLOCK : (k + 1) * QBLOCK]
         mean = jnp.mean(block * block, axis=0, keepdims=True) + 1e-06
-        root = lax.rsqrt(mean)
-        codes = jnp.clip(block * (3.5 * root), -7.0, 7.0).astype(jnp.bfloat16)
-        parts.append(codes.astype(jnp.float32) * (mean * root * (2.0 / 7.0)))
+        largest = 2.0 * (mean * lax.rsqrt(mean))
+        parts.append(jnp.minimum(jnp.maximum(block, -largest), largest))
     return jnp.concatenate(parts, axis=0)
 
 
@@ -36,7 +36,9 @@
     return jnp.tanh(math.sqrt(2.0 / math.pi) * (v + 0.044715 * v * v * v))
 
 
-def hidden_kernel(weights_hbm, tokens_ref, grads_ref, both_hbm, weights, both, pre, back, in_sems, out_sems):
+def hidden_kernel(
+    weights_hbm, tokens_ref, grads_ref, act_hbm, hidden_ref, weights, act, pre, back, in_sems, out_sems
+):
     n, groups, _, piece, width = weights.shape
     shard = groups * piece
     arrivals = [
@@ -55,21 +57,20 @@
         back[...] += jnp.dot(grads_ref[:, columns], down, preferred_element_type=jnp.float32)
     v = pre[...]
     t = inner_tanh(v)
-    act = (0.5 * v * (1.0 + t)).astype(jnp.bfloat16).astype(jnp.float32)
+    act[...] = (0.5 * v * (1.0 + t)).astype(jnp.bfloat16).astype(jnp.float32)
+    copies = act_hbm.shape[0]
+    departures = [pltpu.make_async_copy(act, act_hbm.at[k], out_sems.at[k]) for k in range(copies)]
+    for copy in departures:
+        copy.start()
     slope = 0.5 * (1.0 + t) + 0.5 * v * (1.0 - t * t) * math.sqrt(2.0 / math.pi) * (
         1.0 + 3.0 * 0.044715 * v * v
     )
-    hidden = (back[...] * slope).astype(jnp.bfloat16).astype(jnp.float32)
-    both[0] = hidden
-    both[1] = act
-    departures = [pltpu.make_async_copy(both, both_hbm.at[k], out_sems.at[k]) for k in range(n)]
-    for copy in departures:
-        copy.start()
+    hidden_ref[...] = (back[...] * slope).astype(jnp.bfloat16).astype(jnp.float32)
     for copy in departures:
         copy.wait()
 
 
-def hidden_pass(weights, tokens, grads):
+def hidden_pass(weights, tokens, grads, copies):
     groups, n, kinds, piece, width = weights.shape
     rows, depth = tokens.shape
     return pl.pallas_call(
@@ -79,15 +80,18 @@
             pl.BlockSpec(memory_space=pltpu.VMEM),
             pl.BlockSpec(memory_space=pltpu.VMEM),
         ],
-        out_specs=pl.BlockSpec(memory_space=pltpu.HBM),
-        out_shape=jax.ShapeDtypeStruct((n, 2, rows, width), jnp.float32),
+        out_specs=[pl.BlockSpec(memory_space=pltpu.HBM), pl.BlockSpec(memory_space=pltpu.VMEM)],
+        out_shape=[
+            pltpu.HBM((copies, rows, width), jnp.float32),
+            jax.ShapeDtypeStruct((rows, width), jnp.float32),
+        ],
         scratch_shapes=[
             pltpu.VMEM((n, groups, kinds, piece, width), jnp.float32),
-            pltpu.VMEM((2, rows, width), jnp.float32),
+            pltpu.VMEM((rows, width), jnp.float32),
             pltpu.VMEM((rows, width), jnp.float32),
             pltpu.VMEM((rows, width), jnp.float32),
             pltpu.SemaphoreType.DMA((n,)),
-            pltpu.SemaphoreType.DMA((n,)),
+            pltpu.SemaphoreType.DMA((copies,)),
         ],
         compiler_params=pltpu.CompilerParams(vmem_limit_bytes=HIDDEN_LIMIT),
         cost_estimate=pl.CostEstimate(
@@ -108,15 +112,15 @@
         ).astype(out_ref.dtype)
 
 
-def input_pass(both, weights):
+def input_pass(hidden, weights):
     groups, n, _, piece, width = weights.shape
-    rows = both.shape[2]
+    rows = hidden.shape[0]
     depth = groups * n * piece
     return pl.pallas_call(
         input_kernel,
         grid=(n // SHARDS,),
         in_specs=[
-            pl.BlockSpec((None, None, rows, width), lambda k: (0, 0, 0, 0)),
+            pl.BlockSpec((rows, width), lambda k: (0, 0)),
             pl.BlockSpec((groups, SHARDS, None, piece, width), lambda k: (0, k, 0, 0, 0)),
         ],
         out_specs=pl.BlockSpec((rows, SHARDS * depth // n), lambda k: (0, k)),
@@ -126,7 +130,7 @@
             flops=2 * rows * depth * width, bytes_accessed=6000000, transcendentals=0
         ),
         name="input_pass",
-    )(both, weights)
+    )(hidden, weights)
 
 
 def piece_kernel(place_ref, up_ref, up_scales_ref, down_ref, down_scales_ref, out_ref):
@@ -204,42 +208,51 @@
     )(tokens, grads)
 
 
-def node_kernel(core_ref, left_hbm, right_ref, mine_ref, other_ref, left, sems):
-    n, kinds, rows, _ = right_ref.shape
-    owned = mine_ref.shape[1] // kinds
-    arrivals = [pltpu.make_async_copy(left_hbm.at[p], left.at[p], sems.at[p]) for p in range(n)]
-    for copy in arrivals:
+def node_kernel(place_ref, left_hbm, hidden_ref, act_ref, act_peer_ref, mine_ref, other_ref, left, sems):
+    rows, width = act_ref.shape[1:]
+    n = left.shape[0]
+    copies = [
+        pltpu.make_async_copy(
+            left_hbm.at[2 * (p // 2) + lax.rem(place_ref[1] + p, 2)], left.at[p], sems.at[p]
+        )
+        for p in range(n)
+    ]
+    for copy in copies:
         copy.start()
-    totals = [None] * kinds
+    totals = [None, None]
     for p in range(n):
-        arrivals[p].wait()
-        for kind in range(kinds):
+        copies[p].wait()
+        rights = (hidden_ref[p // 2, p % 2], (act_peer_ref if p % 2 else act_ref)[p // 2])
+        for kind in range(2):
             term = lax.dot_general(
-                right_ref[p, kind].astype(jnp.bfloat16),
+                rights[kind].astype(jnp.bfloat16),
                 left[p, kind * rows : (kind + 1) * rows],
                 (((0,), (0,)), ((), ())),
                 preferred_element_type=jnp.float32,
             )
             clipped = clip_blocks(term)
             totals[kind] = clipped if totals[kind] is None else totals[kind] + clipped
-    for kind in range(kinds):
-        summed = clip_blocks(totals[kind]).T.reshape(mine_ref.shape[0], 2, owned, mine_ref.shape[2])
-        first = core_ref[0] == 0
+    owned = mine_ref.shape[1] // 2
+    for kind in range(2):
+        summed = clip_blocks(totals[kind]).T.reshape(mine_ref.shape[0], 2, owned, width)
+        first = place_ref[0] == 0
         part = slice(kind * owned, (kind + 1) * owned)
         mine_ref[:, part] = jnp.where(first, summed[:, 0], summed[:, 1])
         other_ref[:, part] = jnp.where(first, summed[:, 1], summed[:, 0])
 
 
-def node_sums(core, left, right, owned):
-    height = left.shape[2]
-    n, kinds, rows, width = right.shape
-    half = (height // (2 * owned), kinds * owned, width)
+def node_sums(place, left, hidden, act, act_peer, owned):
+    n, _, height = left.shape
+    _, rows, width = act.shape
+    half = (height // (2 * owned), 2 * owned, width)
     vmem = pl.BlockSpec(memory_space=pltpu.VMEM)
     return pl.pallas_call(
         node_kernel,
         in_specs=[
             pl.BlockSpec(memory_space=pltpu.SMEM),
             pl.BlockSpec(memory_space=pltpu.HBM),
+            vmem,
+            vmem,
             vmem,
         ],
         out_specs=[vmem, vmem],
@@ -250,7 +263,7 @@
             flops=4 * n * rows * height * width, bytes_accessed=9000000, transcendentals=0
         ),
         name="node_sums",
-    )(core, pltpu.with_memory_space_constraint(left, pltpu.HBM), right)
+    )(place, pltpu.with_memory_space_constraint(left, pltpu.HBM), hidden, act, act_peer)
 
 
 def local(tokens, out_grad, up_codes, up_scales, down_codes, down_scales):
@@ -268,12 +281,20 @@
     pieces, cut = lax.optimization_barrier((pieces, cut_columns(tokens, out_grad, n_local)))
     weights = lax.all_gather(pieces, GROUP, axis=0)
     columns = exchange(cut, LOCAL)
-    both = hidden_pass(weights, tokens, out_grad)
-    both_all = exchange(both, LOCAL)
-
-    mine, other = node_sums(core[None], narrow(columns), both_all, owned)
-    input_grad = input_pass(both, weights)
-    pairs = mine + lax.ppermute(other, "c", [(0, 1), (1, 0)])
+    n_x = lax.axis_size("x")
+    act_copies, hidden = hidden_pass(weights, tokens, out_grad, n_x)
+    hidden_peer = lax.ppermute(hidden, "yl", SWAP)
+    columns, act_copies = lax.optimization_barrier((columns, act_copies))
+    act_all = exchange(act_copies, "x")
+    hidden_pair = jnp.stack([hidden, hidden_peer])
+    hidden_copies = jnp.broadcast_to(hidden_pair[None], (n_x,) + hidden_pair.shape)
+    act_all, hidden_copies = lax.optimization_barrier((act_all, hidden_copies))
+    act_peer_all = lax.ppermute(act_all, "yl", SWAP)
+    hidden_all = exchange(hidden_copies, "x")
+    place = jnp.stack([core, lax.axis_index("yl")])
+    mine, other = node_sums(place, narrow(columns), hidden_all, act_all, act_peer_all, owned)
+    input_grad = input_pass(hidden, weights)
+    pairs = mine + lax.ppermute(other, "c", SWAP)
     owned_sums = exchange(pairs, ("yh", "z"))
     grads = jnp.sum(owned_sums, axis=0) / devices_all
     return (input_grad, grads[:owned], grads[owned:])

time: 179 us -> 178 us (level)
  waiting for transfers between devices: 104 us -> 93.8 us
  starting transfers between devices: 27.9 us -> 37.5 us
    all_to_all x4 -> x5, waiting for transfers between devices: 42.6 us -> 19 us  [exchange(): return lax.all_to_all(array, axes, split_axis=0, concat_axis=0, tiled=True)]
    ppermute x1 -> x3, waiting for transfers between devices: 1.51 us -> 15.3 us  [the longest x1 9.79 us: local(): act_peer_all = lax.ppermute(act_all, 'yl', SWAP)]
    ppermute x1 -> x3, starting transfers between devices: 3.58 us -> 10.4 us  [the longest x1 4.22 us: local(): pairs = mine + lax.ppermute(other, 'c', SWAP)]
    all_to_all x4 -> x5, starting transfers between devices: 24.2 us -> 27 us  [exchange(): return lax.all_to_all(array, axes, split_axis=0, concat_axis=0, tiled=True)]
    unnamed x12 -> x10, local copies, waits for them, and re-layouts: 7.76 us -> 7.76 us
  transfers between devices with their start and end apart: 6 -> 9, of which waited for: 5 -> 7; matrix products, arithmetic and copies ran while one was open for 0% -> 0% of each run, Pallas kernels for 8% -> 7%
where the time goes in v7:
time: 178 us; the launch traced here: 177 us
  waiting for transfers between devices  93.8 us (53%)
  starting transfers between devices  37.5 us (21%)
  Pallas kernels  20.7 us (12%)
  between operations  14.2 us (8%)
  local copies, waits for them, and re-layouts  9.53 us (5%)
    all_gather x1, waiting for transfers between devices, local(): weights = lax.all_gather(pieces, GROUP, axis=0)  59.6 us
    all_to_all x5, starting transfers between devices, exchange(): return lax.all_to_all(array, axes, split_axis=0, concat_axis=0, tiled=True)  27 us
    all_to_all x5, waiting for transfers between devices, exchange(): return lax.all_to_all(array, axes, split_axis=0, concat_axis=0, tiled=True)  19 us
    ppermute x1, waiting for transfers between devices, local(): act_peer_all = lax.ppermute(act_all, 'yl', SWAP)  9.79 us
    unnamed x10, local copies, waits for them, and re-layouts  7.76 us
    pallas_call x1, Pallas kernels, hidden_pass(): pl.pallas_call(hidden_kernel, in_specs=[pl.BlockSpec(memory_space=pltpu.H...  5.99 us
    pallas_call x1, Pallas kernels, node_sums(): pl.pallas_call(node_kernel, in_specs=[pl.BlockSpec(memory_space=pltpu.SME...  5.82 us
    ppermute x1, starting transfers between devices, local(): pairs = mine + lax.ppermute(other, 'c', SWAP)  4.22 us
  transfers between devices with their start and end apart: 9, of which 7 were waited for; matrix products, arithmetic and copies ran while one was open for 0% of the time, Pallas kernels for 7%

profile of v7, /device:TPU:1, one launch (start us, length us, event | category | flops | bytes accessed | tf_op | source)
XLA Modules:
  0.0 176.8 jit_solution(12806258082962454112)
XLA Ops:
  7.2 1.8 %make_pieces.1 = f32[8,2,32,256]{3,2,1,0:T(8,128)} custom-call(s32[1]{0:T(128)} %bitcast.place_ref, bf16[512,256]{1,0:T(8,128)(2,1)} %up_ref.1, f32[2,512]{1,0:T(2,128)} %bitcast.12, bf16[512,256]{1,0:T(8,128)(2,1)} %down_ref.1, f32[2,512]{1,0:T(2,128)} %bitcast.13), custom_call_target="tpu_custom_call" | custom-call | tf_op jit(solution)/shard_map/make_pieces/pallas_call | solution.py:157
  9.0 5.9 %all-to-all-start = ((f32[8,2,32,256]{3,2,1,0:T(8,128)}), f32[8,2,32,256]{3,2,1,0:T(8,128)S(1)}, u32[]{:S(2)}, u32[]{:S(2)}) async-start(f32[8,2,32,256]{3,2,1,0:T(8,128)} %make_pieces.1), calls=%async_computation | async-start | bytes 1048576 | tf_op jit(solution)/shard_map/all_to_all | solution.py:22
  14.8 0.0 all-gather.3.cloned.1.call-start
  14.9 0.0 copy-start.3
  14.9 1.3 copy-done.3
  16.2 0.7 cut_columns.1
  16.9 2.3 %copy-done.1 = f32[8,320,512]{2,1,0:T(8,128)} copy-done((f32[8,320,512]{2,1,0:T(8,128)}, f32[8,320,512]{2,1,0:T(8,128)S(1)}, u32[]{:S(2)}) %copy-start.1) | copy-done | bytes 5242904
  19.2 3.2 %all-to-all-done = f32[8,2,32,256]{3,2,1,0:T(8,128)S(1)} async-done(((f32[8,2,32,256]{3,2,1,0:T(8,128)}), f32[8,2,32,256]{3,2,1,0:T(8,128)S(1)}, u32[]{:S(2)}, u32[]{:S(2)}) %all-to-all-start) | async-done | bytes 524320 | tf_op jit(solution)/shard_map/all_to_all | solution.py:22
  22.4 0.8 copy-done.4
  23.2 0.0 all-gather.3.cloned.1.call-update
  23.2 4.7 %all-to-all-start.1 = ((f32[8,320,512]{2,1,0:T(8,128)}), f32[8,320,512]{2,1,0:T(8,128)}, u32[]{:S(2)}, u32[]{:S(2)}) async-start(f32[8,320,512]{2,1,0:T(8,128)} %copy-done.1), calls=%async_computation.1 | async-start | bytes 10485760 | tf_op jit(solution)/shard_map/all_to_all | solution.py:22
  27.9 59.6 %all-gather.3.cloned.1.call-done = f32[128,2,32,256]{3,2,1,0:T(8,128)} async-done(((f32[8,2,32,256]{3,2,1,0:T(8,128)}), f32[128,2,32,256]{3,2,1,0:T(8,128)}) %all-gather.3.cloned.1.call-update) | async-done | bytes 8388624 | tf_op jit(solution)/shard_map/all_gather | solution.py:282
  87.5 6.0 %hidden_pass.1 = (f32[4,160,256]{2,1,0:T(8,128)}, f32[160,256]{1,0:T(8,128)S(1)}) custom-call(f32[16,8,2,32,256]{4,3,2,1,0:T(8,128)} %bitcast.8, bf16[160,4096]{1,0:T(8,128)(2,1)S(1)} %copy-done.2, bf16[160,4096]{1,0:T(8,128)(2,1)} %grads_ref.3), custom_call_target="tpu_custom_call" | custom-call | flops 671088640 | bytes 13000000 | tf_op jit(solution)/shard_map/hidden_pass/pallas_call | solution.py:76
  93.5 4.0 %all-to-all-start.2 = ((f32[4,160,256]{2,1,0:T(8,128)}), f32[4,160,256]{2,1,0:T(8,128)S(1)}, u32[]{:S(2)}, u32[]{:S(2)}) async-start(f32[4,160,256]{2,1,0:T(8,128)} %get-tuple-element.18), calls=%async_computation.2 | async-start | bytes 1310720 | tf_op jit(solution)/shard_map/all_to_all | solution.py:22
  97.5 3.1 %collective-permute-start = (f32[160,256]{1,0:T(8,128)S(1)}, f32[160,256]{1,0:T(8,128)S(1)}, u32[]{:S(2)}, u32[]{:S(2)}) collective-permute-start(f32[160,256]{1,0:T(8,128)S(1)} %get-tuple-element.14.hidden_ref), channel_id=1, source_target_pairs={{0,1},{1,0},{2,3},{3,2},{4,5},{5,4},{6,7},{7,6},{8,9},{9,8},{10,11... | collective-permute-start | bytes 491528 | tf_op jit(solution)/shard_map/ppermute | solution.py:286
  100.6 4.0 %collective-permute-done = f32[160,256]{1,0:T(8,128)S(1)} collective-permute-done((f32[160,256]{1,0:T(8,128)S(1)}, f32[160,256]{1,0:T(8,128)S(1)}, u32[]{:S(2)}, u32[]{:S(2)}) %collective-permute-start) | collective-permute-done | bytes 163872 | tf_op jit(solution)/shard_map/ppermute | solution.py:286
  104.6 3.3 %all-to-all-done.2.act_ref = f32[4,160,256]{2,1,0:T(8,128)S(1)} async-done(((f32[4,160,256]{2,1,0:T(8,128)}), f32[4,160,256]{2,1,0:T(8,128)S(1)}, u32[]{:S(2)}, u32[]{:S(2)}) %all-to-all-start.2) | async-done | bytes 655392 | tf_op jit(solution)/shard_map/all_to_all | solution.py:22
  107.9 1.2 broadcast_in_dim.10
  109.1 3.5 %all-to-all-start.3 = ((f32[4,2,160,256]{3,2,1,0:T(8,128)}), f32[4,2,160,256]{3,2,1,0:T(8,128)S(1)}, u32[]{:S(2)}, u32[]{:S(2)}) async-start(f32[4,2,160,256]{3,2,1,0:T(8,128)} %broadcast_in_dim.10), calls=%async_computation.3 | async-start | bytes 2621440 | tf_op jit(solution)/shard_map/all_to_all | solution.py:22
  112.6 3.1 %collective-permute-start.1 = (f32[4,160,256]{2,1,0:T(8,128)S(1)}, f32[4,160,256]{2,1,0:T(8,128)S(1)}, u32[]{:S(2)}, u32[]{:S(2)}) collective-permute-start(f32[4,160,256]{2,1,0:T(8,128)S(1)} %all-to-all-done.2.act_ref), channel_id=1, source_target_pairs={{0,1},{1,0},{2,3},{3,2},{4,5},{5,4},{6,7},{7,6},{8,9},{9,8},{10,11... | collective-permute-start | bytes 1966088 | tf_op jit(solution)/shard_map/ppermute | solution.py:292
  115.8 0.1 pad_add_fusion.place_ref
  115.9 3.7 %narrow.1.left_hbm = bf16[8,320,512]{2,1,0:T(8,128)(2,1)} custom-call(f32[8,320,512]{2,1,0:T(8,128)} %all-to-all-done.1.columns_ref), custom_call_target="tpu_custom_call" | custom-call | bytes 12000000 | tf_op jit(solution)/shard_map/narrow/pallas_call | solution.py:178
  119.6 9.8 %collective-permute-done.1.act_peer_ref = f32[4,160,256]{2,1,0:T(8,128)S(1)} collective-permute-done((f32[4,160,256]{2,1,0:T(8,128)S(1)}, f32[4,160,256]{2,1,0:T(8,128)S(1)}, u32[]{:S(2)}, u32[]{:S(2)}) %collective-permute-start.1) | collective-permute-done | bytes 655392 | tf_op jit(solution)/shard_map/ppermute | solution.py:292
  129.4 5.8 %node_sums.1 = (f32[32,16,256]{2,1,0:T(8,128)S(1)}, f32[32,16,256]{2,1,0:T(8,128)S(1)}) custom-call(s32[2]{0:T(128)S(1)} %pad_add_fusion.place_ref, bf16[8,320,512]{2,1,0:T(8,128)(2,1)} %narrow.1.left_hbm, f32[4,2,160,256]{3,2,1,0:T(8,128)S(1)} %all-to-all-done.3.hidden_ref, f32[4,160,256]{2,1,0:T(8,128)S(1)} %all-to-all-done.2.act_ref, ...), custom_call_target="tpu_custom_call" | custom-call | flops 671088640 | bytes 9000000 | tf_op jit(solution)/shard_map/node_sums/pallas_call | solution.py:249
  135.2 4.2 %collective-permute-start.2 = (f32[32,16,256]{2,1,0:T(8,128)S(1)}, f32[32,16,256]{2,1,0:T(8,128)S(1)}, u32[]{:S(2)}, u32[]{:S(2)}) collective-permute-start(f32[32,16,256]{2,1,0:T(8,128)S(1)} %get-tuple-element.22), channel_id=1, source_target_pairs={{0,8},{8,0},{1,9},{9,1},{2,10},{10,2},{3,11},{11,3},{4,12},{12,4},... | collective-permute-start | bytes 1572872 | tf_op jit(solution)/shard_map/ppermute | solution.py:297
  139.4 1.5 collective-permute-done.2
  141.0 0.9 add.7
  141.9 8.9 %all-to-all-start.4 = ((f32[32,16,256]{2,1,0:T(8,128)}), f32[32,16,256]{2,1,0:T(8,128)S(1)}, u32[]{:S(2)}, u32[]{:S(2)}) async-start(f32[32,16,256]{2,1,0:T(8,128)} %add.7), calls=%async_computation.4 | async-start | bytes 1048576 | tf_op jit(solution)/shard_map/all_to_all | solution.py:22
  150.8 3.4 %copy-done = f32[128,2,32,256]{3,2,1,0:T(8,128)S(1)} copy-done((f32[128,2,32,256]{3,2,1,0:T(8,128)S(1)}, f32[128,2,32,256]{3,2,1,0:T(8,128)}, u32[]{:S(2)}) %copy-start) | copy-done | bytes 8388632
  154.2 2.7 %input_pass.1 = bf16[160,4096]{1,0:T(8,128)(2,1)} custom-call(f32[160,256]{1,0:T(8,128)S(1)} %get-tuple-element.14.hidden_ref, f32[16,8,2,32,256]{4,3,2,1,0:T(8,128)S(1)} %bitcast.9), custom_call_target="tpu_custom_call" | custom-call | flops 335544320 | bytes 6000000 | tf_op jit(solution)/shard_map/input_pass/pallas_call | solution.py:119
  156.8 12.5 %all-to-all-done.4 = f32[32,16,256]{2,1,0:T(8,128)S(1)} async-done(((f32[32,16,256]{2,1,0:T(8,128)}), f32[32,16,256]{2,1,0:T(8,128)S(1)}, u32[]{:S(2)}, u32[]{:S(2)}) %all-to-all-start.4) | async-done | bytes 524320 | tf_op jit(solution)/shard_map/all_to_all | solution.py:22
  169.3 0.6 fusion
  (10 shorter events, 0.1 us)
Async XLA Ops:
  7.2 7.7 %copy-start.2 = (bf16[160,4096]{1,0:T(8,128)(2,1)S(1)}, bf16[160,4096]{1,0:T(8,128)(2,1)}, u32[]{:S(2)}) copy-start(bf16[160,4096]{1,0:T(8,128)(2,1)} %tokens_ref.3) | copy-start | bytes 3932164
  9.0 13.4 %all-to-all-start = ((f32[8,2,32,256]{3,2,1,0:T(8,128)}), f32[8,2,32,256]{3,2,1,0:T(8,128)S(1)}, u32[]{:S(2)}, u32[]{:S(2)}) async-start(f32[8,2,32,256]{3,2,1,0:T(8,128)} %make_pieces.1), calls=%async_computation | async-start | bytes 1048576 | tf_op jit(solution)/shard_map/all_to_all | solution.py:22
  14.8 72.7 %all-gather.3.cloned.1.call-start = ((), (), s32[]{:S(2)}) async-start(), calls=%async_computation.5 | async-start | bytes 8912896 | tf_op jit(solution)/shard_map/all_gather | solution.py:282
  14.9 1.3 copy-start.3
  16.9 2.3 %copy-start.1 = (f32[8,320,512]{2,1,0:T(8,128)}, f32[8,320,512]{2,1,0:T(8,128)S(1)}, u32[]{:S(2)}) copy-start(f32[8,320,512]{2,1,0:T(8,128)S(1)} %cut_columns.1) | copy-start | bytes 15728644
  22.4 0.8 copy-start.4
  23.2 70.3 %all-to-all-start.1 = ((f32[8,320,512]{2,1,0:T(8,128)}), f32[8,320,512]{2,1,0:T(8,128)}, u32[]{:S(2)}, u32[]{:S(2)}) async-start(f32[8,320,512]{2,1,0:T(8,128)} %copy-done.1), calls=%async_computation.1 | async-start | bytes 10485760 | tf_op jit(solution)/shard_map/all_to_all | solution.py:22
  93.5 14.4 %all-to-all-start.2 = ((f32[4,160,256]{2,1,0:T(8,128)}), f32[4,160,256]{2,1,0:T(8,128)S(1)}, u32[]{:S(2)}, u32[]{:S(2)}) async-start(f32[4,160,256]{2,1,0:T(8,128)} %get-tuple-element.18), calls=%async_computation.2 | async-start | bytes 1310720 | tf_op jit(solution)/shard_map/all_to_all | solution.py:22
  97.5 7.1 %collective-permute-start = (f32[160,256]{1,0:T(8,128)S(1)}, f32[160,256]{1,0:T(8,128)S(1)}, u32[]{:S(2)}, u32[]{:S(2)}) collective-permute-start(f32[160,256]{1,0:T(8,128)S(1)} %get-tuple-element.14.hidden_ref), channel_id=1, source_target_pairs={{0,1},{1,0},{2,3},{3,2},{4,5},{5,4},{6,7},{7,6},{8,9},{9,8},{10,11... | collective-permute-start | bytes 491528 | tf_op jit(solution)/shard_map/ppermute | solution.py:286
  109.1 20.3 %all-to-all-start.3 = ((f32[4,2,160,256]{3,2,1,0:T(8,128)}), f32[4,2,160,256]{3,2,1,0:T(8,128)S(1)}, u32[]{:S(2)}, u32[]{:S(2)}) async-start(f32[4,2,160,256]{3,2,1,0:T(8,128)} %broadcast_in_dim.10), calls=%async_computation.3 | async-start | bytes 2621440 | tf_op jit(solution)/shard_map/all_to_all | solution.py:22
  112.6 16.7 %collective-permute-start.1 = (f32[4,160,256]{2,1,0:T(8,128)S(1)}, f32[4,160,256]{2,1,0:T(8,128)S(1)}, u32[]{:S(2)}, u32[]{:S(2)}) collective-permute-start(f32[4,160,256]{2,1,0:T(8,128)S(1)} %all-to-all-done.2.act_ref), channel_id=1, source_target_pairs={{0,1},{1,0},{2,3},{3,2},{4,5},{5,4},{6,7},{7,6},{8,9},{9,8},{10,11... | collective-permute-start | bytes 1966088 | tf_op jit(solution)/shard_map/ppermute | solution.py:292
  135.2 5.7 %collective-permute-start.2 = (f32[32,16,256]{2,1,0:T(8,128)S(1)}, f32[32,16,256]{2,1,0:T(8,128)S(1)}, u32[]{:S(2)}, u32[]{:S(2)}) collective-permute-start(f32[32,16,256]{2,1,0:T(8,128)S(1)} %get-tuple-element.22), channel_id=1, source_target_pairs={{0,8},{8,0},{1,9},{9,1},{2,10},{10,2},{3,11},{11,3},{4,12},{12,4},... | collective-permute-start | bytes 1572872 | tf_op jit(solution)/shard_map/ppermute | solution.py:297
  141.9 27.4 %all-to-all-start.4 = ((f32[32,16,256]{2,1,0:T(8,128)}), f32[32,16,256]{2,1,0:T(8,128)S(1)}, u32[]{:S(2)}, u32[]{:S(2)}) async-start(f32[32,16,256]{2,1,0:T(8,128)} %add.7), calls=%async_computation.4 | async-start | bytes 1048576 | tf_op jit(solution)/shard_map/all_to_all | solution.py:22
  150.8 3.4 %copy-start = (f32[128,2,32,256]{3,2,1,0:T(8,128)S(1)}, f32[128,2,32,256]{3,2,1,0:T(8,128)}, u32[]{:S(2)}) copy-start(f32[128,2,32,256]{3,2,1,0:T(8,128)} %all-gather.3.cloned.1.call-done) | copy-start | bytes 25165828
Sparse Core Ops, SparseCore 0:
  23.3 64.1 all-gather.2

commit v8 on v7

--- a/solution.py
+++ b/solution.py
@@ -14,8 +14,11 @@
 GROUP = ("z", "c")
 SHARDS = 2
 VMEM_LIMIT = 16 * 1024 * 1024
-HIDDEN_LIMIT = 52 * 1024 * 1024
-PIECE_LIMIT = 60 * 1024 * 1024
+HIDDEN_LIMIT = 20 * 1024 * 1024
+
+
+def in_hbm(array):
+    return pltpu.with_memory_space_constraint(array, pltpu.HBM)
 
 
 def exchange(array, axes):
@@ -37,25 +40,31 @@
 
 
 def hidden_kernel(
-    weights_hbm, tokens_ref, grads_ref, act_hbm, hidden_ref, weights, act, pre, back, in_sems, out_sems
+    weights_hbm, tokens_ref, grads_ref, act_hbm, hidden_ref, weights, act, in_sems, out_sems
 ):
-    n, groups, _, piece, width = weights.shape
+    kinds, n, groups, piece, width = weights.shape
     shard = groups * piece
     arrivals = [
-        pltpu.make_async_copy(weights_hbm.at[:, k], weights.at[k], in_sems.at[k]) for k in range(n)
+        [
+            pltpu.make_async_copy(weights_hbm.at[:, k, kind], weights.at[kind, k], in_sems.at[kind, k])
+            for k in range(n)
+        ]
+        for kind in range(kinds)
     ]
-    for copy in arrivals:
+    for copy in arrivals[0] + arrivals[1]:
         copy.start()
-    pre[...] = jnp.zeros_like(pre)
-    back[...] = jnp.zeros_like(back)
-    for k in range(n):
-        arrivals[k].wait()
-        up = weights[k, :, 0].reshape(shard, width).astype(jnp.bfloat16)
-        down = weights[k, :, 1].reshape(shard, width).astype(jnp.bfloat16)
-        columns = slice(k * shard, (k + 1) * shard)
-        pre[...] += jnp.dot(tokens_ref[:, columns], up, preferred_element_type=jnp.float32)
-        back[...] += jnp.dot(grads_ref[:, columns], down, preferred_element_type=jnp.float32)
-    v = pre[...]
+
+    def product(kind, left):
+        total = None
+        for k in range(n):
+            arrivals[kind][k].wait()
+            block = weights[kind, k].reshape(shard, width).astype(jnp.bfloat16)
+            columns = left[:, k * shard : (k + 1) * shard]
+            term = jnp.dot(columns, block, preferred_element_type=jnp.float32)
+            total = term if total is None else total + term
+        return total
+
+    v = product(0, tokens_ref)
     t = inner_tanh(v)
     act[...] = (0.5 * v * (1.0 + t)).astype(jnp.bfloat16).astype(jnp.float32)
     copies = act_hbm.shape[0]
@@ -65,7 +74,8 @@
     slope = 0.5 * (1.0 + t) + 0.5 * v * (1.0 - t * t) * math.sqrt(2.0 / math.pi) * (
         1.0 + 3.0 * 0.044715 * v * v
     )
-    hidden_ref[...] = (back[...] * slope).astype(jnp.bfloat16).astype(jnp.float32)
+    back = product(1, grads_ref)
+    hidden_ref[...] = (back * slope).astype(jnp.bfloat16).astype(jnp.float32)
     for copy in departures:
         copy.wait()
 
@@ -86,11 +96,9 @@
             jax.ShapeDtypeStruct((rows, width), jnp.float32),
         ],
         scratch_shapes=[
-            pltpu.VMEM((n, groups, kinds, piece, width), jnp.float32),
+            pltpu.VMEM((kinds, n, groups, piece, width), jnp.float32),
             pltpu.VMEM((rows, width), jnp.float32),
-            pltpu.VMEM((rows, width), jnp.float32),
-            pltpu.VMEM((rows, width), jnp.float32),
-            pltpu.SemaphoreType.DMA((n,)),
+            pltpu.SemaphoreType.DMA((kinds, n)),
             pltpu.SemaphoreType.DMA((copies,)),
         ],
         compiler_params=pltpu.CompilerParams(vmem_limit_bytes=HIDDEN_LIMIT),
@@ -98,7 +106,7 @@
             flops=4 * rows * depth * width, bytes_accessed=13000000, transcendentals=rows * width
         ),
         name="hidden_pass",
-    )(weights, tokens, grads)
+    )(in_hbm(weights), tokens, grads)
 
 
 def input_kernel(hidden_ref, weights_ref, out_ref):
@@ -163,9 +171,15 @@
             out_specs=pl.BlockSpec(out, lambda k, place_ref: (0, 0, 0, 0)),
         ),
         out_shape=jax.ShapeDtypeStruct(out, jnp.float32),
-        compiler_params=pltpu.CompilerParams(vmem_limit_bytes=PIECE_LIMIT),
+        compiler_params=pltpu.CompilerParams(vmem_limit_bytes=VMEM_LIMIT),
         name="make_pieces",
-    )(place[None], up_codes, up_scales.T, down_codes, down_scales.T)
+    )(
+        place[None],
+        in_hbm(up_codes),
+        in_hbm(up_scales.T),
+        in_hbm(down_codes),
+        in_hbm(down_scales.T),
+    )
 
 
 def narrow_kernel(columns_ref, out_ref):
@@ -181,7 +195,7 @@
         in_specs=[block],
         out_specs=block,
         out_shape=jax.ShapeDtypeStruct(columns.shape, jnp.bfloat16),
-        compiler_params=pltpu.CompilerParams(vmem_limit_bytes=PIECE_LIMIT),
+        compiler_params=pltpu.CompilerParams(vmem_limit_bytes=VMEM_LIMIT),
         cost_estimate=pl.CostEstimate(flops=0, bytes_accessed=12000000, transcendentals=0),
         name="narrow",
     )(columns)
@@ -208,25 +222,17 @@
     )(tokens, grads)
 
 
-def node_kernel(place_ref, left_hbm, hidden_ref, act_ref, act_peer_ref, mine_ref, other_ref, left, sems):
+def node_kernel(place_ref, left, hidden_ref, act_ref, act_peer_ref, mine_ref, other_ref):
     rows, width = act_ref.shape[1:]
     n = left.shape[0]
-    copies = [
-        pltpu.make_async_copy(
-            left_hbm.at[2 * (p // 2) + lax.rem(place_ref[1] + p, 2)], left.at[p], sems.at[p]
-        )
-        for p in range(n)
-    ]
-    for copy in copies:
-        copy.start()
     totals = [None, None]
     for p in range(n):
-        copies[p].wait()
+        owner = 2 * (p // 2) + lax.rem(place_ref[1] + p, 2)
         rights = (hidden_ref[p // 2, p % 2], (act_peer_ref if p % 2 else act_ref)[p // 2])
         for kind in range(2):
             term = lax.dot_general(
                 rights[kind].astype(jnp.bfloat16),
-                left[p, kind * rows : (kind + 1) * rows],
+                left[owner, kind * rows : (kind + 1) * rows],
                 (((0,), (0,)), ((), ())),
                 preferred_element_type=jnp.float32,
             )
@@ -242,28 +248,27 @@
 
 
 def node_sums(place, left, hidden, act, act_peer, owned):
-    n, _, height = left.shape
-    _, rows, width = act.shape
+    height = left.shape[2]
+    n, rows, width = 2 * act.shape[0], act.shape[1], act.shape[2]
     half = (height // (2 * owned), 2 * owned, width)
     vmem = pl.BlockSpec(memory_space=pltpu.VMEM)
     return pl.pallas_call(
         node_kernel,
         in_specs=[
             pl.BlockSpec(memory_space=pltpu.SMEM),
-            pl.BlockSpec(memory_space=pltpu.HBM),
             vmem,
             vmem,
             vmem,
+            vmem,
         ],
         out_specs=[vmem, vmem],
         out_shape=[jax.ShapeDtypeStruct(half, jnp.float32)] * 2,
-        scratch_shapes=[pltpu.VMEM(left.shape, left.dtype), pltpu.SemaphoreType.DMA((n,))],
         compiler_params=pltpu.CompilerParams(vmem_limit_bytes=VMEM_LIMIT),
         cost_estimate=pl.CostEstimate(
             flops=4 * n * rows * height * width, bytes_accessed=9000000, transcendentals=0
         ),
         name="node_sums",
-    )(place, pltpu.with_memory_space_constraint(left, pltpu.HBM), hidden, act, act_peer)
+    )(place, left, hidden, act, act_peer)
 
 
 def local(tokens, out_grad, up_codes, up_scales, down_codes, down_scales):

time: 178 us -> 177 us (level)
  the two profiles are of different devices: /device:TPU:1 before, /device:TPU:10 now
where the time goes in v8:
time: 177 us; the launch traced here: 176 us
  waiting for transfers between devices  91.5 us (52%)
  starting transfers between devices  43.8 us (25%)
  Pallas kernels  15.8 us (9%)
  between operations  14.2 us (8%)
  local copies, waits for them, and re-layouts  9.53 us (5%)
    all_gather x1, waiting for transfers between devices, local(): weights = lax.all_gather(pieces, GROUP, axis=0)  53.7 us
    all_to_all x5, starting transfers between devices, exchange(): return lax.all_to_all(array, axes, split_axis=0, concat_axis=0, tiled=True)  37 us
    all_to_all x5, waiting for transfers between devices, exchange(): return lax.all_to_all(array, axes, split_axis=0, concat_axis=0, tiled=True)  18.4 us
    ppermute x1, waiting for transfers between devices, local(): act_peer_all = lax.ppermute(act_all, 'yl', SWAP)  12.3 us
    unnamed x12, local copies, waits for them, and re-layouts  7.76 us
    ppermute x1, waiting for transfers between devices, local(): hidden_peer = lax.ppermute(hidden, 'yl', SWAP)  5.23 us
    pallas_call x1, Pallas kernels, node_sums(): pl.pallas_call(node_kernel, in_specs=[pl.BlockSpec(memory_space=pltpu.SME...  4.15 us
    pallas_call x1, Pallas kernels, hidden_pass(): pl.pallas_call(hidden_kernel, in_specs=[pl.BlockSpec(memory_space=pltpu.H...  3.85 us
  transfers between devices with their start and end apart: 9, of which 7 were waited for; matrix products, arithmetic and copies ran while one was open for 0% of the time, Pallas kernels for 6%

profile of v8, /device:TPU:10, one launch (start us, length us, event | category | flops | bytes accessed | tf_op | source)
XLA Modules:
  0.0 175.9 jit_solution(13268541126724869921)
XLA Ops:
  7.2 1.8 %make_pieces.1 = f32[8,2,32,256]{3,2,1,0:T(8,128)} custom-call(s32[1]{0:T(128)} %bitcast.place_ref, bf16[512,256]{1,0:T(8,128)(2,1)} %up_ref.1, f32[2,512]{1,0:T(2,128)} %bitcast.12, bf16[512,256]{1,0:T(8,128)(2,1)} %down_ref.1, f32[2,512]{1,0:T(2,128)} %bitcast.13), custom_call_target="tpu_custom_call" | custom-call | tf_op jit(solution)/shard_map/make_pieces/pallas_call | solution.py:165
  9.0 9.2 %all-to-all-start = ((f32[8,2,32,256]{3,2,1,0:T(8,128)}), f32[8,2,32,256]{3,2,1,0:T(8,128)S(1)}, u32[]{:S(2)}, u32[]{:S(2)}) async-start(f32[8,2,32,256]{3,2,1,0:T(8,128)} %make_pieces.1), calls=%async_computation | async-start | bytes 1048576 | tf_op jit(solution)/shard_map/all_to_all | solution.py:25
  18.2 0.0 copy-start.3
  18.2 1.3 copy-done.3
  19.5 0.7 cut_columns.1
  20.2 2.3 %copy-done.1 = f32[8,320,512]{2,1,0:T(8,128)} copy-done((f32[8,320,512]{2,1,0:T(8,128)}, f32[8,320,512]{2,1,0:T(8,128)S(1)}, u32[]{:S(2)}) %copy-start.1) | copy-done | bytes 5242904
  22.5 2.3 %all-to-all-done = f32[8,2,32,256]{3,2,1,0:T(8,128)S(1)} async-done(((f32[8,2,32,256]{3,2,1,0:T(8,128)}), f32[8,2,32,256]{3,2,1,0:T(8,128)S(1)}, u32[]{:S(2)}, u32[]{:S(2)}) %all-to-all-start) | async-done | bytes 524320 | tf_op jit(solution)/shard_map/all_to_all | solution.py:25
  24.8 0.8 copy-done.5
  25.6 0.0 all-gather.3.cloned.1.call-update
  25.6 0.0 copy-start.4
  25.6 6.8 %all-to-all-start.1 = ((f32[8,320,512]{2,1,0:T(8,128)}), f32[8,320,512]{2,1,0:T(8,128)}, u32[]{:S(2)}, u32[]{:S(2)}) async-start(f32[8,320,512]{2,1,0:T(8,128)} %copy-done.1), calls=%async_computation.1 | async-start | bytes 10485760 | tf_op jit(solution)/shard_map/all_to_all | solution.py:25
  32.5 53.7 %all-gather.3.cloned.1.call-done = f32[128,2,32,256]{3,2,1,0:T(8,128)} async-done(((f32[8,2,32,256]{3,2,1,0:T(8,128)}), f32[128,2,32,256]{3,2,1,0:T(8,128)}) %all-gather.3.cloned.1.call-update) | async-done | bytes 8388624 | tf_op jit(solution)/shard_map/all_gather | solution.py:287
  86.2 3.9 %hidden_pass.1 = (f32[4,160,256]{2,1,0:T(8,128)}, f32[160,256]{1,0:T(8,128)S(1)}) custom-call(f32[16,8,2,32,256]{4,3,2,1,0:T(8,128)} %bitcast.8, bf16[160,4096]{1,0:T(8,128)(2,1)S(1)} %copy-done.2, bf16[160,4096]{1,0:T(8,128)(2,1)S(1)} %copy-done.4), custom_call_target="tpu_custom_call" | custom-call | flops 671088640 | bytes 13000000 | tf_op jit(solution)/shard_map/hidden_pass/pallas_call | solution.py:86
  90.0 4.8 %all-to-all-start.2 = ((f32[4,160,256]{2,1,0:T(8,128)}), f32[4,160,256]{2,1,0:T(8,128)S(1)}, u32[]{:S(2)}, u32[]{:S(2)}) async-start(f32[4,160,256]{2,1,0:T(8,128)} %get-tuple-element.18), calls=%async_computation.2 | async-start | bytes 1310720 | tf_op jit(solution)/shard_map/all_to_all | solution.py:25
  94.8 2.4 %collective-permute-start = (f32[160,256]{1,0:T(8,128)S(1)}, f32[160,256]{1,0:T(8,128)S(1)}, u32[]{:S(2)}, u32[]{:S(2)}) collective-permute-start(f32[160,256]{1,0:T(8,128)S(1)} %get-tuple-element.14.hidden_ref), channel_id=1, source_target_pairs={{0,1},{1,0},{2,3},{3,2},{4,5},{5,4},{6,7},{7,6},{8,9},{9,8},{10,11... | collective-permute-start | bytes 491528 | tf_op jit(solution)/shard_map/ppermute | solution.py:291
  97.3 5.2 %collective-permute-done = f32[160,256]{1,0:T(8,128)S(1)} collective-permute-done((f32[160,256]{1,0:T(8,128)S(1)}, f32[160,256]{1,0:T(8,128)S(1)}, u32[]{:S(2)}, u32[]{:S(2)}) %collective-permute-start) | collective-permute-done | bytes 163872 | tf_op jit(solution)/shard_map/ppermute | solution.py:291
  102.5 2.1 %all-to-all-done.2.act_ref = f32[4,160,256]{2,1,0:T(8,128)S(1)} async-done(((f32[4,160,256]{2,1,0:T(8,128)}), f32[4,160,256]{2,1,0:T(8,128)S(1)}, u32[]{:S(2)}, u32[]{:S(2)}) %all-to-all-start.2) | async-done | bytes 655392 | tf_op jit(solution)/shard_map/all_to_all | solution.py:25
  104.7 1.2 broadcast_in_dim.10
  105.8 5.7 %all-to-all-start.3 = ((f32[4,2,160,256]{3,2,1,0:T(8,128)}), f32[4,2,160,256]{3,2,1,0:T(8,128)}, u32[]{:S(2)}, u32[]{:S(2)}) async-start(f32[4,2,160,256]{3,2,1,0:T(8,128)} %broadcast_in_dim.10), calls=%async_computation.3 | async-start | bytes 2621440 | tf_op jit(solution)/shard_map/all_to_all | solution.py:25
  111.6 2.4 %collective-permute-start.1 = (f32[4,160,256]{2,1,0:T(8,128)S(1)}, f32[4,160,256]{2,1,0:T(8,128)}, u32[]{:S(2)}, u32[]{:S(2)}) collective-permute-start(f32[4,160,256]{2,1,0:T(8,128)S(1)} %all-to-all-done.2.act_ref), channel_id=1, source_target_pairs={{0,1},{1,0},{2,3},{3,2},{4,5},{5,4},{6,7},{7,6},{8,9},{9,8},{10,11... | collective-permute-start | bytes 1966088 | tf_op jit(solution)/shard_map/ppermute | solution.py:297
  114.0 0.1 pad_add_fusion.place_ref
  114.1 2.7 %narrow.1.left = bf16[8,320,512]{2,1,0:T(8,128)(2,1)S(1)} custom-call(f32[8,320,512]{2,1,0:T(8,128)} %all-to-all-done.1.columns_ref), custom_call_target="tpu_custom_call" | custom-call | bytes 12000000 | tf_op jit(solution)/shard_map/narrow/pallas_call | solution.py:192
  116.8 12.3 %collective-permute-done.1.act_peer_ref = f32[4,160,256]{2,1,0:T(8,128)} collective-permute-done((f32[4,160,256]{2,1,0:T(8,128)S(1)}, f32[4,160,256]{2,1,0:T(8,128)}, u32[]{:S(2)}, u32[]{:S(2)}) %collective-permute-start.1) | collective-permute-done | bytes 655392 | tf_op jit(solution)/shard_map/ppermute | solution.py:297
  129.0 4.1 %node_sums.1 = (f32[32,16,256]{2,1,0:T(8,128)S(1)}, f32[32,16,256]{2,1,0:T(8,128)S(1)}) custom-call(s32[2]{0:T(128)S(1)} %pad_add_fusion.place_ref, bf16[8,320,512]{2,1,0:T(8,128)(2,1)S(1)} %narrow.1.left, f32[4,2,160,256]{3,2,1,0:T(8,128)} %all-to-all-done.3.hidden_ref, f32[4,160,256]{2,1,0:T(8,128)S(1)} %all-to-all-done.2.act_ref, ...), custom_call_target="tpu_custom_call" | custom-call | flops 671088640 | bytes 9000000 | tf_op jit(solution)/shard_map/node_sums/pallas_call | solution.py:255
  133.2 1.9 %collective-permute-start.2 = (f32[32,16,256]{2,1,0:T(8,128)S(1)}, f32[32,16,256]{2,1,0:T(8,128)S(1)}, u32[]{:S(2)}, u32[]{:S(2)}) collective-permute-start(f32[32,16,256]{2,1,0:T(8,128)S(1)} %get-tuple-element.22), channel_id=1, source_target_pairs={{0,8},{8,0},{1,9},{9,1},{2,10},{10,2},{3,11},{11,3},{4,12},{12,4},... | collective-permute-start | bytes 1572872 | tf_op jit(solution)/shard_map/ppermute | solution.py:302
  135.1 1.9 %collective-permute-done.2 = f32[32,16,256]{2,1,0:T(8,128)S(1)} collective-permute-done((f32[32,16,256]{2,1,0:T(8,128)S(1)}, f32[32,16,256]{2,1,0:T(8,128)S(1)}, u32[]{:S(2)}, u32[]{:S(2)}) %collective-permute-start.2) | collective-permute-done | bytes 524320 | tf_op jit(solution)/shard_map/ppermute | solution.py:302
  137.0 0.9 add.7
  137.9 10.4 %all-to-all-start.4 = ((f32[32,16,256]{2,1,0:T(8,128)}), f32[32,16,256]{2,1,0:T(8,128)S(1)}, u32[]{:S(2)}, u32[]{:S(2)}) async-start(f32[32,16,256]{2,1,0:T(8,128)} %add.7), calls=%async_computation.4 | async-start | bytes 1048576 | tf_op jit(solution)/shard_map/all_to_all | solution.py:25
  148.4 3.4 %copy-done = f32[128,2,32,256]{3,2,1,0:T(8,128)S(1)} copy-done((f32[128,2,32,256]{3,2,1,0:T(8,128)S(1)}, f32[128,2,32,256]{3,2,1,0:T(8,128)}, u32[]{:S(2)}) %copy-start) | copy-done | bytes 8388632
  151.7 2.7 %input_pass.1 = bf16[160,4096]{1,0:T(8,128)(2,1)} custom-call(f32[160,256]{1,0:T(8,128)S(1)} %get-tuple-element.14.hidden_ref, f32[16,8,2,32,256]{4,3,2,1,0:T(8,128)S(1)} %bitcast.9), custom_call_target="tpu_custom_call" | custom-call | flops 335544320 | bytes 6000000 | tf_op jit(solution)/shard_map/input_pass/pallas_call | solution.py:127
  154.4 13.9 %all-to-all-done.4 = f32[32,16,256]{2,1,0:T(8,128)S(1)} async-done(((f32[32,16,256]{2,1,0:T(8,128)}), f32[32,16,256]{2,1,0:T(8,128)S(1)}, u32[]{:S(2)}, u32[]{:S(2)}) %all-to-all-start.4) | async-done | bytes 524320 | tf_op jit(solution)/shard_map/all_to_all | solution.py:25
  168.4 0.6 fusion
  (12 shorter events, 0.1 us)
Async XLA Ops:
  7.2 11.0 %copy-start.2 = (bf16[160,4096]{1,0:T(8,128)(2,1)S(1)}, bf16[160,4096]{1,0:T(8,128)(2,1)}, u32[]{:S(2)}) copy-start(bf16[160,4096]{1,0:T(8,128)(2,1)} %tokens_ref.3) | copy-start | bytes 3932164
  9.0 15.8 %all-to-all-start = ((f32[8,2,32,256]{3,2,1,0:T(8,128)}), f32[8,2,32,256]{3,2,1,0:T(8,128)S(1)}, u32[]{:S(2)}, u32[]{:S(2)}) async-start(f32[8,2,32,256]{3,2,1,0:T(8,128)} %make_pieces.1), calls=%async_computation | async-start | bytes 1048576 | tf_op jit(solution)/shard_map/all_to_all | solution.py:25
  18.2 68.0 %all-gather.3.cloned.1.call-start = ((), (), s32[]{:S(2)}) async-start(), calls=%async_computation.5 | async-start | bytes 8912896 | tf_op jit(solution)/shard_map/all_gather | solution.py:287
  18.2 1.3 copy-start.3
  20.2 2.3 %copy-start.1 = (f32[8,320,512]{2,1,0:T(8,128)}, f32[8,320,512]{2,1,0:T(8,128)S(1)}, u32[]{:S(2)}) copy-start(f32[8,320,512]{2,1,0:T(8,128)S(1)} %cut_columns.1) | copy-start | bytes 15728644
  24.8 0.8 copy-start.5
  25.6 60.5 %copy-start.4 = (bf16[160,4096]{1,0:T(8,128)(2,1)S(1)}, bf16[160,4096]{1,0:T(8,128)(2,1)}, u32[]{:S(2)}) copy-start(bf16[160,4096]{1,0:T(8,128)(2,1)} %grads_ref.3) | copy-start | bytes 3932164
  25.6 64.4 %all-to-all-start.1 = ((f32[8,320,512]{2,1,0:T(8,128)}), f32[8,320,512]{2,1,0:T(8,128)}, u32[]{:S(2)}, u32[]{:S(2)}) async-start(f32[8,320,512]{2,1,0:T(8,128)} %copy-done.1), calls=%async_computation.1 | async-start | bytes 10485760 | tf_op jit(solution)/shard_map/all_to_all | solution.py:25
  90.0 14.7 %all-to-all-start.2 = ((f32[4,160,256]{2,1,0:T(8,128)}), f32[4,160,256]{2,1,0:T(8,128)S(1)}, u32[]{:S(2)}, u32[]{:S(2)}) async-start(f32[4,160,256]{2,1,0:T(8,128)} %get-tuple-element.18), calls=%async_computation.2 | async-start | bytes 1310720 | tf_op jit(solution)/shard_map/all_to_all | solution.py:25
  94.8 7.7 %collective-permute-start = (f32[160,256]{1,0:T(8,128)S(1)}, f32[160,256]{1,0:T(8,128)S(1)}, u32[]{:S(2)}, u32[]{:S(2)}) collective-permute-start(f32[160,256]{1,0:T(8,128)S(1)} %get-tuple-element.14.hidden_ref), channel_id=1, source_target_pairs={{0,1},{1,0},{2,3},{3,2},{4,5},{5,4},{6,7},{7,6},{8,9},{9,8},{10,11... | collective-permute-start | bytes 491528 | tf_op jit(solution)/shard_map/ppermute | solution.py:291
  105.8 23.2 %all-to-all-start.3 = ((f32[4,2,160,256]{3,2,1,0:T(8,128)}), f32[4,2,160,256]{3,2,1,0:T(8,128)}, u32[]{:S(2)}, u32[]{:S(2)}) async-start(f32[4,2,160,256]{3,2,1,0:T(8,128)} %broadcast_in_dim.10), calls=%async_computation.3 | async-start | bytes 2621440 | tf_op jit(solution)/shard_map/all_to_all | solution.py:25
  111.6 17.5 %collective-permute-start.1 = (f32[4,160,256]{2,1,0:T(8,128)S(1)}, f32[4,160,256]{2,1,0:T(8,128)}, u32[]{:S(2)}, u32[]{:S(2)}) collective-permute-start(f32[4,160,256]{2,1,0:T(8,128)S(1)} %all-to-all-done.2.act_ref), channel_id=1, source_target_pairs={{0,1},{1,0},{2,3},{3,2},{4,5},{5,4},{6,7},{7,6},{8,9},{9,8},{10,11... | collective-permute-start | bytes 1966088 | tf_op jit(solution)/shard_map/ppermute | solution.py:297
  133.2 3.8 %collective-permute-start.2 = (f32[32,16,256]{2,1,0:T(8,128)S(1)}, f32[32,16,256]{2,1,0:T(8,128)S(1)}, u32[]{:S(2)}, u32[]{:S(2)}) collective-permute-start(f32[32,16,256]{2,1,0:T(8,128)S(1)} %get-tuple-element.22), channel_id=1, source_target_pairs={{0,8},{8,0},{1,9},{9,1},{2,10},{10,2},{3,11},{11,3},{4,12},{12,4},... | collective-permute-start | bytes 1572872 | tf_op jit(solution)/shard_map/ppermute | solution.py:302
  137.9 30.4 %all-to-all-start.4 = ((f32[32,16,256]{2,1,0:T(8,128)}), f32[32,16,256]{2,1,0:T(8,128)S(1)}, u32[]{:S(2)}, u32[]{:S(2)}) async-start(f32[32,16,256]{2,1,0:T(8,128)} %add.7), calls=%async_computation.4 | async-start | bytes 1048576 | tf_op jit(solution)/shard_map/all_to_all | solution.py:25
  148.4 3.4 %copy-start = (f32[128,2,32,256]{3,2,1,0:T(8,128)S(1)}, f32[128,2,32,256]{3,2,1,0:T(8,128)}, u32[]{:S(2)}) copy-start(f32[128,2,32,256]{3,2,1,0:T(8,128)} %all-gather.3.cloned.1.call-done) | copy-start | bytes 25165828
Sparse Core Ops, SparseCore 0:
  25.7 60.3 all-gather.2

commit v9 on v8

--- a/solution.py
+++ b/solution.py
@@ -107,6 +107,32 @@
         ),
         name="hidden_pass",
     )(in_hbm(weights), tokens, grads)
+
+
+def pair_kernel(own_ref, peer_ref, out_hbm, sems):
+    copies = [
+        pltpu.make_async_copy(source, out_hbm.at[k, j], sems.at[k, j])
+        for k in range(out_hbm.shape[0])
+        for j, source in enumerate((own_ref, peer_ref))
+    ]
+    for copy in copies:
+        copy.start()
+    for copy in copies:
+        copy.wait()
+
+
+def pair_copies(own, peer, copies):
+    vmem = pl.BlockSpec(memory_space=pltpu.VMEM)
+    return pl.pallas_call(
+        pair_kernel,
+        in_specs=[vmem, vmem],
+        out_specs=pl.BlockSpec(memory_space=pltpu.HBM),
+        out_shape=pltpu.HBM((copies, 2) + own.shape, own.dtype),
+        scratch_shapes=[pltpu.SemaphoreType.DMA((copies, 2))],
+        compiler_params=pltpu.CompilerParams(vmem_limit_bytes=VMEM_LIMIT),
+        cost_estimate=pl.CostEstimate(flops=0, bytes_accessed=2000000, transcendentals=0),
+        name="pair_copies",
+    )(own, peer)
 
 
 def input_kernel(hidden_ref, weights_ref, out_ref):
@@ -291,8 +317,7 @@
     hidden_peer = lax.ppermute(hidden, "yl", SWAP)
     columns, act_copies = lax.optimization_barrier((columns, act_copies))
     act_all = exchange(act_copies, "x")
-    hidden_pair = jnp.stack([hidden, hidden_peer])
-    hidden_copies = jnp.broadcast_to(hidden_pair[None], (n_x,) + hidden_pair.shape)
+    hidden_copies = pair_copies(hidden, hidden_peer, n_x)
     act_all, hidden_copies = lax.optimization_barrier((act_all, hidden_copies))
     act_peer_all = lax.ppermute(act_all, "yl", SWAP)
     hidden_all = exchange(hidden_copies, "x")

time: 177 us -> 175 us (0.989)
  no operation moved by 1% of the time
where the time goes in v9:
time: 175 us
  waiting for transfers between devices  90.4 us (52%)
  starting transfers between devices  43.8 us (25%)
  Pallas kernels  16.8 us (10%)
  between operations  14.2 us (8%)
  local copies, waits for them, and re-layouts  8.37 us (5%)
    all_gather x1, waiting for transfers between devices, local(): weights = lax.all_gather(pieces, GROUP, axis=0)  53.7 us
    all_to_all x5, starting transfers between devices, exchange(): return lax.all_to_all(array, axes, split_axis=0, concat_axis=0, tiled=True)  37 us
    all_to_all x5, waiting for transfers between devices, exchange(): return lax.all_to_all(array, axes, split_axis=0, concat_axis=0, tiled=True)  17.3 us
    ppermute x1, waiting for transfers between devices, local(): act_peer_all = lax.ppermute(act_all, 'yl', SWAP)  12.3 us
    unnamed x12, local copies, waits for them, and re-layouts  7.76 us
    ppermute x1, waiting for transfers between devices, local(): hidden_peer = lax.ppermute(hidden, 'yl', SWAP)  5.23 us
    pallas_call x1, Pallas kernels, node_sums(): pl.pallas_call(node_kernel, in_specs=[pl.BlockSpec(memory_space=pltpu.SME...  4.07 us
    pallas_call x1, Pallas kernels, hidden_pass(): pl.pallas_call(hidden_kernel, in_specs=[pl.BlockSpec(memory_space=pltpu.H...  3.85 us
  transfers between devices with their start and end apart: 9, of which 7 were waited for; matrix products, arithmetic and copies ran while one was open for 0% of the time, Pallas kernels for 6%

profile of v9, /device:TPU:10, one launch (start us, length us, event | category | flops | bytes accessed | tf_op | source)
XLA Modules:
  0.0 174.6 jit_solution(10704475732572243023)
XLA Ops:
  7.2 1.8 %make_pieces.1 = f32[8,2,32,256]{3,2,1,0:T(8,128)} custom-call(s32[1]{0:T(128)} %bitcast.place_ref, bf16[512,256]{1,0:T(8,128)(2,1)} %up_ref.1, f32[2,512]{1,0:T(2,128)} %bitcast.8, bf16[512,256]{1,0:T(8,128)(2,1)} %down_ref.1, f32[2,512]{1,0:T(2,128)} %bitcast.9), custom_call_target="tpu_custom_call" | custom-call | tf_op jit(solution)/shard_map/make_pieces/pallas_call | solution.py:191
  9.0 9.2 %all-to-all-start = ((f32[8,2,32,256]{3,2,1,0:T(8,128)}), f32[8,2,32,256]{3,2,1,0:T(8,128)S(1)}, u32[]{:S(2)}, u32[]{:S(2)}) async-start(f32[8,2,32,256]{3,2,1,0:T(8,128)} %make_pieces.1), calls=%async_computation | async-start | bytes 1048576 | tf_op jit(solution)/shard_map/all_to_all | solution.py:25
  18.2 0.0 copy-start.3
  18.2 1.3 copy-done.3
  19.5 0.7 cut_columns.1
  20.2 2.3 %copy-done.1 = f32[8,320,512]{2,1,0:T(8,128)} copy-done((f32[8,320,512]{2,1,0:T(8,128)}, f32[8,320,512]{2,1,0:T(8,128)S(1)}, u32[]{:S(2)}) %copy-start.1) | copy-done | bytes 5242904
  22.5 2.3 %all-to-all-done = f32[8,2,32,256]{3,2,1,0:T(8,128)S(1)} async-done(((f32[8,2,32,256]{3,2,1,0:T(8,128)}), f32[8,2,32,256]{3,2,1,0:T(8,128)S(1)}, u32[]{:S(2)}, u32[]{:S(2)}) %all-to-all-start) | async-done | bytes 524320 | tf_op jit(solution)/shard_map/all_to_all | solution.py:25
  24.8 0.8 copy-done.5
  25.6 0.0 all-gather.3.cloned.1.call-update
  25.6 0.0 copy-start.4
  25.6 6.8 %all-to-all-start.1 = ((f32[8,320,512]{2,1,0:T(8,128)}), f32[8,320,512]{2,1,0:T(8,128)}, u32[]{:S(2)}, u32[]{:S(2)}) async-start(f32[8,320,512]{2,1,0:T(8,128)} %copy-done.1), calls=%async_computation.1 | async-start | bytes 10485760 | tf_op jit(solution)/shard_map/all_to_all | solution.py:25
  32.5 53.7 %all-gather.3.cloned.1.call-done = f32[128,2,32,256]{3,2,1,0:T(8,128)} async-done(((f32[8,2,32,256]{3,2,1,0:T(8,128)}), f32[128,2,32,256]{3,2,1,0:T(8,128)}) %all-gather.3.cloned.1.call-update) | async-done | bytes 8388624 | tf_op jit(solution)/shard_map/all_gather | solution.py:313
  86.2 3.9 %hidden_pass.1 = (f32[4,160,256]{2,1,0:T(8,128)}, f32[160,256]{1,0:T(8,128)S(1)}) custom-call(f32[16,8,2,32,256]{4,3,2,1,0:T(8,128)} %bitcast.6, bf16[160,4096]{1,0:T(8,128)(2,1)S(1)} %copy-done.2, bf16[160,4096]{1,0:T(8,128)(2,1)S(1)} %copy-done.4), custom_call_target="tpu_custom_call" | custom-call | flops 671088640 | bytes 13000000 | tf_op jit(solution)/shard_map/hidden_pass/pallas_call | solution.py:86
  90.0 4.8 %all-to-all-start.2 = ((f32[4,160,256]{2,1,0:T(8,128)}), f32[4,160,256]{2,1,0:T(8,128)S(1)}, u32[]{:S(2)}, u32[]{:S(2)}) async-start(f32[4,160,256]{2,1,0:T(8,128)} %get-tuple-element.18), calls=%async_computation.2 | async-start | bytes 1310720 | tf_op jit(solution)/shard_map/all_to_all | solution.py:25
  94.8 2.4 %collective-permute-start = (f32[160,256]{1,0:T(8,128)S(1)}, f32[160,256]{1,0:T(8,128)S(1)}, u32[]{:S(2)}, u32[]{:S(2)}) collective-permute-start(f32[160,256]{1,0:T(8,128)S(1)} %get-tuple-element.14.hidden_ref.own_ref), channel_id=1, source_target_pairs={{0,1},{1,0},{2,3},{3,2},{4,5},{5,4},{6,7},{7,6},{8,9},{9,8},{10,11... | collective-permute-start | bytes 491528 | tf_op jit(solution)/shard_map/ppermute | solution.py:317
  97.3 5.2 %collective-permute-done.peer_ref = f32[160,256]{1,0:T(8,128)S(1)} collective-permute-done((f32[160,256]{1,0:T(8,128)S(1)}, f32[160,256]{1,0:T(8,128)S(1)}, u32[]{:S(2)}, u32[]{:S(2)}) %collective-permute-start) | collective-permute-done | bytes 163872 | tf_op jit(solution)/shard_map/ppermute | solution.py:317
  102.5 1.1 pair_copies.1
  103.6 1.0 all-to-all-done.2.act_ref
  104.7 5.7 %all-to-all-start.3 = ((f32[4,2,160,256]{3,2,1,0:T(8,128)}), f32[4,2,160,256]{3,2,1,0:T(8,128)}, u32[]{:S(2)}, u32[]{:S(2)}) async-start(f32[4,2,160,256]{3,2,1,0:T(8,128)} %pair_copies.1), calls=%async_computation.3 | async-start | bytes 2621440 | tf_op jit(solution)/shard_map/all_to_all | solution.py:25
  110.4 2.4 %collective-permute-start.1 = (f32[4,160,256]{2,1,0:T(8,128)S(1)}, f32[4,160,256]{2,1,0:T(8,128)}, u32[]{:S(2)}, u32[]{:S(2)}) collective-permute-start(f32[4,160,256]{2,1,0:T(8,128)S(1)} %all-to-all-done.2.act_ref), channel_id=1, source_target_pairs={{0,1},{1,0},{2,3},{3,2},{4,5},{5,4},{6,7},{7,6},{8,9},{9,8},{10,11... | collective-permute-start | bytes 1966088 | tf_op jit(solution)/shard_map/ppermute | solution.py:322
  112.9 0.1 pad_add_fusion.place_ref
  112.9 2.7 %narrow.1.left = bf16[8,320,512]{2,1,0:T(8,128)(2,1)S(1)} custom-call(f32[8,320,512]{2,1,0:T(8,128)} %all-to-all-done.1.columns_ref), custom_call_target="tpu_custom_call" | custom-call | bytes 12000000 | tf_op jit(solution)/shard_map/narrow/pallas_call | solution.py:218
  115.6 12.3 %collective-permute-done.1.act_peer_ref = f32[4,160,256]{2,1,0:T(8,128)} collective-permute-done((f32[4,160,256]{2,1,0:T(8,128)S(1)}, f32[4,160,256]{2,1,0:T(8,128)}, u32[]{:S(2)}, u32[]{:S(2)}) %collective-permute-start.1) | collective-permute-done | bytes 655392 | tf_op jit(solution)/shard_map/ppermute | solution.py:322
  127.9 4.1 %node_sums.1 = (f32[32,16,256]{2,1,0:T(8,128)S(1)}, f32[32,16,256]{2,1,0:T(8,128)S(1)}) custom-call(s32[2]{0:T(128)S(1)} %pad_add_fusion.place_ref, bf16[8,320,512]{2,1,0:T(8,128)(2,1)S(1)} %narrow.1.left, f32[4,2,160,256]{3,2,1,0:T(8,128)} %all-to-all-done.3.hidden_ref, f32[4,160,256]{2,1,0:T(8,128)S(1)} %all-to-all-done.2.act_ref, ...), custom_call_target="tpu_custom_call" | custom-call | flops 671088640 | bytes 9000000 | tf_op jit(solution)/shard_map/node_sums/pallas_call | solution.py:281
  132.0 1.9 %collective-permute-start.2 = (f32[32,16,256]{2,1,0:T(8,128)S(1)}, f32[32,16,256]{2,1,0:T(8,128)S(1)}, u32[]{:S(2)}, u32[]{:S(2)}) collective-permute-start(f32[32,16,256]{2,1,0:T(8,128)S(1)} %get-tuple-element.22), channel_id=1, source_target_pairs={{0,8},{8,0},{1,9},{9,1},{2,10},{10,2},{3,11},{11,3},{4,12},{12,4},... | collective-permute-start | bytes 1572872 | tf_op jit(solution)/shard_map/ppermute | solution.py:327
  133.9 1.9 %collective-permute-done.2 = f32[32,16,256]{2,1,0:T(8,128)S(1)} collective-permute-done((f32[32,16,256]{2,1,0:T(8,128)S(1)}, f32[32,16,256]{2,1,0:T(8,128)S(1)}, u32[]{:S(2)}, u32[]{:S(2)}) %collective-permute-start.2) | collective-permute-done | bytes 524320 | tf_op jit(solution)/shard_map/ppermute | solution.py:327
  135.8 0.9 add.7
  136.7 10.4 %all-to-all-start.4 = ((f32[32,16,256]{2,1,0:T(8,128)}), f32[32,16,256]{2,1,0:T(8,128)S(1)}, u32[]{:S(2)}, u32[]{:S(2)}) async-start(f32[32,16,256]{2,1,0:T(8,128)} %add.7), calls=%async_computation.4 | async-start | bytes 1048576 | tf_op jit(solution)/shard_map/all_to_all | solution.py:25
  147.1 3.4 %copy-done = f32[128,2,32,256]{3,2,1,0:T(8,128)S(1)} copy-done((f32[128,2,32,256]{3,2,1,0:T(8,128)S(1)}, f32[128,2,32,256]{3,2,1,0:T(8,128)}, u32[]{:S(2)}) %copy-start) | copy-done | bytes 8388632
  150.5 2.7 %input_pass.1 = bf16[160,4096]{1,0:T(8,128)(2,1)} custom-call(f32[160,256]{1,0:T(8,128)S(1)} %get-tuple-element.14.hidden_ref.own_ref, f32[16,8,2,32,256]{4,3,2,1,0:T(8,128)S(1)} %bitcast.7), custom_call_target="tpu_custom_call" | custom-call | flops 335544320 | bytes 6000000 | tf_op jit(solution)/shard_map/input_pass/pallas_call | solution.py:153
  153.1 13.9 %all-to-all-done.4 = f32[32,16,256]{2,1,0:T(8,128)S(1)} async-done(((f32[32,16,256]{2,1,0:T(8,128)}), f32[32,16,256]{2,1,0:T(8,128)S(1)}, u32[]{:S(2)}, u32[]{:S(2)}) %all-to-all-start.4) | async-done | bytes 524320 | tf_op jit(solution)/shard_map/all_to_all | solution.py:25
  167.1 0.6 fusion
  (11 shorter events, 0.1 us)
Async XLA Ops:
  7.2 11.0 %copy-start.2 = (bf16[160,4096]{1,0:T(8,128)(2,1)S(1)}, bf16[160,4096]{1,0:T(8,128)(2,1)}, u32[]{:S(2)}) copy-start(bf16[160,4096]{1,0:T(8,128)(2,1)} %tokens_ref.3) | copy-start | bytes 3932164
  9.0 15.8 %all-to-all-start = ((f32[8,2,32,256]{3,2,1,0:T(8,128)}), f32[8,2,32,256]{3,2,1,0:T(8,128)S(1)}, u32[]{:S(2)}, u32[]{:S(2)}) async-start(f32[8,2,32,256]{3,2,1,0:T(8,128)} %make_pieces.1), calls=%async_computation | async-start | bytes 1048576 | tf_op jit(solution)/shard_map/all_to_all | solution.py:25
  18.2 68.0 %all-gather.3.cloned.1.call-start = ((), (), s32[]{:S(2)}) async-start(), calls=%async_computation.5 | async-start | bytes 8912896 | tf_op jit(solution)/shard_map/all_gather | solution.py:313
  18.2 1.3 copy-start.3
  20.2 2.3 %copy-start.1 = (f32[8,320,512]{2,1,0:T(8,128)}, f32[8,320,512]{2,1,0:T(8,128)S(1)}, u32[]{:S(2)}) copy-start(f32[8,320,512]{2,1,0:T(8,128)S(1)} %cut_columns.1) | copy-start | bytes 15728644
  24.8 0.8 copy-start.5
  25.6 60.5 %copy-start.4 = (bf16[160,4096]{1,0:T(8,128)(2,1)S(1)}, bf16[160,4096]{1,0:T(8,128)(2,1)}, u32[]{:S(2)}) copy-start(bf16[160,4096]{1,0:T(8,128)(2,1)} %grads_ref.3) | copy-start | bytes 3932164
  25.6 64.4 %all-to-all-start.1 = ((f32[8,320,512]{2,1,0:T(8,128)}), f32[8,320,512]{2,1,0:T(8,128)}, u32[]{:S(2)}, u32[]{:S(2)}) async-start(f32[8,320,512]{2,1,0:T(8,128)} %copy-done.1), calls=%async_computation.1 | async-start | bytes 10485760 | tf_op jit(solution)/shard_map/all_to_all | solution.py:25
  90.0 14.7 %all-to-all-start.2 = ((f32[4,160,256]{2,1,0:T(8,128)}), f32[4,160,256]{2,1,0:T(8,128)S(1)}, u32[]{:S(2)}, u32[]{:S(2)}) async-start(f32[4,160,256]{2,1,0:T(8,128)} %get-tuple-element.18), calls=%async_computation.2 | async-start | bytes 1310720 | tf_op jit(solution)/shard_map/all_to_all | solution.py:25
  94.8 7.7 %collective-permute-start = (f32[160,256]{1,0:T(8,128)S(1)}, f32[160,256]{1,0:T(8,128)S(1)}, u32[]{:S(2)}, u32[]{:S(2)}) collective-permute-start(f32[160,256]{1,0:T(8,128)S(1)} %get-tuple-element.14.hidden_ref.own_ref), channel_id=1, source_target_pairs={{0,1},{1,0},{2,3},{3,2},{4,5},{5,4},{6,7},{7,6},{8,9},{9,8},{10,11... | collective-permute-start | bytes 491528 | tf_op jit(solution)/shard_map/ppermute | solution.py:317
  104.7 23.2 %all-to-all-start.3 = ((f32[4,2,160,256]{3,2,1,0:T(8,128)}), f32[4,2,160,256]{3,2,1,0:T(8,128)}, u32[]{:S(2)}, u32[]{:S(2)}) async-start(f32[4,2,160,256]{3,2,1,0:T(8,128)} %pair_copies.1), calls=%async_computation.3 | async-start | bytes 2621440 | tf_op jit(solution)/shard_map/all_to_all | solution.py:25
  110.4 17.5 %collective-permute-start.1 = (f32[4,160,256]{2,1,0:T(8,128)S(1)}, f32[4,160,256]{2,1,0:T(8,128)}, u32[]{:S(2)}, u32[]{:S(2)}) collective-permute-start(f32[4,160,256]{2,1,0:T(8,128)S(1)} %all-to-all-done.2.act_ref), channel_id=1, source_target_pairs={{0,1},{1,0},{2,3},{3,2},{4,5},{5,4},{6,7},{7,6},{8,9},{9,8},{10,11... | collective-permute-start | bytes 1966088 | tf_op jit(solution)/shard_map/ppermute | solution.py:322
  132.0 3.8 %collective-permute-start.2 = (f32[32,16,256]{2,1,0:T(8,128)S(1)}, f32[32,16,256]{2,1,0:T(8,128)S(1)}, u32[]{:S(2)}, u32[]{:S(2)}) collective-permute-start(f32[32,16,256]{2,1,0:T(8,128)S(1)} %get-tuple-element.22), channel_id=1, source_target_pairs={{0,8},{8,0},{1,9},{9,1},{2,10},{10,2},{3,11},{11,3},{4,12},{12,4},... | collective-permute-start | bytes 1572872 | tf_op jit(solution)/shard_map/ppermute | solution.py:327
  136.7 30.4 %all-to-all-start.4 = ((f32[32,16,256]{2,1,0:T(8,128)}), f32[32,16,256]{2,1,0:T(8,128)S(1)}, u32[]{:S(2)}, u32[]{:S(2)}) async-start(f32[32,16,256]{2,1,0:T(8,128)} %add.7), calls=%async_computation.4 | async-start | bytes 1048576 | tf_op jit(solution)/shard_map/all_to_all | solution.py:25
  147.1 3.4 %copy-start = (f32[128,2,32,256]{3,2,1,0:T(8,128)S(1)}, f32[128,2,32,256]{3,2,1,0:T(8,128)}, u32[]{:S(2)}) copy-start(f32[128,2,32,256]{3,2,1,0:T(8,128)} %all-gather.3.cloned.1.call-done) | copy-start | bytes 25165828
Sparse Core Ops, SparseCore 0:
  25.7 60.3 all-gather.2

commit v10 on v9

--- a/solution.py
+++ b/solution.py
@@ -248,29 +248,50 @@
     )(tokens, grads)
 
 
-def node_kernel(place_ref, left, hidden_ref, act_ref, act_peer_ref, mine_ref, other_ref):
-    rows, width = act_ref.shape[1:]
-    n = left.shape[0]
-    totals = [None, None]
-    for p in range(n):
-        owner = 2 * (p // 2) + lax.rem(place_ref[1] + p, 2)
-        rights = (hidden_ref[p // 2, p % 2], (act_peer_ref if p % 2 else act_ref)[p // 2])
-        for kind in range(2):
-            term = lax.dot_general(
-                rights[kind].astype(jnp.bfloat16),
+def node_kernel(
+    place_ref, left, hidden_hbm, act_ref, act_peer_hbm, mine_ref, other_ref, hidden, act_peer, sems
+):
+    n_x, rows, width = act_ref.shape
+    copies = [
+        [pltpu.make_async_copy(act_peer_hbm.at[k], act_peer.at[k], sems.at[0, k]) for k in range(n_x)],
+        [pltpu.make_async_copy(hidden_hbm.at[k], hidden.at[k], sems.at[1, k]) for k in range(n_x)],
+    ]
+    for copy in copies[0] + copies[1]:
+        copy.start()
+
+    def term(owner, kind, right):
+        return clip_blocks(
+            lax.dot_general(
+                right.astype(jnp.bfloat16),
                 left[owner, kind * rows : (kind + 1) * rows],
                 (((0,), (0,)), ((), ())),
                 preferred_element_type=jnp.float32,
             )
-            clipped = clip_blocks(term)
-            totals[kind] = clipped if totals[kind] is None else totals[kind] + clipped
-    owned = mine_ref.shape[1] // 2
-    for kind in range(2):
-        summed = clip_blocks(totals[kind]).T.reshape(mine_ref.shape[0], 2, owned, width)
+        )
+
+    def finish(kind, total):
+        owned = mine_ref.shape[1] // 2
+        summed = clip_blocks(total).T.reshape(mine_ref.shape[0], 2, owned, width)
         first = place_ref[0] == 0
         part = slice(kind * owned, (kind + 1) * owned)
         mine_ref[:, part] = jnp.where(first, summed[:, 0], summed[:, 1])
         other_ref[:, part] = jnp.where(first, summed[:, 1], summed[:, 0])
+
+    own = place_ref[1]
+    peer = 1 - own
+    total = term(own, 1, act_ref[0])
+    for k in range(1, n_x):
+        total += term(2 * k + own, 1, act_ref[k])
+    for k in range(n_x):
+        copies[0][k].wait()
+        total += term(2 * k + peer, 1, act_peer[k])
+    finish(1, total)
+    total = None
+    for k in range(n_x):
+        copies[1][k].wait()
+        pair = term(2 * k + own, 0, hidden[k, 0]) + term(2 * k + peer, 0, hidden[k, 1])
+        total = pair if total is None else total + pair
+    finish(0, total)
 
 
 def node_sums(place, left, hidden, act, act_peer, owned):
@@ -283,18 +304,23 @@
         in_specs=[
             pl.BlockSpec(memory_space=pltpu.SMEM),
             vmem,
+            pl.BlockSpec(memory_space=pltpu.HBM),
             vmem,
-            vmem,
-            vmem,
+            pl.BlockSpec(memory_space=pltpu.HBM),
         ],
         out_specs=[vmem, vmem],
         out_shape=[jax.ShapeDtypeStruct(half, jnp.float32)] * 2,
+        scratch_shapes=[
+            pltpu.VMEM(hidden.shape, hidden.dtype),
+            pltpu.VMEM(act_peer.shape, act_peer.dtype),
+            pltpu.SemaphoreType.DMA((2, act.shape[0])),
+        ],
         compiler_params=pltpu.CompilerParams(vmem_limit_bytes=VMEM_LIMIT),
         cost_estimate=pl.CostEstimate(
             flops=4 * n * rows * height * width, bytes_accessed=9000000, transcendentals=0
         ),
         name="node_sums",
-    )(place, left, hidden, act, act_peer)
+    )(place, left, in_hbm(hidden), act, in_hbm(act_peer))
 
 
 def local(tokens, out_grad, up_codes, up_scales, down_codes, down_scales):

time: 175 us -> 177 us (1.011)
  no operation moved by 1% of the time
where the time goes in v10:
time: 177 us; the launch traced here: 176 us
  waiting for transfers between devices  90.4 us (51%)
  starting transfers between devices  43.8 us (25%)
  Pallas kernels  18.2 us (10%)
  between operations  14.2 us (8%)
  local copies, waits for them, and re-layouts  8.37 us (5%)
    all_gather x1, waiting for transfers between devices, local(): weights = lax.all_gather(pieces, GROUP, axis=0)  53.7 us
    all_to_all x5, starting transfers between devices, exchange(): return lax.all_to_all(array, axes, split_axis=0, concat_axis=0, tiled=True)  37 us
    all_to_all x5, waiting for transfers between devices, exchange(): return lax.all_to_all(array, axes, split_axis=0, concat_axis=0, tiled=True)  17.3 us
    ppermute x1, waiting for transfers between devices, local(): act_peer_all = lax.ppermute(act_all, 'yl', SWAP)  12.3 us
    unnamed x12, local copies, waits for them, and re-layouts  7.76 us
    pallas_call x1, Pallas kernels, node_sums(): pl.pallas_call(node_kernel, in_specs=[pl.BlockSpec(memory_space=pltpu.SME...  5.46 us
    ppermute x1, waiting for transfers between devices, local(): hidden_peer = lax.ppermute(hidden, 'yl', SWAP)  5.23 us
    pallas_call x1, Pallas kernels, hidden_pass(): pl.pallas_call(hidden_kernel, in_specs=[pl.BlockSpec(memory_space=pltpu.H...  3.85 us
  transfers between devices with their start and end apart: 9, of which 7 were waited for; matrix products, arithmetic and copies ran while one was open for 0% of the time, Pallas kernels for 6%

profile of v10, /device:TPU:10, one launch (start us, length us, event | category | flops | bytes accessed | tf_op | source)
XLA Modules:
  0.0 176.0 jit_solution(14475418270899876461)
XLA Ops:
  7.2 1.8 %make_pieces.1 = f32[8,2,32,256]{3,2,1,0:T(8,128)} custom-call(s32[1]{0:T(128)} %bitcast.place_ref, bf16[512,256]{1,0:T(8,128)(2,1)} %up_ref.1, f32[2,512]{1,0:T(2,128)} %bitcast.8, bf16[512,256]{1,0:T(8,128)(2,1)} %down_ref.1, f32[2,512]{1,0:T(2,128)} %bitcast.9), custom_call_target="tpu_custom_call" | custom-call | tf_op jit(solution)/shard_map/make_pieces/pallas_call | solution.py:191
  9.0 9.2 %all-to-all-start = ((f32[8,2,32,256]{3,2,1,0:T(8,128)}), f32[8,2,32,256]{3,2,1,0:T(8,128)S(1)}, u32[]{:S(2)}, u32[]{:S(2)}) async-start(f32[8,2,32,256]{3,2,1,0:T(8,128)} %make_pieces.1), calls=%async_computation | async-start | bytes 1048576 | tf_op jit(solution)/shard_map/all_to_all | solution.py:25
  18.2 0.0 copy-start.3
  18.2 1.3 copy-done.3
  19.5 0.7 cut_columns.1
  20.2 2.3 %copy-done.1 = f32[8,320,512]{2,1,0:T(8,128)} copy-done((f32[8,320,512]{2,1,0:T(8,128)}, f32[8,320,512]{2,1,0:T(8,128)S(1)}, u32[]{:S(2)}) %copy-start.1) | copy-done | bytes 5242904
  22.5 2.3 %all-to-all-done = f32[8,2,32,256]{3,2,1,0:T(8,128)S(1)} async-done(((f32[8,2,32,256]{3,2,1,0:T(8,128)}), f32[8,2,32,256]{3,2,1,0:T(8,128)S(1)}, u32[]{:S(2)}, u32[]{:S(2)}) %all-to-all-start) | async-done | bytes 524320 | tf_op jit(solution)/shard_map/all_to_all | solution.py:25
  24.8 0.8 copy-done.5
  25.6 0.0 all-gather.3.cloned.1.call-update
  25.6 0.0 copy-start.4
  25.6 6.8 %all-to-all-start.1 = ((f32[8,320,512]{2,1,0:T(8,128)}), f32[8,320,512]{2,1,0:T(8,128)}, u32[]{:S(2)}, u32[]{:S(2)}) async-start(f32[8,320,512]{2,1,0:T(8,128)} %copy-done.1), calls=%async_computation.1 | async-start | bytes 10485760 | tf_op jit(solution)/shard_map/all_to_all | solution.py:25
  32.5 53.7 %all-gather.3.cloned.1.call-done = f32[128,2,32,256]{3,2,1,0:T(8,128)} async-done(((f32[8,2,32,256]{3,2,1,0:T(8,128)}), f32[128,2,32,256]{3,2,1,0:T(8,128)}) %all-gather.3.cloned.1.call-update) | async-done | bytes 8388624 | tf_op jit(solution)/shard_map/all_gather | solution.py:339
  86.2 3.9 %hidden_pass.1 = (f32[4,160,256]{2,1,0:T(8,128)}, f32[160,256]{1,0:T(8,128)S(1)}) custom-call(f32[16,8,2,32,256]{4,3,2,1,0:T(8,128)} %bitcast.6, bf16[160,4096]{1,0:T(8,128)(2,1)S(1)} %copy-done.2, bf16[160,4096]{1,0:T(8,128)(2,1)S(1)} %copy-done.4), custom_call_target="tpu_custom_call" | custom-call | flops 671088640 | bytes 13000000 | tf_op jit(solution)/shard_map/hidden_pass/pallas_call | solution.py:86
  90.0 4.8 %all-to-all-start.2 = ((f32[4,160,256]{2,1,0:T(8,128)}), f32[4,160,256]{2,1,0:T(8,128)S(1)}, u32[]{:S(2)}, u32[]{:S(2)}) async-start(f32[4,160,256]{2,1,0:T(8,128)} %get-tuple-element.18), calls=%async_computation.2 | async-start | bytes 1310720 | tf_op jit(solution)/shard_map/all_to_all | solution.py:25
  94.8 2.4 %collective-permute-start = (f32[160,256]{1,0:T(8,128)S(1)}, f32[160,256]{1,0:T(8,128)S(1)}, u32[]{:S(2)}, u32[]{:S(2)}) collective-permute-start(f32[160,256]{1,0:T(8,128)S(1)} %get-tuple-element.14.hidden_ref.own_ref), channel_id=1, source_target_pairs={{0,1},{1,0},{2,3},{3,2},{4,5},{5,4},{6,7},{7,6},{8,9},{9,8},{10,11... | collective-permute-start | bytes 491528 | tf_op jit(solution)/shard_map/ppermute | solution.py:343
  97.3 5.2 %collective-permute-done.peer_ref = f32[160,256]{1,0:T(8,128)S(1)} collective-permute-done((f32[160,256]{1,0:T(8,128)S(1)}, f32[160,256]{1,0:T(8,128)S(1)}, u32[]{:S(2)}, u32[]{:S(2)}) %collective-permute-start) | collective-permute-done | bytes 163872 | tf_op jit(solution)/shard_map/ppermute | solution.py:343
  102.5 1.1 pair_copies.1
  103.6 1.0 all-to-all-done.2.act_ref
  104.7 5.7 %all-to-all-start.3 = ((f32[4,2,160,256]{3,2,1,0:T(8,128)}), f32[4,2,160,256]{3,2,1,0:T(8,128)}, u32[]{:S(2)}, u32[]{:S(2)}) async-start(f32[4,2,160,256]{3,2,1,0:T(8,128)} %pair_copies.1), calls=%async_computation.3 | async-start | bytes 2621440 | tf_op jit(solution)/shard_map/all_to_all | solution.py:25
  110.4 2.4 %collective-permute-start.1 = (f32[4,160,256]{2,1,0:T(8,128)S(1)}, f32[4,160,256]{2,1,0:T(8,128)}, u32[]{:S(2)}, u32[]{:S(2)}) collective-permute-start(f32[4,160,256]{2,1,0:T(8,128)S(1)} %all-to-all-done.2.act_ref), channel_id=1, source_target_pairs={{0,1},{1,0},{2,3},{3,2},{4,5},{5,4},{6,7},{7,6},{8,9},{9,8},{10,11... | collective-permute-start | bytes 1966088 | tf_op jit(solution)/shard_map/ppermute | solution.py:348
  112.9 0.1 pad_add_fusion.place_ref
  112.9 2.7 %narrow.1.left = bf16[8,320,512]{2,1,0:T(8,128)(2,1)S(1)} custom-call(f32[8,320,512]{2,1,0:T(8,128)} %all-to-all-done.1.columns_ref), custom_call_target="tpu_custom_call" | custom-call | bytes 12000000 | tf_op jit(solution)/shard_map/narrow/pallas_call | solution.py:218
  115.6 12.3 %collective-permute-done.1.act_peer_hbm = f32[4,160,256]{2,1,0:T(8,128)} collective-permute-done((f32[4,160,256]{2,1,0:T(8,128)S(1)}, f32[4,160,256]{2,1,0:T(8,128)}, u32[]{:S(2)}, u32[]{:S(2)}) %collective-permute-start.1) | collective-permute-done | bytes 655392 | tf_op jit(solution)/shard_map/ppermute | solution.py:348
  127.9 5.5 %node_sums.1 = (f32[32,16,256]{2,1,0:T(8,128)S(1)}, f32[32,16,256]{2,1,0:T(8,128)S(1)}) custom-call(s32[2]{0:T(128)S(1)} %pad_add_fusion.place_ref, bf16[8,320,512]{2,1,0:T(8,128)(2,1)S(1)} %narrow.1.left, f32[4,2,160,256]{3,2,1,0:T(8,128)} %all-to-all-done.3.hidden_hbm, f32[4,160,256]{2,1,0:T(8,128)S(1)} %all-to-all-done.2.act_ref, ...), custom_call_target="tpu_custom_call" | custom-call | flops 671088640 | bytes 9000000 | tf_op jit(solution)/shard_map/node_sums/pallas_call | solution.py:302
  133.3 1.9 %collective-permute-start.2 = (f32[32,16,256]{2,1,0:T(8,128)S(1)}, f32[32,16,256]{2,1,0:T(8,128)S(1)}, u32[]{:S(2)}, u32[]{:S(2)}) collective-permute-start(f32[32,16,256]{2,1,0:T(8,128)S(1)} %get-tuple-element.22), channel_id=1, source_target_pairs={{0,8},{8,0},{1,9},{9,1},{2,10},{10,2},{3,11},{11,3},{4,12},{12,4},... | collective-permute-start | bytes 1572872 | tf_op jit(solution)/shard_map/ppermute | solution.py:353
  135.3 1.9 %collective-permute-done.2 = f32[32,16,256]{2,1,0:T(8,128)S(1)} collective-permute-done((f32[32,16,256]{2,1,0:T(8,128)S(1)}, f32[32,16,256]{2,1,0:T(8,128)S(1)}, u32[]{:S(2)}, u32[]{:S(2)}) %collective-permute-start.2) | collective-permute-done | bytes 524320 | tf_op jit(solution)/shard_map/ppermute | solution.py:353
  137.1 0.9 add.7
  138.1 10.4 %all-to-all-start.4 = ((f32[32,16,256]{2,1,0:T(8,128)}), f32[32,16,256]{2,1,0:T(8,128)S(1)}, u32[]{:S(2)}, u32[]{:S(2)}) async-start(f32[32,16,256]{2,1,0:T(8,128)} %add.7), calls=%async_computation.4 | async-start | bytes 1048576 | tf_op jit(solution)/shard_map/all_to_all | solution.py:25
  148.5 3.4 %copy-done = f32[128,2,32,256]{3,2,1,0:T(8,128)S(1)} copy-done((f32[128,2,32,256]{3,2,1,0:T(8,128)S(1)}, f32[128,2,32,256]{3,2,1,0:T(8,128)}, u32[]{:S(2)}) %copy-start) | copy-done | bytes 8388632
  151.9 2.6 %input_pass.1 = bf16[160,4096]{1,0:T(8,128)(2,1)} custom-call(f32[160,256]{1,0:T(8,128)S(1)} %get-tuple-element.14.hidden_ref.own_ref, f32[16,8,2,32,256]{4,3,2,1,0:T(8,128)S(1)} %bitcast.7), custom_call_target="tpu_custom_call" | custom-call | flops 335544320 | bytes 6000000 | tf_op jit(solution)/shard_map/input_pass/pallas_call | solution.py:153
  154.5 14.0 %all-to-all-done.4 = f32[32,16,256]{2,1,0:T(8,128)S(1)} async-done(((f32[32,16,256]{2,1,0:T(8,128)}), f32[32,16,256]{2,1,0:T(8,128)S(1)}, u32[]{:S(2)}, u32[]{:S(2)}) %all-to-all-start.4) | async-done | bytes 524320 | tf_op jit(solution)/shard_map/all_to_all | solution.py:25
  168.5 0.6 fusion
  (11 shorter events, 0.1 us)
Async XLA Ops:
  7.2 11.0 %copy-start.2 = (bf16[160,4096]{1,0:T(8,128)(2,1)S(1)}, bf16[160,4096]{1,0:T(8,128)(2,1)}, u32[]{:S(2)}) copy-start(bf16[160,4096]{1,0:T(8,128)(2,1)} %tokens_ref.3) | copy-start | bytes 3932164
  9.0 15.8 %all-to-all-start = ((f32[8,2,32,256]{3,2,1,0:T(8,128)}), f32[8,2,32,256]{3,2,1,0:T(8,128)S(1)}, u32[]{:S(2)}, u32[]{:S(2)}) async-start(f32[8,2,32,256]{3,2,1,0:T(8,128)} %make_pieces.1), calls=%async_computation | async-start | bytes 1048576 | tf_op jit(solution)/shard_map/all_to_all | solution.py:25
  18.2 68.0 %all-gather.3.cloned.1.call-start = ((), (), s32[]{:S(2)}) async-start(), calls=%async_computation.5 | async-start | bytes 8912896 | tf_op jit(solution)/shard_map/all_gather | solution.py:339
  18.2 1.3 copy-start.3
  20.2 2.3 %copy-start.1 = (f32[8,320,512]{2,1,0:T(8,128)}, f32[8,320,512]{2,1,0:T(8,128)S(1)}, u32[]{:S(2)}) copy-start(f32[8,320,512]{2,1,0:T(8,128)S(1)} %cut_columns.1) | copy-start | bytes 15728644
  24.8 0.8 copy-start.5
  25.6 60.5 %copy-start.4 = (bf16[160,4096]{1,0:T(8,128)(2,1)S(1)}, bf16[160,4096]{1,0:T(8,128)(2,1)}, u32[]{:S(2)}) copy-start(bf16[160,4096]{1,0:T(8,128)(2,1)} %grads_ref.3) | copy-start | bytes 3932164
  25.6 64.4 %all-to-all-start.1 = ((f32[8,320,512]{2,1,0:T(8,128)}), f32[8,320,512]{2,1,0:T(8,128)}, u32[]{:S(2)}, u32[]{:S(2)}) async-start(f32[8,320,512]{2,1,0:T(8,128)} %copy-done.1), calls=%async_computation.1 | async-start | bytes 10485760 | tf_op jit(solution)/shard_map/all_to_all | solution.py:25
  90.0 14.7 %all-to-all-start.2 = ((f32[4,160,256]{2,1,0:T(8,128)}), f32[4,160,256]{2,1,0:T(8,128)S(1)}, u32[]{:S(2)}, u32[]{:S(2)}) async-start(f32[4,160,256]{2,1,0:T(8,128)} %get-tuple-element.18), calls=%async_computation.2 | async-start | bytes 1310720 | tf_op jit(solution)/shard_map/all_to_all | solution.py:25
  94.8 7.7 %collective-permute-start = (f32[160,256]{1,0:T(8,128)S(1)}, f32[160,256]{1,0:T(8,128)S(1)}, u32[]{:S(2)}, u32[]{:S(2)}) collective-permute-start(f32[160,256]{1,0:T(8,128)S(1)} %get-tuple-element.14.hidden_ref.own_ref), channel_id=1, source_target_pairs={{0,1},{1,0},{2,3},{3,2},{4,5},{5,4},{6,7},{7,6},{8,9},{9,8},{10,11... | collective-permute-start | bytes 491528 | tf_op jit(solution)/shard_map/ppermute | solution.py:343
  104.7 23.2 %all-to-all-start.3 = ((f32[4,2,160,256]{3,2,1,0:T(8,128)}), f32[4,2,160,256]{3,2,1,0:T(8,128)}, u32[]{:S(2)}, u32[]{:S(2)}) async-start(f32[4,2,160,256]{3,2,1,0:T(8,128)} %pair_copies.1), calls=%async_computation.3 | async-start | bytes 2621440 | tf_op jit(solution)/shard_map/all_to_all | solution.py:25
  110.4 17.5 %collective-permute-start.1 = (f32[4,160,256]{2,1,0:T(8,128)S(1)}, f32[4,160,256]{2,1,0:T(8,128)}, u32[]{:S(2)}, u32[]{:S(2)}) collective-permute-start(f32[4,160,256]{2,1,0:T(8,128)S(1)} %all-to-all-done.2.act_ref), channel_id=1, source_target_pairs={{0,1},{1,0},{2,3},{3,2},{4,5},{5,4},{6,7},{7,6},{8,9},{9,8},{10,11... | collective-permute-start | bytes 1966088 | tf_op jit(solution)/shard_map/ppermute | solution.py:348
  133.3 3.8 %collective-permute-start.2 = (f32[32,16,256]{2,1,0:T(8,128)S(1)}, f32[32,16,256]{2,1,0:T(8,128)S(1)}, u32[]{:S(2)}, u32[]{:S(2)}) collective-permute-start(f32[32,16,256]{2,1,0:T(8,128)S(1)} %get-tuple-element.22), channel_id=1, source_target_pairs={{0,8},{8,0},{1,9},{9,1},{2,10},{10,2},{3,11},{11,3},{4,12},{12,4},... | collective-permute-start | bytes 1572872 | tf_op jit(solution)/shard_map/ppermute | solution.py:353
  138.1 30.4 %all-to-all-start.4 = ((f32[32,16,256]{2,1,0:T(8,128)}), f32[32,16,256]{2,1,0:T(8,128)S(1)}, u32[]{:S(2)}, u32[]{:S(2)}) async-start(f32[32,16,256]{2,1,0:T(8,128)} %add.7), calls=%async_computation.4 | async-start | bytes 1048576 | tf_op jit(solution)/shard_map/all_to_all | solution.py:25
  148.5 3.4 %copy-start = (f32[128,2,32,256]{3,2,1,0:T(8,128)S(1)}, f32[128,2,32,256]{3,2,1,0:T(8,128)}, u32[]{:S(2)}) copy-start(f32[128,2,32,256]{3,2,1,0:T(8,128)} %all-gather.3.cloned.1.call-done) | copy-start | bytes 25165828
Sparse Core Ops, SparseCore 0:
  25.7 60.3 all-gather.2
